TPU v7x, 32 devices: a whole 2x2x4 slice. The times are simulated.
32 devices in a mesh: groups: 1, fsdp: 8 (over z, y), seq: 4 (over x, core), sub: 1.
Axes of the slice: x: 2, y: 2, z: 4, core: 2. Of those that a mesh axis runs over, the one named last changes fastest.
Arguments:
- tokens: bfloat16 [8, 1, 4, 128, 2048], P(('groups', 'fsdp'), 'sub', 'seq'), may hold values from -6 to 6
- frame_valid: int32 [8, 1, 4], P(('groups', 'fsdp'), 'sub'), may hold values from 0 to 1, as said below
- w_qkv: bfloat16 [2048, 3, 2048], P('fsdp', None, 'seq'), may hold values from -0.1875 to 0.1875
- w_out: bfloat16 [2048, 2048], P('seq', 'fsdp'), may hold values from -0.125 to 0.125
- w_act: bfloat16 [2048, 8192], P(None, 'fsdp'), may hold values from -0.125 to 0.125
- class_table: int32 [8192], P('fsdp'), may hold values from 0 to 120
- cam_bias: float32 [121], replicated, may hold values from -4 to 4
Outputs:
- hidden: bfloat16 [8, 1, 4, 128, 2048], P(('groups', 'fsdp'), 'sub', 'seq')
- logits: float32 [8, 1, 4, 8192], P('groups', 'sub', 'seq', 'fsdp')
Inputs may be any that keep to these rules, and one draw needn't show every extreme that they name: `frame_valid`: each window has at least one frame with value 1.
All inputs are finite; a program needn't handle non-finite values.
Results may differ from a plain program's by a relative error of at most 0.0058.
Values may be sent and summed in bfloat16 or wider, within the bound.
No kernel may reach another device: no remote copies, remote signals or barrier semaphores. Data moves between devices by JAX's collectives and lax.ppermute only.
A program may use at most 128 MiB of HBM per device.

v0:
```python
import math

import jax
import jax.numpy as jnp
from jax import lax
from jax.sharding import PartitionSpec as P

DH = 128


def normalize(values):
    centre = jnp.mean(values, axis=-1, keepdims=True)
    spread = jnp.mean(jnp.square(values - centre), axis=-1, keepdims=True)
    return (values - centre) * lax.rsqrt(spread + 1e-05)


def per_device(tokens, frame_valid, w_qkv, w_out, w_act, class_table, cam_bias):
    windows_here = tokens.shape[0]
    frame_rows = tokens.shape[3]
    model_width = tokens.shape[4]
    own_rows = tokens[:, 0, 0].astype(jnp.float32)
    normed = normalize(own_rows).astype(jnp.bfloat16)
    gathered = lax.all_gather(normed[:, None], "seq", axis=1, tiled=True)
    frame_count = gathered.shape[1]
    span_rows = frame_count * frame_rows
    window_rows = gathered.reshape(windows_here, span_rows, model_width)
    full_qkv = lax.all_gather(w_qkv, "fsdp", axis=0, tiled=True)
    projected = jnp.einsum(
        "wsd,dcn->wscn", window_rows, full_qkv, preferred_element_type=jnp.float32
    ).astype(jnp.bfloat16)
    local_heads = full_qkv.shape[2] // DH
    projected = projected.reshape(windows_here, span_rows, 3, local_heads, DH)
    queries = projected[:, :, 0]
    keys_all = projected[:, :, 1]
    values_all = projected[:, :, 2]
    key_mask = jnp.repeat(frame_valid[:, 0].astype(jnp.float32), frame_rows, axis=1)
    score_scale = 1.0 / math.sqrt(DH)
    scores = (
        jnp.einsum("wqhe,wkhe->whqk", queries, keys_all, preferred_element_type=jnp.float32)
        * score_scale
    )
    weights = jnp.exp(scores) * key_mask[:, None, None, :]
    totals = jnp.sum(weights, axis=-1)
    mixed_heads = jnp.einsum(
        "whqk,wkhe->wqhe",
        weights.astype(jnp.bfloat16),
        values_all,
        preferred_element_type=jnp.float32,
    )
    mixed_heads = mixed_heads / jnp.transpose(totals, (0, 2, 1))[:, :, :, None]
    mixed_heads = mixed_heads.astype(jnp.bfloat16).reshape(
        windows_here, frame_count, frame_rows, local_heads * DH
    )
    frame_major = jnp.transpose(mixed_heads, (1, 0, 2, 3)).reshape(
        frame_count * windows_here * frame_rows, local_heads * DH
    )
    full_out = lax.all_gather(w_out, "fsdp", axis=1, tiled=True)
    branch = lax.psum_scatter(
        jnp.dot(frame_major, full_out, preferred_element_type=jnp.float32),
        "seq",
        scatter_dimension=0,
        tiled=True,
    )
    hidden = own_rows + branch.reshape(windows_here, frame_rows, model_width)
    hidden_out = hidden.astype(jnp.bfloat16)
    hidden_wide = lax.optimization_barrier(hidden_out).astype(jnp.float32)
    pooled = normalize(jnp.mean(hidden_wide, axis=1)).astype(jnp.bfloat16)
    camera_ids = jnp.arange(cam_bias.shape[0], dtype=jnp.int32)
    onehot = (class_table[:, None] == camera_ids[None, :]).astype(jnp.float32)
    bias_cols = jnp.dot(onehot, cam_bias, precision=lax.Precision.HIGHEST)
    logits = (
        jnp.dot(
            lax.all_gather(pooled, "fsdp", axis=0, tiled=True),
            w_act,
            preferred_element_type=jnp.float32,
        )
        + bias_cols[None, :]
    )
    hidden_shard = hidden_out.reshape(windows_here, 1, 1, frame_rows, model_width)
    logit_shard = logits.reshape(logits.shape[0], 1, 1, logits.shape[1])
    return (hidden_shard, logit_shard)


def solution(mesh):
    in_specs = (
        P(("groups", "fsdp"), "sub", "seq", None, None),
        P(("groups", "fsdp"), "sub", None),
        P("fsdp", None, "seq"),
        P("seq", "fsdp"),
        P(None, "fsdp"),
        P("fsdp"),
        P(),
    )
    out_specs = (P(("groups", "fsdp"), "sub", "seq", None, None), P("groups", "sub", "seq", "fsdp"))
    return jax.shard_map(
        per_device, mesh=mesh, in_specs=in_specs, out_specs=out_specs, check_vma=False
    )
```

profile of v0, /device:TPU:0, one launch (start us, length us, event | category | flops | bytes accessed | tf_op | source)
XLA Modules:
  0.0 283.9 jit_solution(5235049157297667890)
XLA Ops:
  7.2 1.2 convert_reduce_fusion
  8.4 1.3 fusion.17
  9.8 2.2 fusion.20
  12.0 0.0 all-gather.7.cloned.1.call-start
  12.0 2.3 copy.15
  14.3 0.0 all-gather.9.cloned.1.call-start
  14.4 0.7 all-gather.9.cloned.1.call-update
  15.1 0.1 broadcast_bitcast_fusion
  15.2 22.2 %all-gather.5.cloned.1.call-done = bf16[1,4,128,2048]{3,2,0,1:T(8,128)(2,1)} async-done(((bf16[1,1,128,2048]{3,2,0,1:T(8,128)(2,1)}), bf16[1,4,128,2048]{3,2,0,1:T(8,128)(2,1)}) %all-gather.5.cloned.1.call-update) | async-done | bytes 2097168 | tf_op jit(solution)/shard_map/all_gather | solution.py:23
  37.4 102.0 %all-gather.7.cloned.1.call-done = bf16[2048,3,512]{0,2,1:T(8,128)(2,1)} async-done(((bf16[256,3,512]{0,2,1:T(8,128)(2,1)}), bf16[2048,3,512]{0,2,1:T(8,128)(2,1)}) %all-gather.7.cloned.1.call-update) | async-done | bytes 6291472 | tf_op jit(solution)/shard_map/all_gather | solution.py:27
  139.4 6.9 %convolution_convert_fusion = bf16[512,3,512]{0,2,1:T(8,128)(2,1)S(1)} fusion(bf16[512,2048,1]{1,0,2:T(8,128)(2,1)} %bitcast.86, bf16[2048,3,512]{0,2,1:T(8,128)(2,1)} %all-gather.7.cloned.1.call-done), kind=kOutput, calls=%fused_computation.10 | convolution fusion | flops 3222011904 | bytes 9961472 | tf_op jit(solution)/shard_map/wsd,dcn->wscn/dot_general | solution.py:28
  146.3 1.1 fusion
  147.4 1.0 divide_convert_fusion
  148.4 42.4 %all-gather.9.cloned.1.call-done = bf16[512,2048]{1,0:T(8,128)(2,1)} async-done(((bf16[512,256]{1,0:T(8,128)(2,1)}), bf16[512,2048]{1,0:T(8,128)(2,1)}) %all-gather.9.cloned.1.call-update) | async-done | bytes 2097168 | tf_op jit(solution)/shard_map/all_gather | solution.py:57
  190.8 4.9 %fusion.28 = f32[512,2048]{1,0:T(8,128)} fusion(bf16[512,512]{0,1:T(8,128)(2,1)S(1)} %bitcast.83, bf16[512,2048]{1,0:T(8,128)(2,1)} %all-gather.9.cloned.1.call-done), kind=kOutput, calls=%fused_computation.43 | convolution fusion | flops 1073741824 | bytes 6815744 | tf_op jit(solution)/shard_map/dot_general | solution.py:59
  195.7 0.4 fusion.22
  196.1 42.4 %reduce-scatter.2.cloned.1.call-done = f32[128,2048]{1,0:T(8,128)} async-done(((f32[512,2048]{1,0:T(8,128)}), f32[128,2048]{1,0:T(8,128)}) %reduce-scatter.2.cloned.1.call-update) | async-done | bytes 1048592 | tf_op jit(solution)/shard_map/reduce_scatter | solution.py:58
  238.5 2.2 fusion.26
  240.7 0.1 convert_reduce_fusion.1
  240.7 0.6 multiply_reduce_fusion.1
  242.0 0.6 multiply_reduce_fusion
  243.3 30.5 %all-gather = bf16[16384]{0:T(1024)(128)(2,1)S(1)} all-gather(bf16[2048]{0:T(1024)(128)(2,1)S(1)} %multiply_convert_fusion), channel_id=2, replica_groups=mesh['groups'=1,'fsdp'=8,'seq'=4,'sub'=1] {'fsdp'}, dimensions={0}, use_global_device_ids=true | all-gather | bytes 36864 | tf_op jit(solution)/shard_map/all_gather | solution.py:73
  273.8 2.8 %fusion.9 = f32[8,1,1,1024]{3,0,2,1:T(8,128)S(1)} fusion(bf16[8,2048]{1,0:T(8,128)(2,1)S(1)} %reshape.252, bf16[2048,1024]{1,0:T(8,128)(2,1)} %param.11, f32[1024]{0:T(1024)S(1)} %bitcast.85), kind=kOutput, calls=%fused_computation.13 | convolution fusion | flops 33562624 | bytes 4263936 | tf_op jit(solution)/shard_map/dot_general | solution.py:72
  276.7 0.7 copy.19
  (18 shorter events, 0.2 us)
Async XLA Ops:
  7.2 188.5 %copy-start = (f32[121]{0:T(128)S(1)}, f32[121]{0:T(128)}, u32[]{:S(2)}) copy-start(f32[121]{0:T(128)} %param.13) | copy-start | bytes 1456
  7.2 7.9 %copy-start.3 = (s32[1,1,4]{2,1,0:T(1,128)S(1)}, s32[1,1,4]{2,1,0:T(1,128)}, u32[]{:S(2)}) copy-start(s32[1,1,4]{2,1,0:T(1,128)} %param.8) | copy-start | bytes 52
  7.2 30.2 %all-gather.5.cloned.1.call-start = ((), (), s32[]{:S(2)}) async-start(), calls=%async_computation.1 | async-start | bytes 2621440 | tf_op jit(solution)/shard_map/all_gather | solution.py:23
  12.0 127.5 %all-gather.7.cloned.1.call-start = ((), (), s32[]{:S(2)}) async-start(), calls=%async_computation.2 | async-start | bytes 7077888 | tf_op jit(solution)/shard_map/all_gather | solution.py:27
  14.3 176.4 %all-gather.9.cloned.1.call-start = ((), (), s32[]{:S(2)}) async-start(), calls=%async_computation.3 | async-start | bytes 2359296 | tf_op jit(solution)/shard_map/all_gather | solution.py:57
  15.1 223.4 %reduce-scatter.2.cloned.1.call-start = ((), (), s32[]{:S(2)}) async-start(), calls=%async_computation.4 | async-start | bytes 5242880 | tf_op jit(solution)/shard_map/reduce_scatter | solution.py:58
  190.8 4.9 %copy-start.2 = (s32[1024]{0:T(1024)S(1)}, s32[1024]{0:T(1024)}, u32[]{:S(2)}) copy-start(s32[1024]{0:T(1024)} %param.12) | copy-start | bytes 12292
  190.8 47.7 %copy-start.1 = (bf16[1,1,1,128,2048]{4,3,2,1,0:T(8,128)(2,1)S(1)}, bf16[1,1,1,128,2048]{4,3,2,1,0:T(8,128)(2,1)}, u32[]{:S(2)}) copy-start(bf16[1,1,1,128,2048]{4,3,2,1,0:T(8,128)(2,1)} %param.7) | copy-start | bytes 1572868
Sparse Core Ops, SparseCore 0:
  12.1 25.2 all-gather.4
  39.4 99.9 all-gather.6
  141.5 49.2 all-gather.8
  195.8 42.6 reduce-scatter.1
where the time goes:
time: 284 us
  waiting for transfers between devices  210 us (74%)
  blocking collectives  30.5 us (11%)
  matrix products  17.1 us (6%)
  between operations  15.2 us (5%)
  other arithmetic  8.18 us (3%)
  local copies, waits for them, and re-layouts  3.06 us (1%)
    all_gather x1, waiting for transfers between devices, per_device(): full_qkv = lax.all_gather(w_qkv, 'fsdp', axis=0, tiled=True)  102 us
    reduce_scatter x1, waiting for transfers between devices, per_device(): lax.psum_scatter(jnp.dot(frame_major, full_out, preferred_element_type=jn...  42.4 us
    all_gather x1, waiting for transfers between devices, per_device(): full_out = lax.all_gather(w_out, 'fsdp', axis=1, tiled=True)  42.4 us
    all_gather x1, blocking collectives, per_device(): lax.all_gather(pooled, 'fsdp', axis=0, tiled=True)  30.5 us
    all_gather x1, waiting for transfers between devices, per_device(): gathered = lax.all_gather(normed[:, None], 'seq', axis=1, tiled=True)  22.2 us
    dot_general x1, matrix products, per_device(): jnp.einsum('wsd,dcn->wscn', window_rows, full_qkv, preferred_element_type...  6.9 us
  transfers between devices with their start and end apart: 4, of which 4 were waited for; matrix products, arithmetic and copies ran while one was open for 4% of the time, Pallas kernels for 0%

commit v1 on v0

v1 whole, which is shorter than its diff:
```python
import math

import jax
import jax.numpy as jnp
from jax import lax
from jax.sharding import PartitionSpec as P

DH = 128


def normalize(values):
    centre = jnp.mean(values, axis=-1, keepdims=True)
    spread = jnp.mean(jnp.square(values - centre), axis=-1, keepdims=True)
    return (values - centre) * lax.rsqrt(spread + 1e-05)


def ring_tables(n):
    order = list(range(0, n, 2)) + list(range(1, n, 2))[::-1]
    place = [order.index(i) for i in range(n)]
    forward = [(order[p], order[(p + 1) % n]) for p in range(n)]
    backward = [(b, a) for a, b in forward]
    return order, place, forward, backward


def ring_gather(blocks, n, forward, backward, split_dim):
    up = list(blocks)
    down = list(blocks)
    got = [{0: b} for b in blocks]
    for t in range(1, (n - 1) // 2 + 1):
        for i in range(len(blocks)):
            up[i] = lax.ppermute(up[i], "fsdp", forward)
            down[i] = lax.ppermute(down[i], "fsdp", backward)
            got[i][-t] = up[i]
            got[i][t] = down[i]
    if n % 2 == 0:
        for i in range(len(blocks)):
            half = blocks[i].shape[split_dim] // 2
            first = lax.slice_in_dim(up[i], 0, half, axis=split_dim)
            second = lax.slice_in_dim(down[i], half, 2 * half, axis=split_dim)
            first = lax.ppermute(first, "fsdp", forward)
            second = lax.ppermute(second, "fsdp", backward)
            got[i][n // 2] = jnp.concatenate([first, second], axis=split_dim)
    return got


def exchange(values, axis, size, bit):
    return lax.ppermute(values, axis, [(i, i ^ bit) for i in range(size)])


def make(mesh):
    fsdp = mesh.shape["fsdp"]
    seq = mesh.shape["seq"]
    order, place, forward, backward = ring_tables(fsdp)

    def per_device(tokens, frame_valid, w_qkv, w_out, w_act, class_table, cam_bias):
        frame_rows, width = tokens.shape[3], tokens.shape[4]
        me_f = lax.axis_index("fsdp")
        me_s = lax.axis_index("seq")
        my_place = jnp.array(place, jnp.int32)[me_f]
        order_t = jnp.array(order, jnp.int32)

        def owner(distance):
            return order_t[(my_place + distance) % fsdp]

        own = tokens[0, 0, 0].astype(jnp.float32)
        normed = normalize(own).astype(jnp.bfloat16)
        slots = normed[None]
        bit = 1
        while bit < seq:
            slots = jnp.concatenate([slots, exchange(slots, "seq", seq, bit)], axis=0)
            bit *= 2
        rows = slots.reshape(seq * frame_rows, width)
        frames = me_s ^ jnp.arange(seq, dtype=jnp.int32)
        valid = frame_valid[0, 0][frames].astype(jnp.float32)
        key_mask = jnp.repeat(valid, frame_rows)

        block = w_qkv.shape[0]
        parts = [w_qkv[:, c] for c in range(3)]
        got = ring_gather(parts, fsdp, forward, backward, 0)
        proj = []
        for c in range(3):
            total = None
            for d in got[c]:
                cols = lax.dynamic_slice_in_dim(rows, owner(d) * block, block, axis=1)
                term = jnp.dot(cols, got[c][d], preferred_element_type=jnp.float32)
                total = term if total is None else total + term
            proj.append(total.astype(jnp.bfloat16))
        heads = w_qkv.shape[2] // DH
        q, k, v = [p.reshape(p.shape[0], heads, DH) for p in proj]
        scores = jnp.einsum("qhe,khe->hqk", q, k, preferred_element_type=jnp.float32) * (
            1.0 / math.sqrt(DH)
        )
        weights = jnp.exp(scores) * key_mask[None, None, :]
        totals = jnp.sum(weights, axis=-1)
        mixed = jnp.einsum(
            "hqk,khe->qhe", weights.astype(jnp.bfloat16), v, preferred_element_type=jnp.float32
        )
        mixed = (mixed / jnp.transpose(totals)[:, :, None]).astype(jnp.bfloat16)
        mixed = mixed.reshape(rows.shape[0], heads * DH)

        last = (fsdp - 1) // 2
        w_out_late, _ = lax.optimization_barrier((w_out, got[0][last]))
        got_out = ring_gather([w_out_late], fsdp, forward, backward, 1)[0]

        cols_out = w_out.shape[1]
        hidden = jnp.zeros((frame_rows, width), jnp.bfloat16)
        pooled = jnp.zeros((width,), jnp.float32)
        names = sorted(got_out, key=abs)
        groups = [names[:3], names[3:5], names[5:]]
        for group in groups:
            if not group:
                continue
            w_group = jnp.concatenate([got_out[d] for d in group], axis=1)
            part = jnp.dot(mixed, w_group, preferred_element_type=jnp.float32)
            part = part.reshape(seq, frame_rows, w_group.shape[1])
            bit = 1
            while part.shape[0] > 1:
                pairs = part.reshape(part.shape[0] // 2, 2, frame_rows, part.shape[2])
                came = exchange(pairs[:, 1].astype(jnp.bfloat16), "seq", seq, bit)
                part = pairs[:, 0] + came.astype(jnp.float32)
                bit *= 2
            for j, d in enumerate(group):
                at = owner(d) * cols_out
                res = lax.dynamic_slice_in_dim(tokens[0, 0, 0], at, cols_out, axis=1)
                piece = res.astype(jnp.float32) + part[0][:, j * cols_out : (j + 1) * cols_out]
                piece = lax.optimization_barrier(piece.astype(jnp.bfloat16))
                hidden = lax.dynamic_update_slice_in_dim(hidden, piece, at, axis=1)
                mean = jnp.mean(piece.astype(jnp.float32), axis=0)
                pooled = lax.dynamic_update_slice_in_dim(pooled, mean, at, axis=0)

        pooled = normalize(pooled[None]).astype(jnp.bfloat16)
        bit = 1
        while bit < fsdp:
            pooled = jnp.concatenate([pooled, exchange(pooled, "fsdp", fsdp, bit)], axis=0)
            bit *= 2
        pooled = pooled[me_f ^ jnp.arange(fsdp, dtype=jnp.int32)]
        camera_ids = jnp.arange(cam_bias.shape[0], dtype=jnp.int32)
        onehot = (class_table[:, None] == camera_ids[None, :]).astype(jnp.float32)
        bias_cols = jnp.dot(onehot, cam_bias, precision=lax.Precision.HIGHEST)
        logits = jnp.dot(pooled, w_act, preferred_element_type=jnp.float32) + bias_cols[None, :]
        return (
            hidden.reshape(tokens.shape),
            logits.reshape(logits.shape[0], 1, 1, logits.shape[1]),
        )

    return per_device


def solution(mesh):
    in_specs = (
        P(("groups", "fsdp"), "sub", "seq", None, None),
        P(("groups", "fsdp"), "sub", None),
        P("fsdp", None, "seq"),
        P("seq", "fsdp"),
        P(None, "fsdp"),
        P("fsdp"),
        P(),
    )
    out_specs = (P(("groups", "fsdp"), "sub", "seq", None, None), P("groups", "sub", "seq", "fsdp"))
    return jax.shard_map(
        make(mesh), mesh=mesh, in_specs=in_specs, out_specs=out_specs, check_vma=False
    )
```

time: 284 us -> 162 us (0.57)
  waiting for transfers between devices: 210 us -> 52.7 us
  starting transfers between devices: 0.16 us -> 49.4 us
  blocking collectives: 30.5 us -> 0 us
  matrix products: 17.1 us -> 28 us
  local copies, waits for them, and re-layouts: 3.06 us -> 8.96 us
    all_gather x3 -> x0, waiting for transfers between devices: 167 us -> none  [the longest x1 102 us: per_device(): full_qkv = lax.all_gather(w_qkv, 'fsdp', axis=0, tiled=True)]
    ppermute x0 -> x43, waiting for transfers between devices: none -> 52.7 us  [the longest x12 23.2 us: ring_gather(): down[i] = lax.ppermute(down[i], 'fsdp', backward)]
    ppermute x0 -> x43, starting transfers between devices: none -> 49.4 us  [the longest x12 19.1 us: ring_gather(): down[i] = lax.ppermute(down[i], 'fsdp', backward)]
    reduce_scatter x1 -> x0, waiting for transfers between devices: 42.4 us -> none  [per_device(): lax.psum_scatter(jnp.dot(frame_major, full_out, preferred_element_type=jn...]
    all_gather x1 -> x0, blocking collectives: 30.5 us -> none  [per_device(): lax.all_gather(pooled, 'fsdp', axis=0, tiled=True)]
    dot_general x5 -> x30, matrix products: 16.7 us -> 27.5 us  [the longest x24 19 us: per_device(): term = jnp.dot(cols, got[c][d], preferred_element_type=jnp.float32)]
    slice x0 -> x8, local copies, waits for them, and re-layouts: none -> 3.71 us  [the longest x4 2.77 us: ring_gather(): second = lax.slice_in_dim(down[i], half, 2 * half, axis=split_dim)]
  transfers between devices with their start and end apart: 4 -> 43, of which waited for: 4 -> 19; matrix products, arithmetic and copies ran while one was open for 4% -> 21% of each run, Pallas kernels for 0% -> 0%
where the time goes in v1:
time: 162 us; the launch traced here: 161 us
  waiting for transfers between devices  52.7 us (33%)
  starting transfers between devices  49.4 us (30%)
  matrix products  28 us (17%)
  between operations  14.6 us (9%)
  local copies, waits for them, and re-layouts  8.96 us (6%)
  other arithmetic  7.72 us (5%)
    ppermute x12, waiting for transfers between devices, ring_gather(): down[i] = lax.ppermute(down[i], 'fsdp', backward)  23.2 us
    ppermute x12, starting transfers between devices, ring_gather(): down[i] = lax.ppermute(down[i], 'fsdp', backward)  19.1 us
    dot_general x24, matrix products, per_device(): term = jnp.dot(cols, got[c][d], preferred_element_type=jnp.float32)  19 us
    ppermute x11, waiting for transfers between devices, exchange(): return lax.ppermute(values, axis, [(i, i ^ bit) for i in range(size)])  16.9 us
    ppermute x11, starting transfers between devices, exchange(): return lax.ppermute(values, axis, [(i, i ^ bit) for i in range(size)])  11.7 us
    ppermute x12, starting transfers between devices, ring_gather(): up[i] = lax.ppermute(up[i], 'fsdp', forward)  10.3 us
    ppermute x4, starting transfers between devices, ring_gather(): second = lax.ppermute(second, 'fsdp', backward)  7.56 us
    ppermute x4, waiting for transfers between devices, ring_gather(): second = lax.ppermute(second, 'fsdp', backward)  7.44 us
  transfers between devices with their start and end apart: 43, of which 19 were waited for; matrix products, arithmetic and copies ran while one was open for 21% of the time, Pallas kernels for 0%

profile of v1, /device:TPU:0, one launch (start us, length us, event | category | flops | bytes accessed | tf_op | source)
XLA Modules:
  0.0 161.4 jit_solution(3171670750731646600)
XLA Ops:
  5.3 2.6 %collective-permute-start.3 = (bf16[256,512]{1,0:T(8,128)(2,1)S(1)}, bf16[256,512]{1,0:T(8,128)(2,1)S(1)}, u32[]{:S(2)}, u32[]{:S(2)}) collective-permute-start(bf16[256,512]{1,0:T(8,128)(2,1)S(1)} %get-tuple-element.17), channel_id=1, source_target_pairs={{8,0},{16,8},{24,16},{28,24},{20,28},{12,20},{4,12},{0,4},{9,1},{1... | collective-permute-start | bytes 786440 | tf_op jit(solution)/shard_map/ppermute | solution.py:32
  10.0 5.1 %collective-permute-done.3 = bf16[256,512]{1,0:T(8,128)(2,1)S(1)} collective-permute-done((bf16[256,512]{1,0:T(8,128)(2,1)S(1)}, bf16[256,512]{1,0:T(8,128)(2,1)S(1)}, u32[]{:S(2)}, u32[]{:S(2)}) %collective-permute-start.3) | collective-permute-done | bytes 262176 | tf_op jit(solution)/shard_map/ppermute | solution.py:32
  17.1 3.6 %collective-permute-done.11 = bf16[256,512]{1,0:T(8,128)(2,1)S(1)} collective-permute-done((bf16[256,512]{1,0:T(8,128)(2,1)S(1)}, bf16[256,512]{1,0:T(8,128)(2,1)S(1)}, u32[]{:S(2)}, u32[]{:S(2)}) %collective-permute-start.11) | collective-permute-done | bytes 262176 | tf_op jit(solution)/shard_map/ppermute | solution.py:32
  26.4 1.9 %collective-permute-start.4 = (bf16[256,512]{1,0:T(8,128)(2,1)S(1)}, bf16[256,512]{1,0:T(8,128)(2,1)}, u32[]{:S(2)}, u32[]{:S(2)}) collective-permute-start(bf16[256,512]{1,0:T(8,128)(2,1)S(1)} %collective-permute-done.2), channel_id=1, source_target_pairs={{0,8},{8,16},{16,24},{24,28},{28,20},{20,12},{12,4},{4,0},{1,9},{9... | collective-permute-start | bytes 786440 | tf_op jit(solution)/shard_map/ppermute | solution.py:31
  29.9 2.1 %collective-permute-done.5 = bf16[256,512]{1,0:T(8,128)(2,1)} collective-permute-done((bf16[256,512]{1,0:T(8,128)(2,1)S(1)}, bf16[256,512]{1,0:T(8,128)(2,1)}, u32[]{:S(2)}, u32[]{:S(2)}) %collective-permute-start.5) | collective-permute-done | bytes 262176 | tf_op jit(solution)/shard_map/ppermute | solution.py:32
  33.9 3.7 %collective-permute-done.13 = bf16[256,512]{1,0:T(8,128)(2,1)} collective-permute-done((bf16[256,512]{1,0:T(8,128)(2,1)S(1)}, bf16[256,512]{1,0:T(8,128)(2,1)}, u32[]{:S(2)}, u32[]{:S(2)}) %collective-permute-start.13) | collective-permute-done | bytes 262176 | tf_op jit(solution)/shard_map/ppermute | solution.py:32
  43.3 1.9 %collective-permute-start.6 = (bf16[256,512]{1,0:T(8,128)(2,1)}, bf16[256,512]{1,0:T(8,128)(2,1)S(1)}, u32[]{:S(2)}, u32[]{:S(2)}) collective-permute-start(bf16[256,512]{1,0:T(8,128)(2,1)} %collective-permute-done.4), channel_id=1, source_target_pairs={{0,8},{8,16},{16,24},{24,28},{28,20},{20,12},{12,4},{4,0},{1,9},{9... | collective-permute-start | bytes 786440 | tf_op jit(solution)/shard_map/ppermute | solution.py:31
  45.2 3.7 %collective-permute-done.15 = bf16[256,512]{1,0:T(8,128)(2,1)} collective-permute-done((bf16[256,512]{1,0:T(8,128)(2,1)}, bf16[256,512]{1,0:T(8,128)(2,1)}, u32[]{:S(2)}, u32[]{:S(2)}) %collective-permute-start.15) | collective-permute-done | bytes 262176 | tf_op jit(solution)/shard_map/ppermute | solution.py:32
  48.9 1.9 %collective-permute-start.14 = (bf16[256,512]{1,0:T(8,128)(2,1)}, bf16[256,512]{1,0:T(8,128)(2,1)S(1)}, u32[]{:S(2)}, u32[]{:S(2)}) collective-permute-start(bf16[256,512]{1,0:T(8,128)(2,1)} %collective-permute-done.12), channel_id=1, source_target_pairs={{0,8},{8,16},{16,24},{24,28},{28,20},{20,12},{12,4},{4,0},{1,9},{9... | collective-permute-start | bytes 786440 | tf_op jit(solution)/shard_map/ppermute | solution.py:31
  51.6 2.9 %collective-permute-done.7 = bf16[256,512]{1,0:T(8,128)(2,1)} collective-permute-done((bf16[256,512]{1,0:T(8,128)(2,1)}, bf16[256,512]{1,0:T(8,128)(2,1)}, u32[]{:S(2)}, u32[]{:S(2)}) %collective-permute-start.7) | collective-permute-done | bytes 262176 | tf_op jit(solution)/shard_map/ppermute | solution.py:32
  54.5 1.9 %collective-permute-start.22 = (bf16[256,512]{1,0:T(8,128)(2,1)}, bf16[256,512]{1,0:T(8,128)(2,1)}, u32[]{:S(2)}, u32[]{:S(2)}) collective-permute-start(bf16[256,512]{1,0:T(8,128)(2,1)} %collective-permute-done.20), channel_id=1, source_target_pairs={{0,8},{8,16},{16,24},{24,28},{28,20},{20,12},{12,4},{4,0},{1,9},{9... | collective-permute-start | bytes 786440 | tf_op jit(solution)/shard_map/ppermute | solution.py:31
  56.5 3.0 %collective-permute-done.14 = bf16[256,512]{1,0:T(8,128)(2,1)S(1)} collective-permute-done((bf16[256,512]{1,0:T(8,128)(2,1)}, bf16[256,512]{1,0:T(8,128)(2,1)S(1)}, u32[]{:S(2)}, u32[]{:S(2)}) %collective-permute-start.14) | collective-permute-done | bytes 262176 | tf_op jit(solution)/shard_map/ppermute | solution.py:31
  74.9 2.1 %collective-permute-start.9 = (bf16[128,512]{1,0:T(8,128)(2,1)S(1)}, bf16[128,512]{1,0:T(8,128)(2,1)S(1)}, u32[]{:S(2)}, u32[]{:S(2)}) collective-permute-start(bf16[128,512]{1,0:T(8,128)(2,1)S(1)} %slice.135), channel_id=1, source_target_pairs={{8,0},{16,8},{24,16},{28,24},{20,28},{12,20},{4,12},{0,4},{9,1},{1... | collective-permute-start | bytes 393224 | tf_op jit(solution)/shard_map/ppermute | solution.py:41
  97.0 4.0 %collective-permute-done.25 = bf16[128,512]{1,0:T(8,128)(2,1)S(1)} collective-permute-done((bf16[128,512]{1,0:T(8,128)(2,1)S(1)}, bf16[128,512]{1,0:T(8,128)(2,1)S(1)}, u32[]{:S(2)}, u32[]{:S(2)}) %collective-permute-start.25) | collective-permute-done | bytes 131104 | tf_op jit(solution)/shard_map/ppermute | solution.py:41
  100.9 2.0 %collective-permute-start.35 = (bf16[512,256]{1,0:T(8,128)(2,1)}, bf16[512,256]{1,0:T(8,128)(2,1)S(1)}, u32[]{:S(2)}, u32[]{:S(2)}) collective-permute-start(bf16[512,256]{1,0:T(8,128)(2,1)} %collective-permute-done.31), channel_id=1, source_target_pairs={{8,0},{16,8},{24,16},{28,24},{20,28},{12,20},{4,12},{0,4},{9,1},{1... | collective-permute-start | bytes 786440 | tf_op jit(solution)/shard_map/ppermute | solution.py:32
  118.6 2.0 %collective-permute-start.37 = (bf16[512,128]{1,0:T(8,128)(2,1)S(1)}, bf16[512,128]{1,0:T(8,128)(2,1)S(1)}, u32[]{:S(2)}, u32[]{:S(2)}) collective-permute-start(bf16[512,128]{1,0:T(8,128)(2,1)S(1)} %slice.154), channel_id=1, source_target_pairs={{8,0},{16,8},{24,16},{28,24},{20,28},{12,20},{4,12},{0,4},{9,1},{1... | collective-permute-start | bytes 393224 | tf_op jit(solution)/shard_map/ppermute | solution.py:41
  121.0 3.5 %collective-permute-done.37 = bf16[512,128]{1,0:T(8,128)(2,1)S(1)} collective-permute-done((bf16[512,128]{1,0:T(8,128)(2,1)S(1)}, bf16[512,128]{1,0:T(8,128)(2,1)S(1)}, u32[]{:S(2)}, u32[]{:S(2)}) %collective-permute-start.37) | collective-permute-done | bytes 131104 | tf_op jit(solution)/shard_map/ppermute | solution.py:41
  129.4 4.1 %collective-permute-done.33 = bf16[1,128,512]{2,1,0:T(8,128)(2,1)S(1)} collective-permute-done((bf16[1,128,512]{2,1,0:T(8,128)(2,1)S(1)}, bf16[1,128,512]{2,1,0:T(8,128)(2,1)S(1)}, u32[]{:S(2)}, u32[]{:S(2)}) %collective-permute-start.33) | collective-permute-done | bytes 131104 | tf_op jit(solution)/shard_map/ppermute | solution.py:47
  135.3 2.4 %collective-permute-done.29 = bf16[1,128,768]{2,1,0:T(8,128)(2,1)S(1)} collective-permute-done((bf16[1,128,768]{2,1,0:T(8,128)(2,1)S(1)}, bf16[1,128,768]{2,1,0:T(8,128)(2,1)S(1)}, u32[]{:S(2)}, u32[]{:S(2)}) %collective-permute-start.29) | collective-permute-done | bytes 196640 | tf_op jit(solution)/shard_map/ppermute | solution.py:47
  137.7 3.8 %collective-permute-done.39 = bf16[1,128,768]{2,1,0:T(8,128)(2,1)S(1)} collective-permute-done((bf16[1,128,768]{2,1,0:T(8,128)(2,1)S(1)}, bf16[1,128,768]{2,1,0:T(8,128)(2,1)S(1)}, u32[]{:S(2)}, u32[]{:S(2)}) %collective-permute-start.39) | collective-permute-done | bytes 196640 | tf_op jit(solution)/shard_map/ppermute | solution.py:47
  150.2 2.4 %collective-permute-done.41 = bf16[2,2048]{1,0:T(2,128)(2,1)S(1)} collective-permute-done((bf16[2,2048]{1,0:T(2,128)(2,1)S(1)}, bf16[2,2048]{1,0:T(2,128)(2,1)S(1)}, u32[]{:S(2)}, u32[]{:S(2)}) %collective-permute-start.41) | collective-permute-done | bytes 8224 | tf_op jit(solution)/shard_map/ppermute | solution.py:47
  152.6 2.3 %collective-permute-start.42 = (bf16[4,2048]{1,0:T(4,128)(2,1)S(1)}, bf16[4,2048]{1,0:T(4,128)(2,1)S(1)}, u32[]{:S(2)}, u32[]{:S(2)}) collective-permute-start(bf16[4,2048]{1,0:T(4,128)(2,1)S(1)} %pad_maximum_fusion.3), channel_id=1, source_target_pairs={{0,16},{4,20},{8,24},{12,28},{16,0},{20,4},{24,8},{28,12},{1,17},{... | collective-permute-start | bytes 49160 | tf_op jit(solution)/shard_map/ppermute | solution.py:47
  154.9 2.4 %collective-permute-done.42 = bf16[4,2048]{1,0:T(4,128)(2,1)S(1)} collective-permute-done((bf16[4,2048]{1,0:T(4,128)(2,1)S(1)}, bf16[4,2048]{1,0:T(4,128)(2,1)S(1)}, u32[]{:S(2)}, u32[]{:S(2)}) %collective-permute-start.42) | collective-permute-done | bytes 16416 | tf_op jit(solution)/shard_map/ppermute | solution.py:47
  157.9 2.8 %fusion.30 = f32[8,1,1,1024]{3,0,2,1:T(8,128)S(1)} fusion(bf16[8,2048]{1,0:T(8,128)(2,1)S(1)} %gather_fusion.1, bf16[2048,1024]{1,0:T(8,128)(2,1)} %param.13, f32[1024]{0:T(1024)S(1)} %bitcast.244), kind=kOutput, calls=%fused_computation.40 | convolution fusion | flops 33562624 | bytes 4263936 | tf_op jit(solution)/shard_map/dot_general | solution.py:140
  (213 shorter events, 78.7 us)
Async XLA Ops:
  4.7 17.9 %collective-permute-start = (bf16[1,128,2048]{2,1,0:T(8,128)(2,1)S(1)}, bf16[1,128,2048]{2,1,0:T(8,128)(2,1)S(1)}, u32[]{:S(2)}, u32[]{:S(2)}) collective-permute-start(bf16[1,128,2048]{2,1,0:T(8,128)(2,1)S(1)} %fusion.33), channel_id=1, source_target_pairs={{0,1},{1,0},{2,3},{3,2},{4,5},{5,4},{6,7},{7,6},{8,9},{9,8},{10,11... | collective-permute-start | bytes 1572872 | tf_op jit(solution)/shard_map/ppermute | solution.py:47
  8.0 12.7 %collective-permute-start.11 = (bf16[256,512]{1,0:T(8,128)(2,1)S(1)}, bf16[256,512]{1,0:T(8,128)(2,1)S(1)}, u32[]{:S(2)}, u32[]{:S(2)}) collective-permute-start(bf16[256,512]{1,0:T(8,128)(2,1)S(1)} %get-tuple-element.18), channel_id=1, source_target_pairs={{8,0},{16,8},{24,16},{28,24},{20,28},{12,20},{4,12},{0,4},{9,1},{1... | collective-permute-start | bytes 786440 | tf_op jit(solution)/shard_map/ppermute | solution.py:32
  9.9 14.4 %collective-permute-start.10 = (bf16[256,512]{1,0:T(8,128)(2,1)S(1)}, bf16[256,512]{1,0:T(8,128)(2,1)S(1)}, u32[]{:S(2)}, u32[]{:S(2)}) collective-permute-start(bf16[256,512]{1,0:T(8,128)(2,1)S(1)} %get-tuple-element.18), channel_id=1, source_target_pairs={{0,8},{8,16},{16,24},{24,28},{28,20},{20,12},{12,4},{4,0},{1,9},{9... | collective-permute-start | bytes 786440 | tf_op jit(solution)/shard_map/ppermute | solution.py:31
  15.1 11.3 %collective-permute-start.19 = (bf16[256,512]{1,0:T(8,128)(2,1)S(1)}, bf16[256,512]{1,0:T(8,128)(2,1)}, u32[]{:S(2)}, u32[]{:S(2)}) collective-permute-start(bf16[256,512]{1,0:T(8,128)(2,1)S(1)} %get-tuple-element.16), channel_id=1, source_target_pairs={{8,0},{16,8},{24,16},{28,24},{20,28},{12,20},{4,12},{0,4},{9,1},{1... | collective-permute-start | bytes 786440 | tf_op jit(solution)/shard_map/ppermute | solution.py:32
  17.0 11.4 %collective-permute-start.18 = (bf16[256,512]{1,0:T(8,128)(2,1)S(1)}, bf16[256,512]{1,0:T(8,128)(2,1)S(1)}, u32[]{:S(2)}, u32[]{:S(2)}) collective-permute-start(bf16[256,512]{1,0:T(8,128)(2,1)S(1)} %get-tuple-element.16), channel_id=1, source_target_pairs={{0,8},{8,16},{16,24},{24,28},{28,20},{20,12},{12,4},{4,0},{1,9},{9... | collective-permute-start | bytes 786440 | tf_op jit(solution)/shard_map/ppermute | solution.py:31
  20.7 11.3 %collective-permute-start.5 = (bf16[256,512]{1,0:T(8,128)(2,1)S(1)}, bf16[256,512]{1,0:T(8,128)(2,1)}, u32[]{:S(2)}, u32[]{:S(2)}) collective-permute-start(bf16[256,512]{1,0:T(8,128)(2,1)S(1)} %collective-permute-done.3), channel_id=1, source_target_pairs={{8,0},{16,8},{24,16},{28,24},{20,28},{12,20},{4,12},{0,4},{9,1},{1... | collective-permute-start | bytes 786440 | tf_op jit(solution)/shard_map/ppermute | solution.py:32
  22.6 15.1 %collective-permute-start.13 = (bf16[256,512]{1,0:T(8,128)(2,1)S(1)}, bf16[256,512]{1,0:T(8,128)(2,1)}, u32[]{:S(2)}, u32[]{:S(2)}) collective-permute-start(bf16[256,512]{1,0:T(8,128)(2,1)S(1)} %collective-permute-done.11), channel_id=1, source_target_pairs={{8,0},{16,8},{24,16},{28,24},{20,28},{12,20},{4,12},{0,4},{9,1},{1... | collective-permute-start | bytes 786440 | tf_op jit(solution)/shard_map/ppermute | solution.py:32
  24.3 58.4 %collective-permute-start.1 = (bf16[2,128,2048]{2,1,0:T(8,128)(2,1)S(1)}, bf16[2,128,2048]{2,1,0:T(8,128)(2,1)}, u32[]{:S(2)}, u32[]{:S(2)}) collective-permute-start(bf16[2,128,2048]{2,1,0:T(8,128)(2,1)S(1)} %pad_maximum_fusion.1), channel_id=1, source_target_pairs={{0,2},{1,3},{2,0},{3,1},{4,6},{5,7},{6,4},{7,5},{8,10},{9,11},{10,... | collective-permute-start | bytes 3145736 | tf_op jit(solution)/shard_map/ppermute | solution.py:47
  26.4 13.1 %collective-permute-start.4 = (bf16[256,512]{1,0:T(8,128)(2,1)S(1)}, bf16[256,512]{1,0:T(8,128)(2,1)}, u32[]{:S(2)}, u32[]{:S(2)}) collective-permute-start(bf16[256,512]{1,0:T(8,128)(2,1)S(1)} %collective-permute-done.2), channel_id=1, source_target_pairs={{0,8},{8,16},{16,24},{24,28},{28,20},{20,12},{12,4},{4,0},{1,9},{9... | collective-permute-start | bytes 786440 | tf_op jit(solution)/shard_map/ppermute | solution.py:31
  28.4 11.7 %collective-permute-start.12 = (bf16[256,512]{1,0:T(8,128)(2,1)S(1)}, bf16[256,512]{1,0:T(8,128)(2,1)}, u32[]{:S(2)}, u32[]{:S(2)}) collective-permute-start(bf16[256,512]{1,0:T(8,128)(2,1)S(1)} %collective-permute-done.10), channel_id=1, source_target_pairs={{0,8},{8,16},{16,24},{24,28},{28,20},{20,12},{12,4},{4,0},{1,9},{9... | collective-permute-start | bytes 786440 | tf_op jit(solution)/shard_map/ppermute | solution.py:31
  39.6 12.0 %collective-permute-start.20 = (bf16[256,512]{1,0:T(8,128)(2,1)}, bf16[256,512]{1,0:T(8,128)(2,1)}, u32[]{:S(2)}, u32[]{:S(2)}) collective-permute-start(bf16[256,512]{1,0:T(8,128)(2,1)} %copy-done.13), channel_id=1, source_target_pairs={{0,8},{8,16},{16,24},{24,28},{28,20},{20,12},{12,4},{4,0},{1,9},{9... | collective-permute-start | bytes 786440 | tf_op jit(solution)/shard_map/ppermute | solution.py:31
  40.0 14.4 %collective-permute-start.7 = (bf16[256,512]{1,0:T(8,128)(2,1)}, bf16[256,512]{1,0:T(8,128)(2,1)}, u32[]{:S(2)}, u32[]{:S(2)}) collective-permute-start(bf16[256,512]{1,0:T(8,128)(2,1)} %collective-permute-done.5), channel_id=1, source_target_pairs={{8,0},{16,8},{24,16},{28,24},{20,28},{12,20},{4,12},{0,4},{9,1},{1... | collective-permute-start | bytes 786440 | tf_op jit(solution)/shard_map/ppermute | solution.py:32
  43.3 13.2 %collective-permute-start.6 = (bf16[256,512]{1,0:T(8,128)(2,1)}, bf16[256,512]{1,0:T(8,128)(2,1)S(1)}, u32[]{:S(2)}, u32[]{:S(2)}) collective-permute-start(bf16[256,512]{1,0:T(8,128)(2,1)} %collective-permute-done.4), channel_id=1, source_target_pairs={{0,8},{8,16},{16,24},{24,28},{28,20},{20,12},{12,4},{4,0},{1,9},{9... | collective-permute-start | bytes 786440 | tf_op jit(solution)/shard_map/ppermute | solution.py:31
  51.6 23.4 %collective-permute-start.23 = (bf16[256,512]{1,0:T(8,128)(2,1)}, bf16[256,512]{1,0:T(8,128)(2,1)}, u32[]{:S(2)}, u32[]{:S(2)}) collective-permute-start(bf16[256,512]{1,0:T(8,128)(2,1)} %collective-permute-done.21), channel_id=1, source_target_pairs={{8,0},{16,8},{24,16},{28,24},{20,28},{12,20},{4,12},{0,4},{9,1},{1... | collective-permute-start | bytes 786440 | tf_op jit(solution)/shard_map/ppermute | solution.py:32
  54.5 23.4 %collective-permute-start.22 = (bf16[256,512]{1,0:T(8,128)(2,1)}, bf16[256,512]{1,0:T(8,128)(2,1)}, u32[]{:S(2)}, u32[]{:S(2)}) collective-permute-start(bf16[256,512]{1,0:T(8,128)(2,1)} %collective-permute-done.20), channel_id=1, source_target_pairs={{0,8},{8,16},{16,24},{24,28},{28,20},{20,12},{12,4},{4,0},{1,9},{9... | collective-permute-start | bytes 786440 | tf_op jit(solution)/shard_map/ppermute | solution.py:31
  56.4 24.1 %collective-permute-start.27 = (bf16[512,256]{1,0:T(8,128)(2,1)}, bf16[512,256]{1,0:T(8,128)(2,1)}, u32[]{:S(2)}, u32[]{:S(2)}) collective-permute-start(bf16[512,256]{1,0:T(8,128)(2,1)} %param.12), channel_id=1, source_target_pairs={{8,0},{16,8},{24,16},{28,24},{20,28},{12,20},{4,12},{0,4},{9,1},{1... | collective-permute-start | bytes 786440 | tf_op jit(solution)/shard_map/ppermute | solution.py:32
  59.5 21.5 %collective-permute-start.26 = (bf16[512,256]{1,0:T(8,128)(2,1)}, bf16[512,256]{1,0:T(8,128)(2,1)}, u32[]{:S(2)}, u32[]{:S(2)}) collective-permute-start(bf16[512,256]{1,0:T(8,128)(2,1)} %param.12), channel_id=1, source_target_pairs={{0,8},{8,16},{16,24},{24,28},{28,20},{20,12},{12,4},{4,0},{1,9},{9... | collective-permute-start | bytes 786440 | tf_op jit(solution)/shard_map/ppermute | solution.py:31
  74.9 36.5 %collective-permute-start.9 = (bf16[128,512]{1,0:T(8,128)(2,1)S(1)}, bf16[128,512]{1,0:T(8,128)(2,1)S(1)}, u32[]{:S(2)}, u32[]{:S(2)}) collective-permute-start(bf16[128,512]{1,0:T(8,128)(2,1)S(1)} %slice.135), channel_id=1, source_target_pairs={{8,0},{16,8},{24,16},{28,24},{20,28},{12,20},{4,12},{0,4},{9,1},{1... | collective-permute-start | bytes 393224 | tf_op jit(solution)/shard_map/ppermute | solution.py:41
  77.9 16.6 %collective-permute-start.17 = (bf16[128,512]{1,0:T(8,128)(2,1)S(1)}, bf16[128,512]{1,0:T(8,128)(2,1)S(1)}, u32[]{:S(2)}, u32[]{:S(2)}) collective-permute-start(bf16[128,512]{1,0:T(8,128)(2,1)S(1)} %slice.137), channel_id=1, source_target_pairs={{8,0},{16,8},{24,16},{28,24},{20,28},{12,20},{4,12},{0,4},{9,1},{1... | collective-permute-start | bytes 393224 | tf_op jit(solution)/shard_map/ppermute | solution.py:41
  80.6 15.7 %collective-permute-start.16 = (bf16[128,512]{1,0:T(8,128)(2,1)S(1)}, bf16[128,512]{1,0:T(8,128)(2,1)S(1)}, u32[]{:S(2)}, u32[]{:S(2)}) collective-permute-start(bf16[128,512]{1,0:T(8,128)(2,1)S(1)} %slice.136), channel_id=1, source_target_pairs={{0,8},{8,16},{16,24},{24,28},{28,20},{20,12},{12,4},{4,0},{1,9},{9... | collective-permute-start | bytes 393224 | tf_op jit(solution)/shard_map/ppermute | solution.py:40
  81.0 19.9 %collective-permute-start.31 = (bf16[512,256]{1,0:T(8,128)(2,1)}, bf16[512,256]{1,0:T(8,128)(2,1)}, u32[]{:S(2)}, u32[]{:S(2)}) collective-permute-start(bf16[512,256]{1,0:T(8,128)(2,1)} %collective-permute-done.27), channel_id=1, source_target_pairs={{8,0},{16,8},{24,16},{28,24},{20,28},{12,20},{4,12},{0,4},{9,1},{1... | collective-permute-start | bytes 786440 | tf_op jit(solution)/shard_map/ppermute | solution.py:32
  82.7 20.3 %collective-permute-start.30 = (bf16[512,256]{1,0:T(8,128)(2,1)}, bf16[512,256]{1,0:T(8,128)(2,1)S(1)}, u32[]{:S(2)}, u32[]{:S(2)}) collective-permute-start(bf16[512,256]{1,0:T(8,128)(2,1)} %collective-permute-done.26), channel_id=1, source_target_pairs={{0,8},{8,16},{16,24},{24,28},{28,20},{20,12},{12,4},{4,0},{1,9},{9... | collective-permute-start | bytes 786440 | tf_op jit(solution)/shard_map/ppermute | solution.py:31
  100.9 17.6 %collective-permute-start.35 = (bf16[512,256]{1,0:T(8,128)(2,1)}, bf16[512,256]{1,0:T(8,128)(2,1)S(1)}, u32[]{:S(2)}, u32[]{:S(2)}) collective-permute-start(bf16[512,256]{1,0:T(8,128)(2,1)} %collective-permute-done.31), channel_id=1, source_target_pairs={{8,0},{16,8},{24,16},{28,24},{20,28},{12,20},{4,12},{0,4},{9,1},{1... | collective-permute-start | bytes 786440 | tf_op jit(solution)/shard_map/ppermute | solution.py:32
  103.0 17.7 %collective-permute-start.34 = (bf16[512,256]{1,0:T(8,128)(2,1)S(1)}, bf16[512,256]{1,0:T(8,128)(2,1)S(1)}, u32[]{:S(2)}, u32[]{:S(2)}) collective-permute-start(bf16[512,256]{1,0:T(8,128)(2,1)S(1)} %collective-permute-done.30), channel_id=1, source_target_pairs={{0,8},{8,16},{16,24},{24,28},{28,20},{20,12},{12,4},{4,0},{1,9},{9... | collective-permute-start | bytes 786440 | tf_op jit(solution)/shard_map/ppermute | solution.py:31
  (38 other events, 559.9 us)

commit v2 on v0

v2 whole, which is shorter than its diff:
```python
import functools
import math

import jax
import jax.numpy as jnp
from jax import lax
from jax.experimental import pallas as pl
from jax.experimental.pallas import tpu as pltpu
from jax.sharding import PartitionSpec as P

DH = 128
LANES = 128
PAIR = 2
F32 = jnp.float32
BF16 = jnp.bfloat16
VMEM = pl.BlockSpec(memory_space=pltpu.VMEM)
SMEM = pl.BlockSpec(memory_space=pltpu.SMEM)
PARAMS = pltpu.CompilerParams(vmem_limit_bytes=40 * 2**20)


def normalize(values):
    centre = jnp.mean(values, axis=-1, keepdims=True)
    spread = jnp.mean(jnp.square(values - centre), axis=-1, keepdims=True)
    return (values - centre) * lax.rsqrt(spread + 1e-05)


def after(value, *done):
    return lax.optimization_barrier((value, *done))[0]


def cost(flops, size):
    return pl.CostEstimate(flops=flops, bytes_accessed=size, transcendentals=0)


def norm_kernel(order_ref, tokens_ref, normed_ref, mean_ref):
    values = tokens_ref[...].astype(F32)
    width = values.shape[1]
    centre = jnp.mean(values, axis=1, keepdims=True)
    spread = jnp.mean(jnp.square(values - centre), axis=1, keepdims=True)
    scale = lax.rsqrt(spread + 1e-05)
    mean_ref[...] = jnp.mean(values, axis=0, keepdims=True)
    count = order_ref.shape[0]
    block = width // count
    for i in range(count):
        at = pl.multiple_of(order_ref[i] * block, LANES)
        piece = tokens_ref[:, pl.ds(at, block)].astype(F32)
        normed_ref[:, i * block : (i + 1) * block] = ((piece - centre) * scale).astype(BF16)


def norm_call(order, tokens):
    rows, width = tokens.shape
    return pl.pallas_call(
        norm_kernel,
        out_shape=(
            jax.ShapeDtypeStruct((rows, width), BF16),
            jax.ShapeDtypeStruct((1, width), F32),
        ),
        in_specs=[SMEM, VMEM],
        out_specs=(VMEM, VMEM),
        compiler_params=PARAMS,
        cost_estimate=cost(8 * rows * width, 4 * rows * width),
        name="norm",
    )(order, tokens)


def project(rows, slots, swap):
    total = None
    block = slots[0].shape[0]
    for i, slot in enumerate(slots):
        j = i ^ 1 if swap else i
        term = jnp.dot(rows[:, j * block : (j + 1) * block], slot, preferred_element_type=F32)
        total = term if total is None else total + term
    return total.astype(BF16)


def slot_list(refs):
    return [ref[i] for ref in refs for i in range(ref.shape[0])]


def project_kernel(tensors, pieces, *refs):
    tokens = refs[:4]
    weights = refs[4 : 4 + tensors * pieces]
    outs = refs[4 + tensors * pieces :]
    for t in range(tensors):
        slots = slot_list(weights[t * pieces : (t + 1) * pieces])
        for w in range(2):
            half = 0
            for source, swap in ((tokens[w], False), (tokens[2 + w], True)):
                for frame in range(source.shape[0]):
                    rows = source.shape[1]
                    outs[t][w, half : half + rows, :] = project(source[frame], slots, swap)
                    half += rows


def project_call(tokens, weights):
    pieces = len(weights[0])
    rows = 2 * tokens[0].shape[0] * tokens[0].shape[1]
    columns = weights[0][0].shape[-1]
    depth = tokens[0].shape[2]
    flat = [w for tensor in weights for w in tensor]
    shape = jax.ShapeDtypeStruct((2, rows, columns), BF16)
    return pl.pallas_call(
        functools.partial(project_kernel, len(weights), pieces),
        out_shape=[shape] * len(weights),
        in_specs=[VMEM] * (4 + len(flat)),
        out_specs=[VMEM] * len(weights),
        compiler_params=PARAMS,
        cost_estimate=cost(4 * rows * columns * depth * len(weights), 4 * rows * depth),
        name="project",
    )(*tokens, *flat)


def attend_kernel(pieces, mask_ref, q_ref, k_ref, *refs):
    tokens = refs[:4]
    slots = slot_list(refs[4 : 4 + pieces])
    own_ref, pair_ref = refs[4 + pieces :]
    scale = 1.0 / math.sqrt(DH)
    for w, out in ((0, own_ref), (1, pair_ref)):
        parts = []
        for source, swap in ((tokens[w], False), (tokens[2 + w], True)):
            for frame in range(source.shape[0]):
                parts.append(project(source[frame], slots, swap))
        v = jnp.concatenate(parts, axis=0)
        for head in range(v.shape[1] // DH):
            at = slice(head * DH, (head + 1) * DH)
            scores = lax.dot_general(
                q_ref[w, :, at], k_ref[w, :, at], (((1,), (1,)), ((), ())), preferred_element_type=F32
            )
            weights = jnp.exp(scores * scale) * mask_ref[w]
            totals = jnp.sum(weights, axis=1, keepdims=True)
            mixed = jnp.dot(weights.astype(BF16), v[:, at], preferred_element_type=F32)
            out[:, at] = (mixed / totals).astype(BF16)


def attend_call(mask, q, k, tokens, v_slots):
    rows, columns = q.shape[1], q.shape[2]
    shape = jax.ShapeDtypeStruct((rows, columns), BF16)
    depth = tokens[0].shape[2]
    return pl.pallas_call(
        functools.partial(attend_kernel, len(v_slots)),
        out_shape=(shape, shape),
        in_specs=[VMEM] * (7 + len(v_slots)),
        out_specs=(VMEM, VMEM),
        compiler_params=PARAMS,
        cost_estimate=cost(4 * rows * columns * (depth + 2 * rows), 4 * rows * depth),
        name="attend",
    )(mask, q, k, *tokens, *v_slots)


def join_kernel(frames, flag_ref, own_ref, came_ref, mixed_ref, mean_ref):
    half = own_ref.shape[1]
    rows = own_ref.shape[0] // frames

    def write(first, second):
        for j, source in ((0, first), (1, second)):
            at = slice(j * half, (j + 1) * half)
            mixed_ref[:, at] = source[...]
            for frame in range(frames):
                part = source[frame * rows : (frame + 1) * rows, :].astype(F32)
                mean_ref[frame : frame + 1, at] = jnp.mean(part, axis=0, keepdims=True)

    @pl.when(flag_ref[0] == 0)
    def _():
        write(own_ref, came_ref)

    @pl.when(flag_ref[0] != 0)
    def _():
        write(came_ref, own_ref)


def join_call(flag, own, came, frames):
    rows, half = own.shape
    return pl.pallas_call(
        functools.partial(join_kernel, frames),
        out_shape=(
            jax.ShapeDtypeStruct((rows, 2 * half), BF16),
            jax.ShapeDtypeStruct((frames, 2 * half), F32),
        ),
        in_specs=[SMEM, VMEM, VMEM],
        out_specs=(VMEM, VMEM),
        compiler_params=PARAMS,
        cost_estimate=cost(4 * rows * half, 8 * rows * half),
        name="join",
    )(flag, own, came)


def times_block(values, parts):
    total, at = None, 0
    for part in parts:
        term = jnp.dot(values[:, at : at + part.shape[0]], part[...], preferred_element_type=F32)
        total = term if total is None else total + term
        at += part.shape[0]
    return total


def out_kernel(counts, mixed_ref, *refs):
    blocks, at = [], 0
    for count in counts:
        blocks.append(refs[at : at + count])
        at += count
    send_ref, keep_ref = refs[at:]
    half = mixed_ref.shape[0] // 2
    columns = blocks[0][0].shape[1]
    for i, parts in enumerate(blocks):
        result = times_block(mixed_ref, parts)
        keep_ref[:, i * columns : (i + 1) * columns] = result[:half]
        send_ref[:, i * columns : (i + 1) * columns] = result[half:].astype(BF16)


def out_call(mixed, blocks):
    flat = [part for parts in blocks for part in parts]
    rows, depth = mixed.shape
    columns = len(blocks) * blocks[0][0].shape[1]
    return pl.pallas_call(
        functools.partial(out_kernel, [len(parts) for parts in blocks]),
        out_shape=(
            jax.ShapeDtypeStruct((rows // 2, columns), BF16),
            jax.ShapeDtypeStruct((rows // 2, columns), F32),
        ),
        in_specs=[VMEM] * (1 + len(flat)),
        out_specs=(VMEM, VMEM),
        compiler_params=PARAMS,
        cost_estimate=cost(2 * rows * columns * depth, 2 * depth * columns + 6 * rows * columns),
        name="out",
    )(mixed, *flat)


def pool_kernel(counts, frames, means_ref, *refs):
    blocks, at = [], 0
    for count in counts:
        blocks.append(refs[at : at + count])
        at += count
    send_ref, keep_ref = refs[at:]
    rows = means_ref.shape[0]
    values = means_ref[...]
    upper = values.astype(BF16)
    lower = (values - upper.astype(F32)).astype(BF16)
    both = jnp.concatenate([upper, lower], axis=0)
    columns = blocks[0][0].shape[1]
    for i, parts in enumerate(blocks):
        result = times_block(both, parts)
        result = result[:rows] + result[rows:]
        keep_ref[:, i * columns : (i + 1) * columns] = result[: rows // 2]
        send_ref[:, i * columns : (i + 1) * columns] = result[rows // 2 :]


def pool_call(means, blocks, frames):
    flat = [part for parts in blocks for part in parts]
    rows, depth = means.shape
    columns = len(blocks) * blocks[0][0].shape[1]
    shape = jax.ShapeDtypeStruct((rows // 2, columns), F32)
    return pl.pallas_call(
        functools.partial(pool_kernel, [len(parts) for parts in blocks], frames),
        out_shape=(shape, shape),
        in_specs=[VMEM] * (1 + len(flat)),
        out_specs=(VMEM, VMEM),
        compiler_params=PARAMS,
        cost_estimate=cost(4 * rows * columns * depth, 2 * depth * columns),
        name="pool",
    )(means, *flat)


def finish_kernel(groups, owners_ref, tokens_ref, *refs):
    out_ref = refs[-1]
    rows = tokens_ref.shape[0]
    slot = 0
    block = tokens_ref.shape[1] // owners_ref.shape[0]
    for g in range(groups):
        sums, came = refs[2 * g], refs[2 * g + 1]
        for i in range(sums.shape[1] // block):
            at = pl.ds(pl.multiple_of(owners_ref[slot] * block, LANES), block)
            here = slice(i * block, (i + 1) * block)
            total = sums[:rows, here] + came[:, here].astype(F32)
            out_ref[:, at] = (tokens_ref[:, at].astype(F32) + total).astype(BF16)
            slot += 1


def finish_call(owners, tokens, sums):
    flat = [part for pair in sums for part in pair]
    return pl.pallas_call(
        functools.partial(finish_kernel, len(sums)),
        out_shape=jax.ShapeDtypeStruct(tokens.shape, BF16),
        in_specs=[SMEM, VMEM] + [VMEM] * len(flat),
        out_specs=VMEM,
        compiler_params=PARAMS,
        cost_estimate=cost(4 * tokens.size, 10 * tokens.size),
        name="finish",
    )(owners, tokens, *flat)


def head_kernel(owners_ref, windows_ref, sums_ref, came_ref, means_ref, act_ref, bias_ref, out_ref, pooled):
    count = owners_ref.shape[0]
    windows, width = means_ref.shape
    block = width // count
    for i in range(count):
        at = pl.ds(pl.multiple_of(owners_ref[i] * block, LANES), block)
        here = slice(i * block, (i + 1) * block)
        pooled[:, at] = sums_ref[:windows, here] + came_ref[:, here] + means_ref[:, at]
    values = normalize(pooled[...]).astype(BF16)
    logits = jnp.dot(values, act_ref[...], preferred_element_type=F32) + bias_ref[...]
    for i in range(windows):
        out_ref[pl.ds(windows_ref[i], 1), 0, 0, :] = logits[i : i + 1]


def head_call(owners, windows, sums, came, means, act, bias):
    columns = act.shape[1]
    return pl.pallas_call(
        head_kernel,
        out_shape=jax.ShapeDtypeStruct((means.shape[0], 1, 1, columns), F32),
        in_specs=[SMEM, SMEM] + [VMEM] * 5,
        out_specs=VMEM,
        scratch_shapes=[pltpu.VMEM(means.shape, F32)],
        compiler_params=PARAMS,
        cost_estimate=cost(2 * means.size * columns, 2 * act.size),
        name="head",
    )(owners, windows, sums, came, means, act, bias)


def ring_order(n):
    return list(range(0, n, 2)) + list(range(1, n, 2))[::-1]


def make(mesh):
    fsdp, seq = mesh.shape["fsdp"], mesh.shape["seq"]
    both = ("fsdp", "seq")
    order = ring_order(fsdp)
    place = [order.index(i) for i in range(fsdp)]
    forward = [(order[i], order[(i + 1) % fsdp]) for i in range(fsdp)]
    backward = [(b, a) for a, b in forward]
    wide_bits = [1 << i for i in range(1, (seq - 1).bit_length())]
    gather_bits = [1 << i for i in reversed(range((fsdp - 1).bit_length())) if (1 << i) != PAIR]

    def over_fsdp(value, bit):
        return lax.ppermute(value, "fsdp", [(i, i ^ bit) for i in range(fsdp)])

    def over_seq(value, bit):
        return lax.ppermute(value, "seq", [(i, i ^ bit) for i in range(seq)])

    def turn(value, k):
        pairs = []
        for f in range(fsdp):
            for s in range(seq):
                c, p = s & 1, (f // PAIR) & 1
                to_f = (f & ~PAIR) | (c * PAIR)
                to_s = (s & ~1) | (p ^ k)
                pairs.append((f * seq + s, to_f * seq + to_s))
        return lax.ppermute(value, both, pairs)

    def per_device(tokens, frame_valid, w_qkv, w_out, w_act, class_table, cam_bias):
        frame_rows, width = tokens.shape[3], tokens.shape[4]
        own_tokens = tokens.reshape(frame_rows, width)
        f, s = lax.axis_index("fsdp"), lax.axis_index("seq")
        core, parity = s & 1, (f // PAIR) & 1
        base = (f & ~PAIR) | (core * PAIR)
        half = w_qkv.shape[2] // 2
        block = w_qkv.shape[0]

        offsets = [0, PAIR]
        for bit in gather_bits:
            offsets = offsets + [o ^ bit for o in offsets]
        by_tensor = jnp.transpose(w_qkv, (1, 0, 2))

        def part(first, count, k):
            return lax.dynamic_slice(
                by_tensor, (first, 0, (parity ^ k) * half), (count, block, half)
            )

        q0, q1 = turn(part(0, 1, 0), 0), turn(part(0, 1, 1), 1)
        kv0, kv1 = turn(part(1, 2, 0), 0), turn(part(1, 2, 1), 1)
        first = [
            jnp.concatenate([q0, q1], axis=0),
            jnp.concatenate([kv0[:1], kv1[:1]], axis=0),
            jnp.concatenate([kv0[1:], kv1[1:]], axis=0),
        ]
        slots = []
        for start in first:
            held = [start]
            for bit in gather_bits:
                held = held + [over_fsdp(v, bit) for v in held]
            slots.append(held)

        columns = base ^ jnp.array(offsets, jnp.int32)
        normed, token_mean = norm_call(columns, own_tokens)
        own = normed[None]
        pair = over_fsdp(own, PAIR)
        for bit in wide_bits:
            own = jnp.concatenate([own, over_seq(own, bit)], axis=0)
            pair = jnp.concatenate([pair, over_seq(pair, bit)], axis=0)
        rows = (own, pair, over_seq(own, 1), over_seq(pair, 1))
        frame_slots = [0]
        for bit in wide_bits + [1]:
            frame_slots = frame_slots + [o ^ bit for o in frame_slots]
        frames = s ^ jnp.array(frame_slots, jnp.int32)
        valid = frame_valid[0, 0][frames].astype(F32)
        valid = jnp.stack([valid, over_fsdp(valid, PAIR)])
        mask = jnp.repeat(valid, frame_rows, axis=1)[:, None, :]

        q, k = project_call(rows, [slots[0], slots[1]])
        mixed_own, mixed_pair = attend_call(mask, q, k, rows, slots[2])
        came = over_fsdp(mixed_pair, PAIR)
        flag = (parity ^ core).reshape(1)
        mixed, frame_mean = join_call(flag, mixed_own, came, seq)

        rows_out = w_out.shape[0] // 2
        stay = lax.dynamic_slice_in_dim(w_out, core * rows_out, rows_out, axis=0)
        leave = lax.dynamic_slice_in_dim(w_out, (1 - core) * rows_out, rows_out, axis=0)
        start = jnp.concatenate([stay, over_seq(leave, 1)], axis=0)
        up = down = after(start, slots[1][-1])
        blocks, distance = [[start]], [0]
        for t in range(1, fsdp // 2):
            up = lax.ppermute(up, "fsdp", forward)
            down = lax.ppermute(down, "fsdp", backward)
            blocks += [[up], [down]]
            distance += [-t, t]
        blocks.append(
            [
                lax.ppermute(up[:rows_out], "fsdp", forward),
                lax.ppermute(down[rows_out:], "fsdp", backward),
            ]
        )
        distance.append(fsdp // 2)
        my_place = jnp.array(place, jnp.int32)[f]
        owners = jnp.array(order, jnp.int32)[(my_place + jnp.array(distance, jnp.int32)) % fsdp]

        means = jnp.concatenate([frame_mean, token_mean.reshape(seq, -1)], axis=0)[None]
        window_slots = [0]
        for bit in [1 << i for i in range((fsdp - 1).bit_length())]:
            means = jnp.concatenate([means, over_fsdp(means, bit)], axis=0)
            window_slots = window_slots + [o ^ bit for o in window_slots]
        windows = f ^ jnp.array(window_slots, jnp.int32)
        all_tokens = means[:, seq:].reshape(fsdp, width)
        all_frames = jnp.transpose(means[:, :seq], (1, 0, 2)).reshape(seq * fsdp, -1)

        def reduce_once(keep, arrived, to):
            total = keep + arrived.astype(F32)
            count = total.shape[0] // 2
            return total[:count], total[count:].astype(to)

        pool_send, pool_keep = pool_call(all_frames, blocks, seq)
        cuts = [blocks[:5], blocks[5:]] if len(blocks) > 5 else [blocks]
        sums = []
        arrived = over_seq(pool_send, 1)
        for bit in wide_bits[::-1]:
            pool_keep, leave = reduce_once(pool_keep, arrived, F32)
            arrived = over_seq(leave, bit)
        pool_came = arrived
        for cut in cuts:
            send, keep = out_call(mixed, cut)
            arrived = over_seq(send, 1)
            for bit in wide_bits[::-1]:
                keep, leave = reduce_once(keep, arrived, BF16)
                arrived = over_seq(leave, bit)
            sums.append((keep, arrived))
        hidden = finish_call(owners, own_tokens, sums)

        camera_ids = jnp.arange(cam_bias.shape[0], dtype=jnp.int32)
        onehot = (class_table[:, None] == camera_ids[None, :]).astype(F32)
        bias = jnp.dot(onehot, cam_bias, precision=lax.Precision.HIGHEST)[None]
        logits = head_call(owners, windows, pool_keep, pool_came, all_tokens, w_act, bias)
        return hidden.reshape(tokens.shape), logits

    return per_device


def plain(tokens, frame_valid, w_qkv, w_out, w_act, class_table, cam_bias):
    windows_here, frame_rows, width = tokens.shape[0], tokens.shape[3], tokens.shape[4]
    own_rows = tokens[:, 0, 0].astype(F32)
    normed = normalize(own_rows).astype(BF16)
    gathered = lax.all_gather(normed[:, None], "seq", axis=1, tiled=True)
    frame_count = gathered.shape[1]
    span = frame_count * frame_rows
    rows = gathered.reshape(windows_here, span, width)
    full_qkv = lax.all_gather(w_qkv, "fsdp", axis=0, tiled=True)
    projected = jnp.einsum("wsd,dcn->wscn", rows, full_qkv, preferred_element_type=F32)
    heads = full_qkv.shape[2] // DH
    projected = projected.astype(BF16).reshape(windows_here, span, 3, heads, DH)
    q, k, v = projected[:, :, 0], projected[:, :, 1], projected[:, :, 2]
    key_mask = jnp.repeat(frame_valid[:, 0].astype(F32), frame_rows, axis=1)
    scores = jnp.einsum("wqhe,wkhe->whqk", q, k, preferred_element_type=F32) / math.sqrt(DH)
    weights = jnp.exp(scores) * key_mask[:, None, None, :]
    totals = jnp.sum(weights, axis=-1)
    mixed = jnp.einsum("whqk,wkhe->wqhe", weights.astype(BF16), v, preferred_element_type=F32)
    mixed = (mixed / jnp.transpose(totals, (0, 2, 1))[:, :, :, None]).astype(BF16)
    mixed = mixed.reshape(windows_here, frame_count, frame_rows, heads * DH)
    mixed = jnp.transpose(mixed, (1, 0, 2, 3)).reshape(-1, heads * DH)
    full_out = lax.all_gather(w_out, "fsdp", axis=1, tiled=True)
    branch = lax.psum_scatter(
        jnp.dot(mixed, full_out, preferred_element_type=F32), "seq", scatter_dimension=0, tiled=True
    )
    hidden = (own_rows + branch.reshape(windows_here, frame_rows, width)).astype(BF16)
    wide = lax.optimization_barrier(hidden).astype(F32)
    pooled = normalize(jnp.mean(wide, axis=1)).astype(BF16)
    camera_ids = jnp.arange(cam_bias.shape[0], dtype=jnp.int32)
    onehot = (class_table[:, None] == camera_ids[None, :]).astype(F32)
    bias = jnp.dot(onehot, cam_bias, precision=lax.Precision.HIGHEST)
    everywhere = lax.all_gather(pooled, "fsdp", axis=0, tiled=True)
    logits = jnp.dot(everywhere, w_act, preferred_element_type=F32) + bias[None, :]
    return (
        hidden.reshape(windows_here, 1, 1, frame_rows, width),
        logits.reshape(logits.shape[0], 1, 1, logits.shape[1]),
    )


def solution(mesh):
    fsdp, seq = mesh.shape["fsdp"], mesh.shape["seq"]

    def whole(tokens, frame_valid, w_qkv, w_out, w_act, class_table, cam_bias):
        args = (tokens, frame_valid, w_qkv, w_out, w_act, class_table, cam_bias)
        powers = all(n & (n - 1) == 0 for n in (fsdp, seq)) and fsdp >= 4 and seq >= 2
        aligned = w_qkv.shape[0] % (fsdp * LANES) == 0 and w_qkv.shape[2] % (seq * 2 * DH) == 0
        one_window = tokens.shape[0] == mesh.shape["groups"] * fsdp
        one_window = one_window and tokens.shape[1] == mesh.shape["sub"] and tokens.shape[2] == seq
        one = make(mesh) if powers and aligned and one_window else plain
        in_specs = (
            P(("groups", "fsdp"), "sub", "seq", None, None),
            P(("groups", "fsdp"), "sub", None),
            P("fsdp", None, "seq"),
            P("seq", "fsdp"),
            P(None, "fsdp"),
            P("fsdp"),
            P(),
        )
        out_specs = (
            P(("groups", "fsdp"), "sub", "seq", None, None),
            P("groups", "sub", "seq", "fsdp"),
        )
        run = jax.shard_map(
            one, mesh=mesh, in_specs=in_specs, out_specs=out_specs, check_vma=False
        )
        return run(*args)

    return whole
```

time: 284 us -> 148 us (0.52)
  waiting for transfers between devices: 210 us -> 56.2 us
  starting transfers between devices: 0.16 us -> 53.3 us
  blocking collectives: 30.5 us -> 0 us
  Pallas kernels: 0 us -> 17.2 us
  matrix products: 17.1 us -> 0.44 us
  between operations: 15.2 us -> 1.07 us
  local copies, waits for them, and re-layouts: 3.06 us -> 14 us
  other arithmetic: 8.18 us -> 5.23 us
    all_gather x3 -> x0, waiting for transfers between devices: 167 us -> none  [the longest x1 102 us: per_device(): full_qkv = lax.all_gather(w_qkv, 'fsdp', axis=0, tiled=True)]
    ppermute x0 -> x38, waiting for transfers between devices: none -> 56.2 us  [the longest x15 28.9 us: over_fsdp(): return lax.ppermute(value, 'fsdp', [(i, i ^ bit) for i in range(fsdp)])]
    ppermute x0 -> x38, starting transfers between devices: none -> 53.3 us  [the longest x15 25.1 us: over_fsdp(): return lax.ppermute(value, 'fsdp', [(i, i ^ bit) for i in range(fsdp)])]
    reduce_scatter x1 -> x0, waiting for transfers between devices: 42.4 us -> none  [per_device(): lax.psum_scatter(jnp.dot(frame_major, full_out, preferred_element_type=jn...]
    all_gather x1 -> x0, blocking collectives: 30.5 us -> none  [per_device(): lax.all_gather(pooled, 'fsdp', axis=0, tiled=True)]
    pallas_call x0 -> x9, Pallas kernels: none -> 17.2 us  [the longest x1 4.5 us: attend_call(): pl.pallas_call(functools.partial(attend_kernel, len(v_slots)), out_shape=...]
    dot_general x6 -> x1, matrix products: 17.1 us -> 0.44 us  [per_device(): bias = jnp.dot(onehot, cam_bias, precision=lax.Precision.HIGHEST)[None]]
    convert_element_type x4 -> x1, other arithmetic: 4.35 us -> 0.51 us  [per_device(): valid = frame_valid[0, 0][frames].astype(F32)]
  transfers between devices with their start and end apart: 4 -> 38, of which waited for: 4 -> 15; matrix products, arithmetic and copies ran while one was open for 4% -> 10% of each run, Pallas kernels for 0% -> 10%
where the time goes in v2:
time: 148 us; the launch traced here: 147 us
  waiting for transfers between devices  56.2 us (38%)
  starting transfers between devices  53.3 us (36%)
  Pallas kernels  17.2 us (12%)
  local copies, waits for them, and re-layouts  14 us (9%)
  other arithmetic  5.23 us (4%)
    ppermute x15, waiting for transfers between devices, over_fsdp(): return lax.ppermute(value, 'fsdp', [(i, i ^ bit) for i in range(fsdp)])  28.9 us
    ppermute x15, starting transfers between devices, over_fsdp(): return lax.ppermute(value, 'fsdp', [(i, i ^ bit) for i in range(fsdp)])  25.1 us
    ppermute x11, waiting for transfers between devices, over_seq(): return lax.ppermute(value, 'seq', [(i, i ^ bit) for i in range(seq)])  18.3 us
    ppermute x4, starting transfers between devices, turn(): return lax.ppermute(value, both, pairs)  11.2 us
    ppermute x11, starting transfers between devices, over_seq(): return lax.ppermute(value, 'seq', [(i, i ^ bit) for i in range(seq)])  7.58 us
    unnamed x34, local copies, waits for them, and re-layouts  6.44 us
    ppermute x4, waiting for transfers between devices, turn(): return lax.ppermute(value, both, pairs)  4.7 us
    pallas_call x1, Pallas kernels, attend_call(): pl.pallas_call(functools.partial(attend_kernel, len(v_slots)), out_shape=...  4.5 us
  transfers between devices with their start and end apart: 38, of which 15 were waited for; matrix products, arithmetic and copies ran while one was open for 10% of the time, Pallas kernels for 10%

profile of v2, /device:TPU:0, one launch (start us, length us, event | category | flops | bytes accessed | tf_op | source)
XLA Modules:
  0.0 147.5 jit_solution(3380136779687322287)
XLA Ops:
  3.4 3.1 %collective-permute-start.2 = (bf16[1,128,2048]{2,1,0:T(8,128)(2,1)S(1)}, bf16[1,128,2048]{2,1,0:T(8,128)(2,1)}, u32[]{:S(2)}, u32[]{:S(2)}) collective-permute-start(bf16[1,128,2048]{2,1,0:T(8,128)(2,1)S(1)} %bitcast.34), channel_id=1, source_target_pairs={{0,8},{4,12},{8,0},{12,4},{16,24},{20,28},{24,16},{28,20},{1,9},{5... | collective-permute-start | bytes 1572872 | tf_op jit(solution)/shard_map/ppermute | solution.py:334
  11.4 3.6 %collective-permute-start.7 = (bf16[1,256,256]{2,1,0:T(8,128)(2,1)S(1)}, bf16[1,256,256]{2,1,0:T(8,128)(2,1)S(1)}, u32[]{:S(2)}, u32[]{:S(2)}) collective-permute-start(bf16[1,256,256]{2,1,0:T(8,128)(2,1)S(1)} %get-tuple-element.34), channel_id=1, source_target_pairs={{0,1},{1,9},{2,3},{3,11},{4,5},{5,13},{6,7},{7,15},{8,0},{9,8},{10... | collective-permute-start | bytes 393224 | tf_op jit(solution)/shard_map/ppermute | solution.py:347
  16.1 6.3 %collective-permute-start.12 = (bf16[2,256,256]{2,1,0:T(8,128)(2,1)S(1)}, bf16[2,256,256]{2,1,0:T(8,128)(2,1)S(1)}, u32[]{:S(2)}, u32[]{:S(2)}) collective-permute-start(bf16[2,256,256]{2,1,0:T(8,128)(2,1)S(1)} %get-tuple-element.33), channel_id=1, source_target_pairs={{0,1},{1,9},{2,3},{3,11},{4,5},{5,13},{6,7},{7,15},{8,0},{9,8},{10... | collective-permute-start | bytes 786440 | tf_op jit(solution)/shard_map/ppermute | solution.py:347
  24.7 2.8 %collective-permute-start.8 = (bf16[2,256,256]{2,1,0:T(8,128)(2,1)}, bf16[2,256,256]{2,1,0:T(8,128)(2,1)S(1)}, u32[]{:S(2)}, u32[]{:S(2)}) collective-permute-start(bf16[2,256,256]{2,1,0:T(8,128)(2,1)} %constant_dynamic-update-slice_fusion.2.refs_4_), channel_id=1, source_target_pairs={{0,16},{4,20},{8,24},{12,28},{16,0},{20,4},{24,8},{28,12},{1,17},{... | collective-permute-start | bytes 786440 | tf_op jit(solution)/shard_map/ppermute | solution.py:334
  27.4 3.8 %collective-permute-done.12 = bf16[2,256,256]{2,1,0:T(8,128)(2,1)S(1)} collective-permute-done((bf16[2,256,256]{2,1,0:T(8,128)(2,1)S(1)}, bf16[2,256,256]{2,1,0:T(8,128)(2,1)S(1)}, u32[]{:S(2)}, u32[]{:S(2)}) %collective-permute-start.12) | collective-permute-done | bytes 262176 | tf_op jit(solution)/shard_map/ppermute | solution.py:347
  36.7 4.5 %collective-permute-done.3 = bf16[1,128,2048]{2,1,0:T(8,128)(2,1)S(1)} collective-permute-done((bf16[1,128,2048]{2,1,0:T(8,128)(2,1)}, bf16[1,128,2048]{2,1,0:T(8,128)(2,1)S(1)}, u32[]{:S(2)}, u32[]{:S(2)}) %collective-permute-start.3) | collective-permute-done | bytes 524320 | tf_op jit(solution)/shard_map/ppermute | solution.py:337
  43.9 6.4 %collective-permute-done.13.refs_9_ = bf16[2,256,256]{2,1,0:T(8,128)(2,1)} collective-permute-done((bf16[2,256,256]{2,1,0:T(8,128)(2,1)}, bf16[2,256,256]{2,1,0:T(8,128)(2,1)}, u32[]{:S(2)}, u32[]{:S(2)}) %collective-permute-start.13) | collective-permute-done | bytes 262176 | tf_op jit(solution)/shard_map/ppermute | solution.py:334
  57.4 6.3 %collective-permute-done.9.refs_6_ = bf16[2,256,256]{2,1,0:T(8,128)(2,1)S(1)} collective-permute-done((bf16[2,256,256]{2,1,0:T(8,128)(2,1)}, bf16[2,256,256]{2,1,0:T(8,128)(2,1)S(1)}, u32[]{:S(2)}, u32[]{:S(2)}) %collective-permute-start.9) | collective-permute-done | bytes 262176 | tf_op jit(solution)/shard_map/ppermute | solution.py:334
  65.1 4.2 %collective-permute-done.14.refs_10_ = bf16[2,256,256]{2,1,0:T(8,128)(2,1)S(1)} collective-permute-done((bf16[2,256,256]{2,1,0:T(8,128)(2,1)}, bf16[2,256,256]{2,1,0:T(8,128)(2,1)S(1)}, u32[]{:S(2)}, u32[]{:S(2)}) %collective-permute-start.14) | collective-permute-done | bytes 262176 | tf_op jit(solution)/shard_map/ppermute | solution.py:334
  69.3 2.3 %collective-permute-start.21 = (bf16[512,256]{1,0:T(8,128)(2,1)S(1)}, bf16[512,256]{1,0:T(8,128)(2,1)}, u32[]{:S(2)}, u32[]{:S(2)}) collective-permute-start(bf16[512,256]{1,0:T(8,128)(2,1)S(1)} %pad_maximum_fusion.3.refs_0_), channel_id=1, source_target_pairs={{0,8},{8,16},{16,24},{24,28},{28,20},{20,12},{12,4},{4,0},{1,9},{9... | collective-permute-start | bytes 786440 | tf_op jit(solution)/shard_map/ppermute | solution.py:411
  72.3 2.6 %collective-permute-done.10.refs_7_ = bf16[2,256,256]{2,1,0:T(8,128)(2,1)S(1)} collective-permute-done((bf16[2,256,256]{2,1,0:T(8,128)(2,1)}, bf16[2,256,256]{2,1,0:T(8,128)(2,1)S(1)}, u32[]{:S(2)}, u32[]{:S(2)}) %collective-permute-start.10) | collective-permute-done | bytes 262176 | tf_op jit(solution)/shard_map/ppermute | solution.py:334
  76.4 4.3 %collective-permute-done.21.refs_1_ = bf16[512,256]{1,0:T(8,128)(2,1)} collective-permute-done((bf16[512,256]{1,0:T(8,128)(2,1)S(1)}, bf16[512,256]{1,0:T(8,128)(2,1)}, u32[]{:S(2)}, u32[]{:S(2)}) %collective-permute-start.21) | collective-permute-done | bytes 262176 | tf_op jit(solution)/shard_map/ppermute | solution.py:411
  81.4 2.1 %collective-permute-start.24 = (bf16[512,256]{1,0:T(8,128)(2,1)}, bf16[512,256]{1,0:T(8,128)(2,1)}, u32[]{:S(2)}, u32[]{:S(2)}) collective-permute-start(bf16[512,256]{1,0:T(8,128)(2,1)} %collective-permute-done.22.refs_2_), channel_id=1, source_target_pairs={{8,0},{16,8},{24,16},{28,24},{20,28},{12,20},{4,12},{0,4},{9,1},{1... | collective-permute-start | bytes 786440 | tf_op jit(solution)/shard_map/ppermute | solution.py:412
  84.5 3.8 %project.1 = (bf16[2,512,256]{2,1,0:T(8,128)(2,1)S(1)}, bf16[2,512,256]{2,1,0:T(8,128)(2,1)S(1)}) custom-call(bf16[2,128,2048]{2,1,0:T(8,128)(2,1)S(1)} %pad_maximum_fusion.refs_0_, bf16[2,128,2048]{2,1,0:T(8,128)(2,1)S(1)} %constant_dynamic-update-slice_fusion.refs_1_, bf16[2,128,2048]{2,1,0:T(8,128)(2,1)S(1)} %collective-permute-done.4.refs_2_, ...), custom_call_target="tpu_custom_call" | custom-call | flops 2147483648 | bytes 4194304 | tf_op jit(solution)/shard_map/project/pallas_call | solution.py:102
  88.3 3.5 %collective-permute-done.18.refs_7_ = bf16[2,256,256]{2,1,0:T(8,128)(2,1)S(1)} collective-permute-done((bf16[2,256,256]{2,1,0:T(8,128)(2,1)S(1)}, bf16[2,256,256]{2,1,0:T(8,128)(2,1)S(1)}, u32[]{:S(2)}, u32[]{:S(2)}) %collective-permute-start.18) | collective-permute-done | bytes 262176 | tf_op jit(solution)/shard_map/ppermute | solution.py:334
  91.9 4.5 %attend.1 = (bf16[512,256]{1,0:T(8,128)(2,1)S(1)}, bf16[512,256]{1,0:T(8,128)(2,1)}) custom-call(f32[2,1,512]{2,1,0:T(1,128)S(1)} %bitcast.39, bf16[2,512,256]{2,1,0:T(8,128)(2,1)S(1)} %get-tuple-element.18.q_ref, bf16[2,512,256]{2,1,0:T(8,128)(2,1)S(1)} %get-tuple-element.19.k_ref, bf16[2,128,2048]{2,1,0:T(8,128)(2,1)S(1)} %pad_maximum_fusion.refs_0_, ...), custom_call_target="tpu_custom_call" | custom-call | flops 1610612736 | bytes 4194304 | tf_op jit(solution)/shard_map/attend/pallas_call | solution.py:139
  100.9 3.2 %collective-permute-done.19.came_ref = bf16[512,256]{1,0:T(8,128)(2,1)S(1)} collective-permute-done((bf16[512,256]{1,0:T(8,128)(2,1)}, bf16[512,256]{1,0:T(8,128)(2,1)S(1)}, u32[]{:S(2)}, u32[]{:S(2)}) %collective-permute-start.19) | collective-permute-done | bytes 262176 | tf_op jit(solution)/shard_map/ppermute | solution.py:334
  105.3 3.9 %collective-permute-start.33 = (f32[1,8,512]{2,1,0:T(8,128)S(1)}, f32[1,8,512]{2,1,0:T(8,128)S(1)}, u32[]{:S(2)}, u32[]{:S(2)}) collective-permute-start(f32[1,8,512]{2,1,0:T(8,128)S(1)} %maximum_bitcast_fusion), channel_id=1, source_target_pairs={{0,4},{4,0},{8,12},{12,8},{16,20},{20,16},{24,28},{28,24},{1,5},{5... | collective-permute-start | bytes 49160 | tf_op jit(solution)/shard_map/ppermute | solution.py:334
  110.0 2.2 %collective-permute-start.30 = (bf16[256,256]{1,0:T(8,128)(2,1)S(1)}, bf16[256,256]{1,0:T(8,128)(2,1)S(1)}, u32[]{:S(2)}, u32[]{:S(2)}) collective-permute-start(bf16[256,256]{1,0:T(8,128)(2,1)S(1)} %slice.69), channel_id=1, source_target_pairs={{8,0},{16,8},{24,16},{28,24},{20,28},{12,20},{4,12},{0,4},{9,1},{1... | collective-permute-start | bytes 393224 | tf_op jit(solution)/shard_map/ppermute | solution.py:418
  112.2 2.3 %collective-permute-start.34 = (f32[2,8,512]{2,1,0:T(8,128)S(1)}, f32[2,8,512]{2,1,0:T(8,128)S(1)}, u32[]{:S(2)}, u32[]{:S(2)}) collective-permute-start(f32[2,8,512]{2,1,0:T(8,128)S(1)} %pad_maximum_fusion.6), channel_id=1, source_target_pairs={{0,8},{4,12},{8,0},{12,4},{16,24},{20,28},{24,16},{28,20},{1,9},{5... | collective-permute-start | bytes 98312 | tf_op jit(solution)/shard_map/ppermute | solution.py:334
  115.1 2.6 %collective-permute-done.34 = f32[2,8,512]{2,1,0:T(8,128)S(1)} collective-permute-done((f32[2,8,512]{2,1,0:T(8,128)S(1)}, f32[2,8,512]{2,1,0:T(8,128)S(1)}, u32[]{:S(2)}, u32[]{:S(2)}) %collective-permute-start.34) | collective-permute-done | bytes 32800 | tf_op jit(solution)/shard_map/ppermute | solution.py:334
  117.7 3.2 %collective-permute-start.35 = (f32[4,8,512]{2,1,0:T(8,128)S(1)}, f32[4,8,512]{2,1,0:T(8,128)S(1)}, u32[]{:S(2)}, u32[]{:S(2)}) collective-permute-start(f32[4,8,512]{2,1,0:T(8,128)S(1)} %pad_maximum_fusion.5), channel_id=1, source_target_pairs={{0,16},{4,20},{8,24},{12,28},{16,0},{20,4},{24,8},{28,12},{1,17},{... | collective-permute-start | bytes 196616 | tf_op jit(solution)/shard_map/ppermute | solution.py:334
  121.6 2.0 %out.2 = (bf16[256,1280]{1,0:T(8,128)(2,1)S(1)}, f32[256,1280]{1,0:T(8,128)S(1)}) custom-call(bf16[512,512]{1,0:T(8,128)(2,1)S(1)} %get-tuple-element.22.mixed_ref, bf16[512,256]{1,0:T(8,128)(2,1)S(1)} %pad_maximum_fusion.3.refs_0_, bf16[512,256]{1,0:T(8,128)(2,1)} %collective-permute-done.21.refs_1_, bf16[512,256]{1,0:T(8,128)(2,1)} %collective-permute-done.22.refs_2_, ...), custom_call_target="tpu_custom_call" | custom-call | flops 671088640 | bytes 5242880 | tf_op jit(solution)/shard_map/out/pallas_call | solution.py:214
  131.3 11.5 %collective-permute-done.37.came_ref = f32[8,2048]{1,0:T(8,128)S(1)} collective-permute-done((f32[8,2048]{1,0:T(8,128)S(1)}, f32[8,2048]{1,0:T(8,128)S(1)}, u32[]{:S(2)}, u32[]{:S(2)}) %collective-permute-start.37) | collective-permute-done | bytes 65568 | tf_op jit(solution)/shard_map/ppermute | solution.py:337
  (137 shorter events, 51.5 us)
Async XLA Ops:
  3.4 28.5 %collective-permute-start.2 = (bf16[1,128,2048]{2,1,0:T(8,128)(2,1)S(1)}, bf16[1,128,2048]{2,1,0:T(8,128)(2,1)}, u32[]{:S(2)}, u32[]{:S(2)}) collective-permute-start(bf16[1,128,2048]{2,1,0:T(8,128)(2,1)S(1)} %bitcast.34), channel_id=1, source_target_pairs={{0,8},{4,12},{8,0},{12,4},{16,24},{20,28},{24,16},{28,20},{1,9},{5... | collective-permute-start | bytes 1572872 | tf_op jit(solution)/shard_map/ppermute | solution.py:334
  6.5 29.0 %collective-permute-start.1 = (bf16[1,128,2048]{2,1,0:T(8,128)(2,1)S(1)}, bf16[1,128,2048]{2,1,0:T(8,128)(2,1)S(1)}, u32[]{:S(2)}, u32[]{:S(2)}) collective-permute-start(bf16[1,128,2048]{2,1,0:T(8,128)(2,1)S(1)} %bitcast.35), channel_id=1, source_target_pairs={{0,2},{1,3},{2,0},{3,1},{4,6},{5,7},{6,4},{7,5},{8,10},{9,11},{10,... | collective-permute-start | bytes 1572872 | tf_op jit(solution)/shard_map/ppermute | solution.py:337
  9.0 18.4 %collective-permute-start.11 = (bf16[2,256,256]{2,1,0:T(8,128)(2,1)S(1)}, bf16[2,256,256]{2,1,0:T(8,128)(2,1)S(1)}, u32[]{:S(2)}, u32[]{:S(2)}) collective-permute-start(bf16[2,256,256]{2,1,0:T(8,128)(2,1)S(1)} %get-tuple-element.32), channel_id=1, source_target_pairs={{0,0},{1,8},{2,2},{3,10},{4,4},{5,12},{6,6},{7,14},{8,1},{9,9},{10... | collective-permute-start | bytes 786440 | tf_op jit(solution)/shard_map/ppermute | solution.py:347
  11.4 12.6 %collective-permute-start.7 = (bf16[1,256,256]{2,1,0:T(8,128)(2,1)S(1)}, bf16[1,256,256]{2,1,0:T(8,128)(2,1)S(1)}, u32[]{:S(2)}, u32[]{:S(2)}) collective-permute-start(bf16[1,256,256]{2,1,0:T(8,128)(2,1)S(1)} %get-tuple-element.34), channel_id=1, source_target_pairs={{0,1},{1,9},{2,3},{3,11},{4,5},{5,13},{6,7},{7,15},{8,0},{9,8},{10... | collective-permute-start | bytes 393224 | tf_op jit(solution)/shard_map/ppermute | solution.py:347
  16.1 15.1 %collective-permute-start.12 = (bf16[2,256,256]{2,1,0:T(8,128)(2,1)S(1)}, bf16[2,256,256]{2,1,0:T(8,128)(2,1)S(1)}, u32[]{:S(2)}, u32[]{:S(2)}) collective-permute-start(bf16[2,256,256]{2,1,0:T(8,128)(2,1)S(1)} %get-tuple-element.33), channel_id=1, source_target_pairs={{0,1},{1,9},{2,3},{3,11},{4,5},{5,13},{6,7},{7,15},{8,0},{9,8},{10... | collective-permute-start | bytes 786440 | tf_op jit(solution)/shard_map/ppermute | solution.py:347
  24.7 30.2 %collective-permute-start.8 = (bf16[2,256,256]{2,1,0:T(8,128)(2,1)}, bf16[2,256,256]{2,1,0:T(8,128)(2,1)S(1)}, u32[]{:S(2)}, u32[]{:S(2)}) collective-permute-start(bf16[2,256,256]{2,1,0:T(8,128)(2,1)} %constant_dynamic-update-slice_fusion.2.refs_4_), channel_id=1, source_target_pairs={{0,16},{4,20},{8,24},{12,28},{16,0},{20,4},{24,8},{28,12},{1,17},{... | collective-permute-start | bytes 786440 | tf_op jit(solution)/shard_map/ppermute | solution.py:334
  34.1 16.2 %collective-permute-start.13 = (bf16[2,256,256]{2,1,0:T(8,128)(2,1)}, bf16[2,256,256]{2,1,0:T(8,128)(2,1)}, u32[]{:S(2)}, u32[]{:S(2)}) collective-permute-start(bf16[2,256,256]{2,1,0:T(8,128)(2,1)} %pad_maximum_fusion.1.refs_8_), channel_id=1, source_target_pairs={{0,16},{4,20},{8,24},{12,28},{16,0},{20,4},{24,8},{28,12},{1,17},{... | collective-permute-start | bytes 786440 | tf_op jit(solution)/shard_map/ppermute | solution.py:334
  35.6 45.8 %collective-permute-start.4 = (bf16[2,128,2048]{2,1,0:T(8,128)(2,1)S(1)}, bf16[2,128,2048]{2,1,0:T(8,128)(2,1)S(1)}, u32[]{:S(2)}, u32[]{:S(2)}) collective-permute-start(bf16[2,128,2048]{2,1,0:T(8,128)(2,1)S(1)} %pad_maximum_fusion.refs_0_), channel_id=1, source_target_pairs={{0,1},{1,0},{2,3},{3,2},{4,5},{5,4},{6,7},{7,6},{8,9},{9,8},{10,11... | collective-permute-start | bytes 3145736 | tf_op jit(solution)/shard_map/ppermute | solution.py:337
  41.3 42.2 %collective-permute-start.5 = (bf16[2,128,2048]{2,1,0:T(8,128)(2,1)S(1)}, bf16[2,128,2048]{2,1,0:T(8,128)(2,1)}, u32[]{:S(2)}, u32[]{:S(2)}) collective-permute-start(bf16[2,128,2048]{2,1,0:T(8,128)(2,1)S(1)} %constant_dynamic-update-slice_fusion.refs_1_), channel_id=1, source_target_pairs={{0,1},{1,0},{2,3},{3,2},{4,5},{5,4},{6,7},{7,6},{8,9},{9,8},{10,11... | collective-permute-start | bytes 3145736 | tf_op jit(solution)/shard_map/ppermute | solution.py:337
  41.9 11.0 %collective-permute-start = (f32[4]{0:T(128)}, f32[4]{0:T(128)}, u32[]{:S(2)}, u32[]{:S(2)}) collective-permute-start(f32[4]{0:T(128)} %get-tuple-element.47), channel_id=1, source_target_pairs={{0,8},{4,12},{8,0},{12,4},{16,24},{20,28},{24,16},{28,20},{1,9},{5... | collective-permute-start | bytes 56 | tf_op jit(solution)/shard_map/ppermute | solution.py:334
  54.8 14.5 %collective-permute-start.14 = (bf16[2,256,256]{2,1,0:T(8,128)(2,1)}, bf16[2,256,256]{2,1,0:T(8,128)(2,1)S(1)}, u32[]{:S(2)}, u32[]{:S(2)}) collective-permute-start(bf16[2,256,256]{2,1,0:T(8,128)(2,1)} %pad_maximum_fusion.1.refs_8_), channel_id=1, source_target_pairs={{0,4},{4,0},{8,12},{12,8},{16,20},{20,16},{24,28},{28,24},{1,5},{5... | collective-permute-start | bytes 786440 | tf_op jit(solution)/shard_map/ppermute | solution.py:334
  57.3 14.4 %collective-permute-start.16 = (bf16[2,256,256]{2,1,0:T(8,128)(2,1)S(1)}, bf16[2,256,256]{2,1,0:T(8,128)(2,1)S(1)}, u32[]{:S(2)}, u32[]{:S(2)}) collective-permute-start(bf16[2,256,256]{2,1,0:T(8,128)(2,1)S(1)} %pad_maximum_fusion.2.refs_4_), channel_id=1, source_target_pairs={{0,16},{4,20},{8,24},{12,28},{16,0},{20,4},{24,8},{28,12},{1,17},{... | collective-permute-start | bytes 786440 | tf_op jit(solution)/shard_map/ppermute | solution.py:334
  63.7 11.2 %collective-permute-start.10 = (bf16[2,256,256]{2,1,0:T(8,128)(2,1)}, bf16[2,256,256]{2,1,0:T(8,128)(2,1)S(1)}, u32[]{:S(2)}, u32[]{:S(2)}) collective-permute-start(bf16[2,256,256]{2,1,0:T(8,128)(2,1)} %copy-done.6), channel_id=1, source_target_pairs={{0,4},{4,0},{8,12},{12,8},{16,20},{20,16},{24,28},{28,24},{1,5},{5... | collective-permute-start | bytes 786440 | tf_op jit(solution)/shard_map/ppermute | solution.py:334
  69.3 11.3 %collective-permute-start.21 = (bf16[512,256]{1,0:T(8,128)(2,1)S(1)}, bf16[512,256]{1,0:T(8,128)(2,1)}, u32[]{:S(2)}, u32[]{:S(2)}) collective-permute-start(bf16[512,256]{1,0:T(8,128)(2,1)S(1)} %pad_maximum_fusion.3.refs_0_), channel_id=1, source_target_pairs={{0,8},{8,16},{16,24},{24,28},{28,20},{20,12},{12,4},{4,0},{1,9},{9... | collective-permute-start | bytes 786440 | tf_op jit(solution)/shard_map/ppermute | solution.py:411
  74.9 13.4 %collective-permute-start.17 = (bf16[2,256,256]{2,1,0:T(8,128)(2,1)S(1)}, bf16[2,256,256]{2,1,0:T(8,128)(2,1)S(1)}, u32[]{:S(2)}, u32[]{:S(2)}) collective-permute-start(bf16[2,256,256]{2,1,0:T(8,128)(2,1)S(1)} %pad_maximum_fusion.2.refs_4_), channel_id=1, source_target_pairs={{0,4},{4,0},{8,12},{12,8},{16,20},{20,16},{24,28},{28,24},{1,5},{5... | collective-permute-start | bytes 786440 | tf_op jit(solution)/shard_map/ppermute | solution.py:334
  80.7 11.1 %collective-permute-start.18 = (bf16[2,256,256]{2,1,0:T(8,128)(2,1)S(1)}, bf16[2,256,256]{2,1,0:T(8,128)(2,1)S(1)}, u32[]{:S(2)}, u32[]{:S(2)}) collective-permute-start(bf16[2,256,256]{2,1,0:T(8,128)(2,1)S(1)} %collective-permute-done.16.refs_5_), channel_id=1, source_target_pairs={{0,4},{4,0},{8,12},{12,8},{16,20},{20,16},{24,28},{28,24},{1,5},{5... | collective-permute-start | bytes 786440 | tf_op jit(solution)/shard_map/ppermute | solution.py:334
  81.4 17.5 %collective-permute-start.23 = (bf16[512,256]{1,0:T(8,128)(2,1)}, bf16[512,256]{1,0:T(8,128)(2,1)}, u32[]{:S(2)}, u32[]{:S(2)}) collective-permute-start(bf16[512,256]{1,0:T(8,128)(2,1)} %collective-permute-done.21.refs_1_), channel_id=1, source_target_pairs={{0,8},{8,16},{16,24},{24,28},{28,20},{20,12},{12,4},{4,0},{1,9},{9... | collective-permute-start | bytes 786440 | tf_op jit(solution)/shard_map/ppermute | solution.py:411
  81.4 19.5 %collective-permute-start.24 = (bf16[512,256]{1,0:T(8,128)(2,1)}, bf16[512,256]{1,0:T(8,128)(2,1)}, u32[]{:S(2)}, u32[]{:S(2)}) collective-permute-start(bf16[512,256]{1,0:T(8,128)(2,1)} %collective-permute-done.22.refs_2_), channel_id=1, source_target_pairs={{8,0},{16,8},{24,16},{28,24},{20,28},{12,20},{4,12},{0,4},{9,1},{1... | collective-permute-start | bytes 786440 | tf_op jit(solution)/shard_map/ppermute | solution.py:412
  98.9 10.9 %collective-permute-start.27 = (bf16[512,256]{1,0:T(8,128)(2,1)}, bf16[512,256]{1,0:T(8,128)(2,1)S(1)}, u32[]{:S(2)}, u32[]{:S(2)}) collective-permute-start(bf16[512,256]{1,0:T(8,128)(2,1)} %collective-permute-done.23.refs_3_), channel_id=1, source_target_pairs={{0,8},{8,16},{16,24},{24,28},{28,20},{20,12},{12,4},{4,0},{1,9},{9... | collective-permute-start | bytes 786440 | tf_op jit(solution)/shard_map/ppermute | solution.py:411
  109.8 11.1 %collective-permute-start.29 = (bf16[256,256]{1,0:T(8,128)(2,1)S(1)}, bf16[256,256]{1,0:T(8,128)(2,1)S(1)}, u32[]{:S(2)}, u32[]{:S(2)}) collective-permute-start(bf16[256,256]{1,0:T(8,128)(2,1)S(1)} %slice.68), channel_id=1, source_target_pairs={{0,8},{8,16},{16,24},{24,28},{28,20},{20,12},{12,4},{4,0},{1,9},{9... | collective-permute-start | bytes 393224 | tf_op jit(solution)/shard_map/ppermute | solution.py:417
  110.0 10.9 %collective-permute-start.30 = (bf16[256,256]{1,0:T(8,128)(2,1)S(1)}, bf16[256,256]{1,0:T(8,128)(2,1)S(1)}, u32[]{:S(2)}, u32[]{:S(2)}) collective-permute-start(bf16[256,256]{1,0:T(8,128)(2,1)S(1)} %slice.69), channel_id=1, source_target_pairs={{8,0},{16,8},{24,16},{28,24},{20,28},{12,20},{4,12},{0,4},{9,1},{1... | collective-permute-start | bytes 393224 | tf_op jit(solution)/shard_map/ppermute | solution.py:418
  127.4 17.5 %collective-permute-start.32 = (bf16[128,768]{1,0:T(8,128)(2,1)S(1)}, bf16[128,768]{1,0:T(8,128)(2,1)S(1)}, u32[]{:S(2)}, u32[]{:S(2)}) collective-permute-start(bf16[128,768]{1,0:T(8,128)(2,1)S(1)} %slice.81), channel_id=1, source_target_pairs={{0,2},{1,3},{2,0},{3,1},{4,6},{5,7},{6,4},{7,5},{8,10},{9,11},{10,... | collective-permute-start | bytes 589832 | tf_op jit(solution)/shard_map/ppermute | solution.py:337
  129.1 15.8 %collective-permute-start.26 = (bf16[128,1280]{1,0:T(8,128)(2,1)S(1)}, bf16[128,1280]{1,0:T(8,128)(2,1)S(1)}, u32[]{:S(2)}, u32[]{:S(2)}) collective-permute-start(bf16[128,1280]{1,0:T(8,128)(2,1)S(1)} %slice.80), channel_id=1, source_target_pairs={{0,2},{1,3},{2,0},{3,1},{4,6},{5,7},{6,4},{7,5},{8,10},{9,11},{10,... | collective-permute-start | bytes 983048 | tf_op jit(solution)/shard_map/ppermute | solution.py:337
  129.8 13.1 %collective-permute-start.37 = (f32[8,2048]{1,0:T(8,128)S(1)}, f32[8,2048]{1,0:T(8,128)S(1)}, u32[]{:S(2)}, u32[]{:S(2)}) collective-permute-start(f32[8,2048]{1,0:T(8,128)S(1)} %get-tuple-element.44), channel_id=1, source_target_pairs={{0,2},{1,3},{2,0},{3,1},{4,6},{5,7},{6,4},{7,5},{8,10},{9,11},{10,... | collective-permute-start | bytes 196616 | tf_op jit(solution)/shard_map/ppermute | solution.py:337
  (29 other events, 313.6 us)

commit v3 on v2

v3 whole, which is shorter than its diff:
```python
import functools
import math

import jax
import jax.numpy as jnp
from jax import lax
from jax.experimental import pallas as pl
from jax.experimental.pallas import tpu as pltpu
from jax.sharding import PartitionSpec as P

DH = 128
LANES = 128
F32 = jnp.float32
BF16 = jnp.bfloat16
VMEM = pl.BlockSpec(memory_space=pltpu.VMEM)
SMEM = pl.BlockSpec(memory_space=pltpu.SMEM)
PARAMS = pltpu.CompilerParams(vmem_limit_bytes=16 * 2**20)


def normalize(values):
    centre = jnp.mean(values, axis=-1, keepdims=True)
    spread = jnp.mean(jnp.square(values - centre), axis=-1, keepdims=True)
    return (values - centre) * lax.rsqrt(spread + 1e-05)


def after(value, *done):
    return lax.optimization_barrier((value, *done))[0]


def cost(flops, size):
    return pl.CostEstimate(flops=flops, bytes_accessed=size, transcendentals=0)


def ring_place(index, n):
    return index // 2 if index % 2 == 0 else n - 1 - index // 2


def owners(distances):
    n = len(distances)
    me = lax.axis_index("fsdp")
    half = lax.shift_right_logical(me, 1)
    place = jnp.where((me & 1) == 0, half, n - 1 - half)
    found = []
    for distance in distances:
        at = lax.rem(place + (distance + n), n)
        found.append(jnp.where(at < n // 2, 2 * at, 2 * (n - at) - 1))
    return found


def norm_kernel(distances, tokens_ref, normed_ref, mean_ref):
    values = tokens_ref[...].astype(F32)
    width = values.shape[1]
    centre = jnp.mean(values, axis=1, keepdims=True)
    spread = jnp.mean(jnp.square(values - centre), axis=1, keepdims=True)
    scale = lax.rsqrt(spread + 1e-05)
    mean = jnp.mean(values, axis=0, keepdims=True)
    columns = mean_ref.shape[1]
    for i in range(mean_ref.shape[0]):
        mean_ref[i : i + 1, :] = mean[:, i * columns : (i + 1) * columns]
    block = width // len(distances)
    for i, owner in enumerate(owners(distances)):
        at = pl.multiple_of(owner * block, LANES)
        piece = tokens_ref[:, pl.ds(at, block)].astype(F32)
        normed_ref[:, i * block : (i + 1) * block] = ((piece - centre) * scale).astype(BF16)


def norm_call(distances, tokens, columns):
    rows, width = tokens.shape
    return pl.pallas_call(
        functools.partial(norm_kernel, distances),
        out_shape=(
            jax.ShapeDtypeStruct((rows, width), BF16),
            jax.ShapeDtypeStruct((width // columns, columns), F32),
        ),
        in_specs=[VMEM],
        out_specs=(VMEM, VMEM),
        compiler_params=PARAMS,
        cost_estimate=cost(8 * rows * width, 4 * rows * width),
        name="norm",
    )(tokens)


def fetch(sources, buffers, sems):
    copies = [
        pltpu.make_async_copy(source, buffer, sems.at[i])
        for i, (source, buffer) in enumerate(zip(sources, buffers))
    ]
    for copy in copies:
        copy.start()

    def get(i):
        copies[i].wait()
        return buffers[i][...]

    return get


def frames_of(refs):
    return [(ref, frame) for ref in refs for frame in range(ref.shape[0])]


def times_rows(sources, first, blocks, total):
    at = first
    for block in blocks:
        depth = block.shape[0]
        rows = [ref[frame, :, at : at + depth] for ref, frame in frames_of(sources)]
        term = jnp.dot(jnp.concatenate(rows, axis=0), block, preferred_element_type=F32)
        total = term if total is None else total + term
        at += depth
    return total


def early_kernel(tensors, own_ref, core_ref, *refs):
    count = (len(refs) - 2) // 2
    sources, out_ref = refs[:count], refs[count]
    buffers, sems = refs[count + 1 : -1], refs[-1]
    get = fetch(sources, buffers, sems)
    for tensor in range(tensors):
        blocks = [get(i) for i in range(tensor, count, tensors)]
        out_ref[tensor] = times_rows((own_ref, core_ref), 0, blocks, None)


ANY = pl.BlockSpec(memory_space=pltpu.HBM)


def scratch_for(blocks):
    return [pltpu.VMEM(b.shape, b.dtype) for b in blocks] + [pltpu.SemaphoreType.DMA((len(blocks),))]


def early_call(tokens, blocks, tensors):
    rows = 2 * tokens[0].shape[0] * tokens[0].shape[1]
    columns = blocks[0].shape[1]
    depth = sum(b.shape[0] for b in blocks)
    return pl.pallas_call(
        functools.partial(early_kernel, tensors),
        out_shape=jax.ShapeDtypeStruct((tensors, rows, columns), F32),
        in_specs=[VMEM] * 2 + [ANY] * len(blocks),
        out_specs=VMEM,
        scratch_shapes=scratch_for(blocks),
        compiler_params=PARAMS,
        cost_estimate=cost(2 * rows * columns * depth, 2 * columns * depth),
        name="early",
    )(*tokens, *blocks)


def late_kernel(counts, first, own_ref, core_ref, part_ref, *refs):
    count = sum(counts)
    sources, outs = refs[:count], refs[count : count + len(counts)]
    buffers, sems = refs[count + len(counts) : -1], refs[-1]
    get = fetch(sources, buffers, sems)
    at = 0
    for tensor, number in enumerate(counts):
        blocks = [get(at + i) for i in range(number)]
        at += number
        total = times_rows((own_ref, core_ref), first, blocks, part_ref[tensor])
        outs[tensor][...] = total.astype(BF16)


def late_call(tokens, part, blocks):
    flat = [b for tensor in blocks for b in tensor]
    rows, columns = part.shape[1], part.shape[2]
    depth = sum(b.shape[0] for b in flat)
    first = tokens[0].shape[2] - sum(b.shape[0] for b in blocks[0])
    shape = jax.ShapeDtypeStruct((rows, columns), BF16)
    return pl.pallas_call(
        functools.partial(late_kernel, [len(b) for b in blocks], first),
        out_shape=[shape] * len(blocks),
        in_specs=[VMEM] * 3 + [ANY] * len(flat),
        out_specs=[VMEM] * len(blocks),
        scratch_shapes=scratch_for(flat),
        compiler_params=PARAMS,
        cost_estimate=cost(2 * rows * columns * depth, 2 * columns * depth),
        name="late",
    )(*tokens, part, *flat)


def attend_kernel(first, slots, valid_ref, mean_ref, own_ref, core_ref, part_ref, q_ref, k_ref, *refs):
    count = (len(refs) - 3) // 2
    mixed_ref, means_ref = refs[count : count + 2]
    get = fetch(refs[:count], refs[count + 2 : -1], refs[-1])
    scale = 1.0 / math.sqrt(DH)
    rows = own_ref.shape[1]
    frames = mixed_ref.shape[0] // rows
    means_ref[0, frames:, :] = mean_ref[...]
    me = lax.axis_index("seq")
    flags = [valid_ref[me ^ slot].astype(F32) for slot in slots]
    mask = jnp.concatenate([jnp.full((1, rows), flag, F32) for flag in flags], axis=1)
    blocks = [get(i) for i in range(count)]
    v = times_rows((own_ref, core_ref), first, blocks, part_ref[part_ref.shape[0] - 1]).astype(BF16)
    for head in range(v.shape[1] // DH):
        at = slice(head * DH, (head + 1) * DH)
        scores = lax.dot_general(
            q_ref[:, at], k_ref[:, at], (((1,), (1,)), ((), ())), preferred_element_type=F32
        )
        weights = jnp.exp(scores * scale) * mask
        totals = jnp.sum(weights, axis=1, keepdims=True)
        mixed = jnp.dot(weights.astype(BF16), v[:, at], preferred_element_type=F32)
        mixed = (mixed / totals).astype(BF16)
        mixed_ref[:, at] = mixed
        for frame in range(frames):
            part = mixed[frame * rows : (frame + 1) * rows].astype(F32)
            means_ref[0, frame : frame + 1, at] = jnp.mean(part, axis=0, keepdims=True)


def attend_call(slots, valid, token_mean, tokens, part, q, k, blocks):
    rows, columns = q.shape
    depth = tokens[0].shape[2]
    means = rows // tokens[0].shape[1] + token_mean.shape[0]
    first = depth - sum(b.shape[0] for b in blocks)
    return pl.pallas_call(
        functools.partial(attend_kernel, first, slots),
        out_shape=(
            jax.ShapeDtypeStruct((rows, columns), BF16),
            jax.ShapeDtypeStruct((1, means, columns), F32),
        ),
        in_specs=[SMEM] + [VMEM] * 6 + [ANY] * len(blocks),
        out_specs=(VMEM, VMEM),
        scratch_shapes=scratch_for(blocks),
        compiler_params=PARAMS,
        cost_estimate=cost(2 * rows * columns * (depth + 2 * rows), 2 * columns * depth),
        name="attend",
    )(valid, token_mean, *tokens, part, q, k, *blocks)


def times_block(values, parts):
    total, at = None, 0
    for part in parts:
        term = jnp.dot(values[:, at : at + part.shape[0]], part[...], preferred_element_type=F32)
        total = term if total is None else total + term
        at += part.shape[0]
    return total


def out_kernel(counts, mixed_ref, *refs):
    blocks, at = [], 0
    for count in counts:
        blocks.append(refs[at : at + count])
        at += count
    send_ref, keep_ref = refs[at:]
    half = mixed_ref.shape[0] // 2
    columns = blocks[0][0].shape[1]
    for i, parts in enumerate(blocks):
        result = times_block(mixed_ref, parts)
        keep_ref[:, i * columns : (i + 1) * columns] = result[:half]
        send_ref[:, i * columns : (i + 1) * columns] = result[half:].astype(BF16)


def out_call(mixed, blocks):
    flat = [part for parts in blocks for part in parts]
    rows, depth = mixed.shape
    columns = len(blocks) * blocks[0][0].shape[1]
    return pl.pallas_call(
        functools.partial(out_kernel, [len(parts) for parts in blocks]),
        out_shape=(
            jax.ShapeDtypeStruct((rows // 2, columns), BF16),
            jax.ShapeDtypeStruct((rows // 2, columns), F32),
        ),
        in_specs=[VMEM] * (1 + len(flat)),
        out_specs=(VMEM, VMEM),
        compiler_params=PARAMS,
        cost_estimate=cost(2 * rows * columns * depth, 2 * depth * columns + 6 * rows * columns),
        name="out",
    )(mixed, *flat)


def pool_kernel(counts, frames, means_ref, *refs):
    blocks, at = [], 0
    for count in counts:
        blocks.append(refs[at : at + count])
        at += count
    send_ref, keep_ref, held = refs[at:]
    windows = means_ref.shape[0]
    rows = windows * frames
    for r in range(windows):
        for frame in range(frames):
            to = frame * windows + r
            held[to : to + 1, :] = means_ref[r, frame : frame + 1, :]
    values = held[...]
    upper = values.astype(BF16)
    lower = (values - upper.astype(F32)).astype(BF16)
    both = jnp.concatenate([upper, lower], axis=0)
    columns = blocks[0][0].shape[1]
    for i, parts in enumerate(blocks):
        result = times_block(both, parts)
        result = result[:rows] + result[rows:]
        keep_ref[:, i * columns : (i + 1) * columns] = result[: rows // 2]
        send_ref[:, i * columns : (i + 1) * columns] = result[rows // 2 :]


def pool_call(means, blocks, frames):
    flat = [part for parts in blocks for part in parts]
    rows, depth = frames * means.shape[0], means.shape[2]
    columns = len(blocks) * blocks[0][0].shape[1]
    shape = jax.ShapeDtypeStruct((rows // 2, columns), F32)
    return pl.pallas_call(
        functools.partial(pool_kernel, [len(parts) for parts in blocks], frames),
        out_shape=(shape, shape),
        in_specs=[VMEM] * (1 + len(flat)),
        out_specs=(VMEM, VMEM),
        scratch_shapes=[pltpu.VMEM((rows, depth), F32)],
        compiler_params=PARAMS,
        cost_estimate=cost(4 * rows * columns * depth, 2 * depth * columns),
        name="pool",
    )(means, *flat)


def finish_kernel(distances, groups, tokens_ref, *refs):
    out_ref = refs[-1]
    rows = tokens_ref.shape[0]
    slot = 0
    block = tokens_ref.shape[1] // len(distances)
    found = owners(distances)
    for g in range(groups):
        sums, came = refs[2 * g], refs[2 * g + 1]
        for i in range(sums.shape[1] // block):
            at = pl.ds(pl.multiple_of(found[slot] * block, LANES), block)
            here = slice(i * block, (i + 1) * block)
            total = sums[:rows, here] + came[:, here].astype(F32)
            out_ref[:, at] = (tokens_ref[:, at].astype(F32) + total).astype(BF16)
            slot += 1


def finish_call(distances, tokens, sums):
    flat = [part for pair in sums for part in pair]
    return pl.pallas_call(
        functools.partial(finish_kernel, distances, len(sums)),
        out_shape=jax.ShapeDtypeStruct(tokens.shape, BF16),
        in_specs=[VMEM] * (1 + len(flat)),
        out_specs=VMEM,
        compiler_params=PARAMS,
        cost_estimate=cost(4 * tokens.size, 10 * tokens.size),
        name="finish",
    )(tokens, *flat)


def head_kernel(distances, sums_ref, came_ref, means_ref, act_ref, bias_ref, out_ref, pooled):
    windows, width = pooled.shape
    columns = means_ref.shape[2]
    first = means_ref.shape[1] - width // columns
    for i in range(width // columns):
        pooled[:, i * columns : (i + 1) * columns] = means_ref[:, first + i, :]
    block = width // len(distances)
    for i, owner in enumerate(owners(distances)):
        at = pl.ds(pl.multiple_of(owner * block, LANES), block)
        here = slice(i * block, (i + 1) * block)
        pooled[:, at] += sums_ref[:windows, here] + came_ref[:, here]
    values = normalize(pooled[...]).astype(BF16)
    logits = jnp.dot(values, act_ref[...], preferred_element_type=F32) + bias_ref[...]
    me = lax.axis_index("fsdp")
    for i in range(windows):
        out_ref[pl.ds(me ^ i, 1), 0, 0, :] = logits[i : i + 1]


def head_call(distances, sums, came, means, act, bias):
    width, columns = act.shape
    return pl.pallas_call(
        functools.partial(head_kernel, distances),
        out_shape=jax.ShapeDtypeStruct((means.shape[0], 1, 1, columns), F32),
        in_specs=[VMEM] * 5,
        out_specs=VMEM,
        scratch_shapes=[pltpu.VMEM((means.shape[0], width), F32)],
        compiler_params=PARAMS,
        cost_estimate=cost(2 * means.shape[0] * act.size, 2 * act.size),
        name="head",
    )(sums, came, means, act, bias)


def make(mesh):
    fsdp, seq = mesh.shape["fsdp"], mesh.shape["seq"]
    order = sorted(range(fsdp), key=lambda i: ring_place(i, fsdp))
    forward = [(order[i], order[(i + 1) % fsdp]) for i in range(fsdp)]
    backward = [(b, a) for a, b in forward]
    wide_bits = [1 << i for i in range(1, (seq - 1).bit_length())]
    distances = [0]
    for t in range(1, fsdp // 2):
        distances += [-t, t]
    distances.append(fsdp // 2)

    def over_fsdp(value, bit):
        return lax.ppermute(value, "fsdp", [(i, i ^ bit) for i in range(fsdp)])

    def over_seq(value, bit):
        return lax.ppermute(value, "seq", [(i, i ^ bit) for i in range(seq)])

    def ring_step(held):
        blocks, up, down = held
        up = lax.ppermute(up, "fsdp", forward)
        down = lax.ppermute(down, "fsdp", backward)
        return blocks + [up, down], up, down

    def ring_last(held, upwards):
        blocks, up, down = held
        if upwards:
            return blocks + [lax.ppermute(up, "fsdp", forward)]
        return blocks + [lax.ppermute(down, "fsdp", backward)]

    def gate(held, *done):
        blocks, up, down = held
        return blocks, after(up, *done), after(down, *done)

    def per_device(tokens, frame_valid, w_qkv, w_out, w_act, class_table, cam_bias):
        frame_rows, width = tokens.shape[3], tokens.shape[4]
        own_tokens = tokens.reshape(frame_rows, width)
        by_tensor = jnp.transpose(w_qkv, (1, 0, 2))
        steps = fsdp // 2
        rings = [ring_step(([part], part, part)) for part in by_tensor]

        normed, token_mean = norm_call(
            distances, own_tokens, w_qkv.shape[2]
        )
        own = normed[None]
        frame_slots = [0]
        for bit in wide_bits:
            own = jnp.concatenate([own, over_seq(own, bit)], axis=0)
            frame_slots = frame_slots + [o ^ bit for o in frame_slots]
        frame_slots = frame_slots + [o ^ 1 for o in frame_slots]

        soon = 2 if steps > 2 else 1
        for _ in range(1, soon):
            rings = [ring_step(held) for held in rings]
        rows = (own, over_seq(after(own, rings[0][1], rings[0][2]), 1))
        count = 2 * soon + 1
        part = early_call(rows, [held[0][i] for i in range(count) for held in rings], len(rings))
        start = after(w_out, rings[2][1], rings[2][2])
        out = ([start], start, start)
        for i in range(soon, steps - 1):
            rings = [ring_step(held) for held in rings]
            out = ring_step(out)
        out = gate(out, *rings[2][1:])
        qkv = [ring_last(held, upwards) for held, upwards in zip(rings, (True, False, True))]
        while len(out[0]) < 2 * steps - 1:
            out = ring_step(out)
        blocks = [[block] for block in ring_last(out, False)]

        q, k = late_call(rows, part, [qkv[0][count:], qkv[1][count:]])
        mixed, means = attend_call(
            frame_slots, frame_valid.reshape(seq), token_mean, rows, part, q, k, qkv[2][count:]
        )

        cut = len(blocks) - 1
        send, keep = out_call(mixed, blocks[:cut])
        came = over_seq(send, 1)
        bits = [1 << i for i in range((fsdp - 1).bit_length())]
        for bit in bits:
            means = after(means, came) if bit == bits[-1] else means
            means = jnp.concatenate([means, over_fsdp(means, bit)], axis=0)

        def reduce_once(keep, arrived, to):
            total = keep + arrived.astype(F32)
            count = total.shape[0] // 2
            return total[:count], total[count:].astype(to)

        def reduce_all(send, keep, to, arrived=None):
            arrived = over_seq(send, 1) if arrived is None else arrived
            for bit in wide_bits[::-1]:
                keep, leave = reduce_once(keep, arrived, to)
                arrived = over_seq(leave, bit)
            return keep, arrived

        early = reduce_all(send, keep, BF16, came)
        pool_keep, pool_came = reduce_all(*pool_call(after(means, early[1]), blocks, seq), F32)
        sums = [early, reduce_all(*out_call(after(mixed, means), blocks[cut:]), BF16)]
        hidden = finish_call(distances, own_tokens, sums)

        camera_ids = jnp.arange(cam_bias.shape[0], dtype=jnp.int32)
        onehot = (class_table[:, None] == camera_ids[None, :]).astype(F32)
        bias = jnp.dot(onehot, cam_bias, precision=lax.Precision.HIGHEST)[None]
        logits = head_call(distances, pool_keep, pool_came, means, w_act, bias)
        return hidden.reshape(tokens.shape), logits

    return per_device


def plain(tokens, frame_valid, w_qkv, w_out, w_act, class_table, cam_bias):
    windows_here, frame_rows, width = tokens.shape[0], tokens.shape[3], tokens.shape[4]
    own_rows = tokens[:, 0, 0].astype(F32)
    normed = normalize(own_rows).astype(BF16)
    gathered = lax.all_gather(normed[:, None], "seq", axis=1, tiled=True)
    frame_count = gathered.shape[1]
    span = frame_count * frame_rows
    rows = gathered.reshape(windows_here, span, width)
    full_qkv = lax.all_gather(w_qkv, "fsdp", axis=0, tiled=True)
    projected = jnp.einsum("wsd,dcn->wscn", rows, full_qkv, preferred_element_type=F32)
    heads = full_qkv.shape[2] // DH
    projected = projected.astype(BF16).reshape(windows_here, span, 3, heads, DH)
    q, k, v = projected[:, :, 0], projected[:, :, 1], projected[:, :, 2]
    key_mask = jnp.repeat(frame_valid[:, 0].astype(F32), frame_rows, axis=1)
    scores = jnp.einsum("wqhe,wkhe->whqk", q, k, preferred_element_type=F32) / math.sqrt(DH)
    weights = jnp.exp(scores) * key_mask[:, None, None, :]
    totals = jnp.sum(weights, axis=-1)
    mixed = jnp.einsum("whqk,wkhe->wqhe", weights.astype(BF16), v, preferred_element_type=F32)
    mixed = (mixed / jnp.transpose(totals, (0, 2, 1))[:, :, :, None]).astype(BF16)
    mixed = mixed.reshape(windows_here, frame_count, frame_rows, heads * DH)
    mixed = jnp.transpose(mixed, (1, 0, 2, 3)).reshape(-1, heads * DH)
    full_out = lax.all_gather(w_out, "fsdp", axis=1, tiled=True)
    branch = lax.psum_scatter(
        jnp.dot(mixed, full_out, preferred_element_type=F32), "seq", scatter_dimension=0, tiled=True
    )
    hidden = (own_rows + branch.reshape(windows_here, frame_rows, width)).astype(BF16)
    wide = lax.optimization_barrier(hidden).astype(F32)
    pooled = normalize(jnp.mean(wide, axis=1)).astype(BF16)
    camera_ids = jnp.arange(cam_bias.shape[0], dtype=jnp.int32)
    onehot = (class_table[:, None] == camera_ids[None, :]).astype(F32)
    bias = jnp.dot(onehot, cam_bias, precision=lax.Precision.HIGHEST)
    everywhere = lax.all_gather(pooled, "fsdp", axis=0, tiled=True)
    logits = jnp.dot(everywhere, w_act, preferred_element_type=F32) + bias[None, :]
    return (
        hidden.reshape(windows_here, 1, 1, frame_rows, width),
        logits.reshape(logits.shape[0], 1, 1, logits.shape[1]),
    )


def solution(mesh):
    fsdp, seq = mesh.shape["fsdp"], mesh.shape["seq"]

    def whole(tokens, frame_valid, w_qkv, w_out, w_act, class_table, cam_bias):
        args = (tokens, frame_valid, w_qkv, w_out, w_act, class_table, cam_bias)
        powers = all(n & (n - 1) == 0 for n in (fsdp, seq)) and fsdp >= 4 and seq >= 2
        aligned = w_qkv.shape[0] % (fsdp * LANES) == 0 and w_qkv.shape[2] % (seq * 2 * DH) == 0
        one_window = tokens.shape[0] == mesh.shape["groups"] * fsdp
        one_window = one_window and tokens.shape[1] == mesh.shape["sub"] and tokens.shape[2] == seq
        one = make(mesh) if powers and aligned and one_window else plain
        in_specs = (
            P(("groups", "fsdp"), "sub", "seq", None, None),
            P(("groups", "fsdp"), "sub", None),
            P("fsdp", None, "seq"),
            P("seq", "fsdp"),
            P(None, "fsdp"),
            P("fsdp"),
            P(),
        )
        out_specs = (
            P(("groups", "fsdp"), "sub", "seq", None, None),
            P("groups", "sub", "seq", "fsdp"),
        )
        run = jax.shard_map(
            one, mesh=mesh, in_specs=in_specs, out_specs=out_specs, check_vma=False
        )
        return run(*args)

    return whole
```

time: 148 us -> 114 us (0.77)
  starting transfers between devices: 53.3 us -> 40.7 us
  local copies, waits for them, and re-layouts: 14 us -> 2.44 us
  Pallas kernels: 17.2 us -> 11.9 us
  other arithmetic: 5.23 us -> 0.35 us
    ppermute x12 -> x28, waiting for transfers between devices: 8.99 us -> 44.5 us  [the longest x12 41.3 us: ring_step(): up = lax.ppermute(up, 'fsdp', forward)]
    ppermute x15 -> x3, waiting for transfers between devices: 28.9 us -> 8.55 us  [over_fsdp(): return lax.ppermute(value, 'fsdp', [(i, i ^ bit) for i in range(fsdp)])]
    ppermute x15 -> x3, starting transfers between devices: 25.1 us -> 5.9 us  [over_fsdp(): return lax.ppermute(value, 'fsdp', [(i, i ^ bit) for i in range(fsdp)])]
    ppermute x11 -> x8, waiting for transfers between devices: 18.3 us -> 3.81 us  [over_seq(): return lax.ppermute(value, 'seq', [(i, i ^ bit) for i in range(seq)])]
    ppermute x12 -> x28, starting transfers between devices: 20.6 us -> 29.5 us  [the longest x12 19 us: ring_step(): up = lax.ppermute(up, 'fsdp', forward)]
    unnamed x34 -> x15, local copies, waits for them, and re-layouts: 6.44 us -> 1.08 us
    dynamic_slice x4 -> x0, local copies, waits for them, and re-layouts: 3.63 us -> none  [the longest x2 2.06 us: part(): lax.dynamic_slice(by_tensor, (first, 0, (parity ^ k) * half), (count, blo...]
    pallas_call x6, Pallas kernels: 12.9 us -> 10 us  [the longest x1 3.15 us: early_call(): pl.pallas_call(functools.partial(early_kernel, tensors), out_shape=jax.Sh...]
  transfers between devices with their start and end apart: 38 -> 39, of which waited for: 15 -> 20; matrix products, arithmetic and copies ran while one was open for 10% -> 2% of each run, Pallas kernels for 10% -> 8%
where the time goes in v3:
time: 114 us
  waiting for transfers between devices  56.9 us (50%)
  starting transfers between devices  40.7 us (36%)
  Pallas kernels  11.9 us (10%)
  local copies, waits for them, and re-layouts  2.44 us (2%)
    ppermute x12, waiting for transfers between devices, ring_step(): up = lax.ppermute(up, 'fsdp', forward)  41.3 us
    ppermute x12, starting transfers between devices, ring_step(): up = lax.ppermute(up, 'fsdp', forward)  19 us
    ppermute x3, waiting for transfers between devices, over_fsdp(): return lax.ppermute(value, 'fsdp', [(i, i ^ bit) for i in range(fsdp)])  8.55 us
    ppermute x12, starting transfers between devices, ring_step(): down = lax.ppermute(down, 'fsdp', backward)  6.46 us
    ppermute x3, starting transfers between devices, over_fsdp(): return lax.ppermute(value, 'fsdp', [(i, i ^ bit) for i in range(fsdp)])  5.9 us
    ppermute x8, starting transfers between devices, over_seq(): return lax.ppermute(value, 'seq', [(i, i ^ bit) for i in range(seq)])  5.3 us
    ppermute x8, waiting for transfers between devices, over_seq(): return lax.ppermute(value, 'seq', [(i, i ^ bit) for i in range(seq)])  3.81 us
    ppermute x2, starting transfers between devices, ring_last(): return blocks + [lax.ppermute(up, 'fsdp', forward)]  3.15 us
  transfers between devices with their start and end apart: 39, of which 20 were waited for; matrix products, arithmetic and copies ran while one was open for 2% of the time, Pallas kernels for 8%

profile of v3, /device:TPU:0, one launch (start us, length us, event | category | flops | bytes accessed | tf_op | source)
XLA Modules:
  0.0 113.6 jit_solution(1563235465330688879)
XLA Ops:
  2.1 3.0 %collective-permute-start = (bf16[1,128,2048]{2,1,0:T(8,128)(2,1)S(1)}, bf16[1,128,2048]{2,1,0:T(8,128)(2,1)S(1)}, u32[]{:S(2)}, u32[]{:S(2)}) collective-permute-start(bf16[1,128,2048]{2,1,0:T(8,128)(2,1)S(1)} %bitcast.17), channel_id=1, source_target_pairs={{0,2},{1,3},{2,0},{3,1},{4,6},{5,7},{6,4},{7,5},{8,10},{9,11},{10,... | collective-permute-start | bytes 1572872 | tf_op jit(solution)/shard_map/ppermute | solution.py:383
  6.3 1.6 %collective-permute-start.1 = (bf16[256,512]{1,0:T(8,128)(2,1)S(1)}, bf16[256,512]{1,0:T(8,128)(2,1)S(1)}, u32[]{:S(2)}, u32[]{:S(2)}) collective-permute-start(bf16[256,512]{1,0:T(8,128)(2,1)S(1)} %get-tuple-element.42.refs_0_), channel_id=1, source_target_pairs={{0,8},{8,16},{16,24},{24,28},{28,20},{20,12},{12,4},{4,0},{1,9},{9... | collective-permute-start | bytes 786440 | tf_op jit(solution)/shard_map/ppermute | solution.py:387
  10.4 5.2 %collective-permute-done.1.refs_3_ = bf16[256,512]{1,0:T(8,128)(2,1)S(1)} collective-permute-done((bf16[256,512]{1,0:T(8,128)(2,1)S(1)}, bf16[256,512]{1,0:T(8,128)(2,1)S(1)}, u32[]{:S(2)}, u32[]{:S(2)}) %collective-permute-start.1) | collective-permute-done | bytes 262176 | tf_op jit(solution)/shard_map/ppermute | solution.py:387
  17.7 3.6 %collective-permute-done.7.refs_5_ = bf16[256,512]{1,0:T(8,128)(2,1)S(1)} collective-permute-done((bf16[256,512]{1,0:T(8,128)(2,1)S(1)}, bf16[256,512]{1,0:T(8,128)(2,1)S(1)}, u32[]{:S(2)}, u32[]{:S(2)}) %collective-permute-start.7) | collective-permute-done | bytes 262176 | tf_op jit(solution)/shard_map/ppermute | solution.py:387
  23.3 1.6 %collective-permute-start.11 = (bf16[256,512]{1,0:T(8,128)(2,1)S(1)}, bf16[256,512]{1,0:T(8,128)(2,1)S(1)}, u32[]{:S(2)}, u32[]{:S(2)}) collective-permute-start(bf16[256,512]{1,0:T(8,128)(2,1)S(1)} %collective-permute-done.7.refs_5_), channel_id=1, source_target_pairs={{0,8},{8,16},{16,24},{24,28},{28,20},{20,12},{12,4},{4,0},{1,9},{9... | collective-permute-start | bytes 786440 | tf_op jit(solution)/shard_map/ppermute | solution.py:387
  24.9 2.0 %collective-permute-done.2.refs_9_ = bf16[256,512]{1,0:T(8,128)(2,1)S(1)} collective-permute-done((bf16[256,512]{1,0:T(8,128)(2,1)S(1)}, bf16[256,512]{1,0:T(8,128)(2,1)S(1)}, u32[]{:S(2)}, u32[]{:S(2)}) %collective-permute-start.2) | collective-permute-done | bytes 262176 | tf_op jit(solution)/shard_map/ppermute | solution.py:387
  28.6 3.9 %collective-permute-done.6.refs_4_ = bf16[256,512]{1,0:T(8,128)(2,1)S(1)} collective-permute-done((bf16[256,512]{1,0:T(8,128)(2,1)S(1)}, bf16[256,512]{1,0:T(8,128)(2,1)S(1)}, u32[]{:S(2)}, u32[]{:S(2)}) %collective-permute-start.6) | collective-permute-done | bytes 262176 | tf_op jit(solution)/shard_map/ppermute | solution.py:387
  34.5 3.6 %collective-permute-done.11.refs_11_ = bf16[256,512]{1,0:T(8,128)(2,1)S(1)} collective-permute-done((bf16[256,512]{1,0:T(8,128)(2,1)S(1)}, bf16[256,512]{1,0:T(8,128)(2,1)S(1)}, u32[]{:S(2)}, u32[]{:S(2)}) %collective-permute-start.11) | collective-permute-done | bytes 262176 | tf_op jit(solution)/shard_map/ppermute | solution.py:387
  40.1 3.6 %collective-permute-done.10.refs_10_ = bf16[256,512]{1,0:T(8,128)(2,1)S(1)} collective-permute-done((bf16[256,512]{1,0:T(8,128)(2,1)S(1)}, bf16[256,512]{1,0:T(8,128)(2,1)S(1)}, u32[]{:S(2)}, u32[]{:S(2)}) %collective-permute-start.10) | collective-permute-done | bytes 262176 | tf_op jit(solution)/shard_map/ppermute | solution.py:387
  45.8 3.6 %collective-permute-done.20.refs_0_ = bf16[256,512]{1,0:T(8,128)(2,1)S(1)} collective-permute-done((bf16[256,512]{1,0:T(8,128)(2,1)S(1)}, bf16[256,512]{1,0:T(8,128)(2,1)S(1)}, u32[]{:S(2)}, u32[]{:S(2)}) %collective-permute-start.20) | collective-permute-done | bytes 262176 | tf_op jit(solution)/shard_map/ppermute | solution.py:387
  51.4 3.6 %collective-permute-done.23.refs_1_ = bf16[512,256]{1,0:T(8,128)(2,1)S(1)} collective-permute-done((bf16[512,256]{1,0:T(8,128)(2,1)S(1)}, bf16[512,256]{1,0:T(8,128)(2,1)S(1)}, u32[]{:S(2)}, u32[]{:S(2)}) %collective-permute-start.23) | collective-permute-done | bytes 262176 | tf_op jit(solution)/shard_map/ppermute | solution.py:387
  57.0 3.6 %collective-permute-done.14.refs_0_ = bf16[256,512]{1,0:T(8,128)(2,1)S(1)} collective-permute-done((bf16[256,512]{1,0:T(8,128)(2,1)S(1)}, bf16[256,512]{1,0:T(8,128)(2,1)S(1)}, u32[]{:S(2)}, u32[]{:S(2)}) %collective-permute-start.14) | collective-permute-done | bytes 262176 | tf_op jit(solution)/shard_map/ppermute | solution.py:387
  62.6 3.6 %collective-permute-done.17.refs_3_ = bf16[256,512]{1,0:T(8,128)(2,1)S(1)} collective-permute-done((bf16[256,512]{1,0:T(8,128)(2,1)S(1)}, bf16[256,512]{1,0:T(8,128)(2,1)S(1)}, u32[]{:S(2)}, u32[]{:S(2)}) %collective-permute-start.17) | collective-permute-done | bytes 262176 | tf_op jit(solution)/shard_map/ppermute | solution.py:387
  68.2 3.6 %collective-permute-done.25.refs_3_ = bf16[512,256]{1,0:T(8,128)(2,1)S(1)} collective-permute-done((bf16[512,256]{1,0:T(8,128)(2,1)S(1)}, bf16[512,256]{1,0:T(8,128)(2,1)S(1)}, u32[]{:S(2)}, u32[]{:S(2)}) %collective-permute-start.25) | collective-permute-done | bytes 262176 | tf_op jit(solution)/shard_map/ppermute | solution.py:387
  75.4 3.2 %early.1.part_ref = f32[3,512,512]{2,1,0:T(8,128)S(1)} custom-call(bf16[2,128,2048]{2,1,0:T(8,128)(2,1)S(1)} %pad_maximum_fusion.own_ref, bf16[2,128,2048]{2,1,0:T(8,128)(2,1)S(1)} %collective-permute-done.5.core_ref, bf16[256,512]{1,0:T(8,128)(2,1)S(1)} %get-tuple-element.42.refs_0_, bf16[256,512]{1,0:T(8,128)(2,1)S(1)} %get-tuple-element.41.refs_1_, ...), custom_call_target="tpu_custom_call" | custom-call | flops 2013265920 | bytes 3932160 | tf_op jit(solution)/shard_map/early/pallas_call | solution.py:134
  80.4 2.6 %collective-permute-done.22.refs_2_ = bf16[256,512]{1,0:T(8,128)(2,1)S(1)} collective-permute-done((bf16[256,512]{1,0:T(8,128)(2,1)S(1)}, bf16[256,512]{1,0:T(8,128)(2,1)S(1)}, u32[]{:S(2)}, u32[]{:S(2)}) %collective-permute-start.22) | collective-permute-done | bytes 262176 | tf_op jit(solution)/shard_map/ppermute | solution.py:394
  83.0 2.5 %attend.1 = (bf16[512,512]{1,0:T(8,128)(2,1)S(1)}, f32[1,8,512]{2,1,0:T(8,128)S(1)}) custom-call(s32[4]{0:T(128)S(1)} %bitcast.19, f32[4,512]{1,0:T(4,128)S(1)} %get-tuple-element.21.mean_ref, bf16[2,128,2048]{2,1,0:T(8,128)(2,1)S(1)} %pad_maximum_fusion.own_ref, bf16[2,128,2048]{2,1,0:T(8,128)(2,1)S(1)} %collective-permute-done.5.core_ref, ...), custom_call_target="tpu_custom_call" | custom-call | flops 1610612736 | bytes 2097152 | tf_op jit(solution)/shard_map/attend/pallas_call | solution.py:210
  85.5 1.7 %collective-permute-done.27.refs_5_ = bf16[512,256]{1,0:T(8,128)(2,1)S(1)} collective-permute-done((bf16[512,256]{1,0:T(8,128)(2,1)S(1)}, bf16[512,256]{1,0:T(8,128)(2,1)S(1)}, u32[]{:S(2)}, u32[]{:S(2)}) %collective-permute-start.27) | collective-permute-done | bytes 262176 | tf_op jit(solution)/shard_map/ppermute | solution.py:387
  88.4 1.6 %collective-permute-start.31 = (f32[1,8,512]{2,1,0:T(8,128)S(1)}, f32[1,8,512]{2,1,0:T(8,128)S(1)}, u32[]{:S(2)}, u32[]{:S(2)}) collective-permute-start(f32[1,8,512]{2,1,0:T(8,128)S(1)} %get-tuple-element.32), channel_id=1, source_target_pairs={{0,4},{4,0},{8,12},{12,8},{16,20},{20,16},{24,28},{28,24},{1,5},{5... | collective-permute-start | bytes 49160 | tf_op jit(solution)/shard_map/ppermute | solution.py:380
  90.5 1.7 %collective-permute-done.31 = f32[1,8,512]{2,1,0:T(8,128)S(1)} collective-permute-done((f32[1,8,512]{2,1,0:T(8,128)S(1)}, f32[1,8,512]{2,1,0:T(8,128)S(1)}, u32[]{:S(2)}, u32[]{:S(2)}) %collective-permute-start.31) | collective-permute-done | bytes 16416 | tf_op jit(solution)/shard_map/ppermute | solution.py:380
  94.7 4.4 %collective-permute-done.32 = f32[2,8,512]{2,1,0:T(8,128)S(1)} collective-permute-done((f32[2,8,512]{2,1,0:T(8,128)S(1)}, f32[2,8,512]{2,1,0:T(8,128)S(1)}, u32[]{:S(2)}, u32[]{:S(2)}) %collective-permute-start.32) | collective-permute-done | bytes 32800 | tf_op jit(solution)/shard_map/ppermute | solution.py:380
  99.1 2.7 %collective-permute-start.33 = (f32[4,8,512]{2,1,0:T(8,128)S(1)}, f32[4,8,512]{2,1,0:T(8,128)S(1)}, u32[]{:S(2)}, u32[]{:S(2)}) collective-permute-start(f32[4,8,512]{2,1,0:T(8,128)S(1)} %pad_maximum_fusion.1), channel_id=1, source_target_pairs={{0,16},{4,20},{8,24},{12,28},{16,0},{20,4},{24,8},{28,12},{1,17},{... | collective-permute-start | bytes 196616 | tf_op jit(solution)/shard_map/ppermute | solution.py:380
  101.8 2.4 %collective-permute-done.33 = f32[4,8,512]{2,1,0:T(8,128)S(1)} collective-permute-done((f32[4,8,512]{2,1,0:T(8,128)S(1)}, f32[4,8,512]{2,1,0:T(8,128)S(1)}, u32[]{:S(2)}, u32[]{:S(2)}) %collective-permute-start.33) | collective-permute-done | bytes 65568 | tf_op jit(solution)/shard_map/ppermute | solution.py:380
  108.9 2.2 %collective-permute-done.36.refs_3_ = bf16[128,256]{1,0:T(8,128)(2,1)S(1)} collective-permute-done((bf16[128,256]{1,0:T(8,128)(2,1)S(1)}, bf16[128,256]{1,0:T(8,128)(2,1)S(1)}, u32[]{:S(2)}, u32[]{:S(2)}) %collective-permute-start.36) | collective-permute-done | bytes 65568 | tf_op jit(solution)/shard_map/ppermute | solution.py:383
  (92 shorter events, 41.9 us)
Async XLA Ops:
  2.1 21.2 %collective-permute-start = (bf16[1,128,2048]{2,1,0:T(8,128)(2,1)S(1)}, bf16[1,128,2048]{2,1,0:T(8,128)(2,1)S(1)}, u32[]{:S(2)}, u32[]{:S(2)}) collective-permute-start(bf16[1,128,2048]{2,1,0:T(8,128)(2,1)S(1)} %bitcast.17), channel_id=1, source_target_pairs={{0,2},{1,3},{2,0},{3,1},{4,6},{5,7},{6,4},{7,5},{8,10},{9,11},{10,... | collective-permute-start | bytes 1572872 | tf_op jit(solution)/shard_map/ppermute | solution.py:383
  8.4 12.8 %collective-permute-start.7 = (bf16[256,512]{1,0:T(8,128)(2,1)S(1)}, bf16[256,512]{1,0:T(8,128)(2,1)S(1)}, u32[]{:S(2)}, u32[]{:S(2)}) collective-permute-start(bf16[256,512]{1,0:T(8,128)(2,1)S(1)} %get-tuple-element.40.refs_2_), channel_id=1, source_target_pairs={{0,8},{8,16},{16,24},{24,28},{28,20},{20,12},{12,4},{4,0},{1,9},{9... | collective-permute-start | bytes 786440 | tf_op jit(solution)/shard_map/ppermute | solution.py:387
  10.0 12.8 %collective-permute-start.9 = (bf16[256,512]{1,0:T(8,128)(2,1)S(1)}, bf16[256,512]{1,0:T(8,128)(2,1)S(1)}, u32[]{:S(2)}, u32[]{:S(2)}) collective-permute-start(bf16[256,512]{1,0:T(8,128)(2,1)S(1)} %get-tuple-element.40.refs_2_), channel_id=1, source_target_pairs={{8,0},{16,8},{24,16},{28,24},{20,28},{12,20},{4,12},{0,4},{9,1},{1... | collective-permute-start | bytes 786440 | tf_op jit(solution)/shard_map/ppermute | solution.py:388
  15.6 11.2 %collective-permute-start.2 = (bf16[256,512]{1,0:T(8,128)(2,1)S(1)}, bf16[256,512]{1,0:T(8,128)(2,1)S(1)}, u32[]{:S(2)}, u32[]{:S(2)}) collective-permute-start(bf16[256,512]{1,0:T(8,128)(2,1)S(1)} %collective-permute-done.1.refs_3_), channel_id=1, source_target_pairs={{0,8},{8,16},{16,24},{24,28},{28,20},{20,12},{12,4},{4,0},{1,9},{9... | collective-permute-start | bytes 786440 | tf_op jit(solution)/shard_map/ppermute | solution.py:387
  17.2 11.3 %collective-permute-start.4 = (bf16[256,512]{1,0:T(8,128)(2,1)S(1)}, bf16[256,512]{1,0:T(8,128)(2,1)S(1)}, u32[]{:S(2)}, u32[]{:S(2)}) collective-permute-start(bf16[256,512]{1,0:T(8,128)(2,1)S(1)} %collective-permute-done.3.refs_6_), channel_id=1, source_target_pairs={{8,0},{16,8},{24,16},{28,24},{20,28},{12,20},{4,12},{0,4},{9,1},{1... | collective-permute-start | bytes 786440 | tf_op jit(solution)/shard_map/ppermute | solution.py:388
  22.8 11.2 %collective-permute-start.8 = (bf16[256,512]{1,0:T(8,128)(2,1)S(1)}, bf16[256,512]{1,0:T(8,128)(2,1)S(1)}, u32[]{:S(2)}, u32[]{:S(2)}) collective-permute-start(bf16[256,512]{1,0:T(8,128)(2,1)S(1)} %get-tuple-element.41.refs_1_), channel_id=1, source_target_pairs={{8,0},{16,8},{24,16},{28,24},{20,28},{12,20},{4,12},{0,4},{9,1},{1... | collective-permute-start | bytes 786440 | tf_op jit(solution)/shard_map/ppermute | solution.py:388
  23.3 14.8 %collective-permute-start.11 = (bf16[256,512]{1,0:T(8,128)(2,1)S(1)}, bf16[256,512]{1,0:T(8,128)(2,1)S(1)}, u32[]{:S(2)}, u32[]{:S(2)}) collective-permute-start(bf16[256,512]{1,0:T(8,128)(2,1)S(1)} %collective-permute-done.7.refs_5_), channel_id=1, source_target_pairs={{0,8},{8,16},{16,24},{24,28},{28,20},{20,12},{12,4},{4,0},{1,9},{9... | collective-permute-start | bytes 786440 | tf_op jit(solution)/shard_map/ppermute | solution.py:387
  26.9 12.8 %collective-permute-start.13 = (bf16[256,512]{1,0:T(8,128)(2,1)S(1)}, bf16[256,512]{1,0:T(8,128)(2,1)S(1)}, u32[]{:S(2)}, u32[]{:S(2)}) collective-permute-start(bf16[256,512]{1,0:T(8,128)(2,1)S(1)} %collective-permute-done.9.refs_8_), channel_id=1, source_target_pairs={{8,0},{16,8},{24,16},{28,24},{20,28},{12,20},{4,12},{0,4},{9,1},{1... | collective-permute-start | bytes 786440 | tf_op jit(solution)/shard_map/ppermute | solution.py:388
  28.5 46.5 %collective-permute-start.5 = (bf16[2,128,2048]{2,1,0:T(8,128)(2,1)S(1)}, bf16[2,128,2048]{2,1,0:T(8,128)(2,1)S(1)}, u32[]{:S(2)}, u32[]{:S(2)}) collective-permute-start(bf16[2,128,2048]{2,1,0:T(8,128)(2,1)S(1)} %pad_maximum_fusion.own_ref), channel_id=1, source_target_pairs={{0,1},{1,0},{2,3},{3,2},{4,5},{5,4},{6,7},{7,6},{8,9},{9,8},{10,11... | collective-permute-start | bytes 3145736 | tf_op jit(solution)/shard_map/ppermute | solution.py:383
  32.5 11.2 %collective-permute-start.10 = (bf16[256,512]{1,0:T(8,128)(2,1)S(1)}, bf16[256,512]{1,0:T(8,128)(2,1)S(1)}, u32[]{:S(2)}, u32[]{:S(2)}) collective-permute-start(bf16[256,512]{1,0:T(8,128)(2,1)S(1)} %collective-permute-done.6.refs_4_), channel_id=1, source_target_pairs={{0,8},{8,16},{16,24},{24,28},{28,20},{20,12},{12,4},{4,0},{1,9},{9... | collective-permute-start | bytes 786440 | tf_op jit(solution)/shard_map/ppermute | solution.py:387
  34.1 11.2 %collective-permute-start.12 = (bf16[256,512]{1,0:T(8,128)(2,1)S(1)}, bf16[256,512]{1,0:T(8,128)(2,1)S(1)}, u32[]{:S(2)}, u32[]{:S(2)}) collective-permute-start(bf16[256,512]{1,0:T(8,128)(2,1)S(1)} %collective-permute-done.8.refs_7_), channel_id=1, source_target_pairs={{8,0},{16,8},{24,16},{28,24},{20,28},{12,20},{4,12},{0,4},{9,1},{1... | collective-permute-start | bytes 786440 | tf_op jit(solution)/shard_map/ppermute | solution.py:388
  38.1 11.2 %collective-permute-start.20 = (bf16[256,512]{1,0:T(8,128)(2,1)S(1)}, bf16[256,512]{1,0:T(8,128)(2,1)S(1)}, u32[]{:S(2)}, u32[]{:S(2)}) collective-permute-start(bf16[256,512]{1,0:T(8,128)(2,1)S(1)} %collective-permute-done.11.refs_11_), channel_id=1, source_target_pairs={{0,8},{8,16},{16,24},{24,28},{28,20},{20,12},{12,4},{4,0},{1,9},{9... | collective-permute-start | bytes 786440 | tf_op jit(solution)/shard_map/ppermute | solution.py:387
  39.7 11.2 %collective-permute-start.21 = (bf16[256,512]{1,0:T(8,128)(2,1)S(1)}, bf16[256,512]{1,0:T(8,128)(2,1)S(1)}, u32[]{:S(2)}, u32[]{:S(2)}) collective-permute-start(bf16[256,512]{1,0:T(8,128)(2,1)S(1)} %collective-permute-done.13.refs_14_), channel_id=1, source_target_pairs={{8,0},{16,8},{24,16},{28,24},{20,28},{12,20},{4,12},{0,4},{9,1},{1... | collective-permute-start | bytes 786440 | tf_op jit(solution)/shard_map/ppermute | solution.py:388
  45.3 11.2 %collective-permute-start.24 = (bf16[512,256]{1,0:T(8,128)(2,1)S(1)}, bf16[512,256]{1,0:T(8,128)(2,1)S(1)}, u32[]{:S(2)}, u32[]{:S(2)}) collective-permute-start(bf16[512,256]{1,0:T(8,128)(2,1)S(1)} %copy-done.4), channel_id=1, source_target_pairs={{8,0},{16,8},{24,16},{28,24},{20,28},{12,20},{4,12},{0,4},{9,1},{1... | collective-permute-start | bytes 786440 | tf_op jit(solution)/shard_map/ppermute | solution.py:388
  50.9 11.2 %collective-permute-start.15 = (bf16[256,512]{1,0:T(8,128)(2,1)S(1)}, bf16[256,512]{1,0:T(8,128)(2,1)S(1)}, u32[]{:S(2)}, u32[]{:S(2)}) collective-permute-start(bf16[256,512]{1,0:T(8,128)(2,1)S(1)} %collective-permute-done.4.refs_12_), channel_id=1, source_target_pairs={{8,0},{16,8},{24,16},{28,24},{20,28},{12,20},{4,12},{0,4},{9,1},{1... | collective-permute-start | bytes 786440 | tf_op jit(solution)/shard_map/ppermute | solution.py:388
  54.9 11.2 %collective-permute-start.17 = (bf16[256,512]{1,0:T(8,128)(2,1)S(1)}, bf16[256,512]{1,0:T(8,128)(2,1)S(1)}, u32[]{:S(2)}, u32[]{:S(2)}) collective-permute-start(bf16[256,512]{1,0:T(8,128)(2,1)S(1)} %collective-permute-done.10.refs_10_), channel_id=1, source_target_pairs={{0,8},{8,16},{16,24},{24,28},{28,20},{20,12},{12,4},{4,0},{1,9},{9... | collective-permute-start | bytes 786440 | tf_op jit(solution)/shard_map/ppermute | solution.py:387
  56.5 11.2 %collective-permute-start.18 = (bf16[256,512]{1,0:T(8,128)(2,1)S(1)}, bf16[256,512]{1,0:T(8,128)(2,1)S(1)}, u32[]{:S(2)}, u32[]{:S(2)}) collective-permute-start(bf16[256,512]{1,0:T(8,128)(2,1)S(1)} %collective-permute-done.12.refs_13_), channel_id=1, source_target_pairs={{8,0},{16,8},{24,16},{28,24},{20,28},{12,20},{4,12},{0,4},{9,1},{1... | collective-permute-start | bytes 786440 | tf_op jit(solution)/shard_map/ppermute | solution.py:388
  60.6 11.2 %collective-permute-start.25 = (bf16[512,256]{1,0:T(8,128)(2,1)S(1)}, bf16[512,256]{1,0:T(8,128)(2,1)S(1)}, u32[]{:S(2)}, u32[]{:S(2)}) collective-permute-start(bf16[512,256]{1,0:T(8,128)(2,1)S(1)} %collective-permute-done.23.refs_1_), channel_id=1, source_target_pairs={{0,8},{8,16},{16,24},{24,28},{28,20},{20,12},{12,4},{4,0},{1,9},{9... | collective-permute-start | bytes 786440 | tf_op jit(solution)/shard_map/ppermute | solution.py:387
  66.2 12.4 %collective-permute-start.16 = (bf16[256,512]{1,0:T(8,128)(2,1)S(1)}, bf16[256,512]{1,0:T(8,128)(2,1)S(1)}, u32[]{:S(2)}, u32[]{:S(2)}) collective-permute-start(bf16[256,512]{1,0:T(8,128)(2,1)S(1)} %collective-permute-done.14.refs_0_), channel_id=1, source_target_pairs={{0,8},{8,16},{16,24},{24,28},{28,20},{20,12},{12,4},{4,0},{1,9},{9... | collective-permute-start | bytes 786440 | tf_op jit(solution)/shard_map/ppermute | solution.py:394
  71.8 11.2 %collective-permute-start.22 = (bf16[256,512]{1,0:T(8,128)(2,1)S(1)}, bf16[256,512]{1,0:T(8,128)(2,1)S(1)}, u32[]{:S(2)}, u32[]{:S(2)}) collective-permute-start(bf16[256,512]{1,0:T(8,128)(2,1)S(1)} %collective-permute-done.20.refs_0_), channel_id=1, source_target_pairs={{0,8},{8,16},{16,24},{24,28},{28,20},{20,12},{12,4},{4,0},{1,9},{9... | collective-permute-start | bytes 786440 | tf_op jit(solution)/shard_map/ppermute | solution.py:394
  73.4 13.8 %collective-permute-start.27 = (bf16[512,256]{1,0:T(8,128)(2,1)S(1)}, bf16[512,256]{1,0:T(8,128)(2,1)S(1)}, u32[]{:S(2)}, u32[]{:S(2)}) collective-permute-start(bf16[512,256]{1,0:T(8,128)(2,1)S(1)} %collective-permute-done.25.refs_3_), channel_id=1, source_target_pairs={{0,8},{8,16},{16,24},{24,28},{28,20},{20,12},{12,4},{4,0},{1,9},{9... | collective-permute-start | bytes 786440 | tf_op jit(solution)/shard_map/ppermute | solution.py:387
  75.0 12.2 %collective-permute-start.28 = (bf16[512,256]{1,0:T(8,128)(2,1)S(1)}, bf16[512,256]{1,0:T(8,128)(2,1)S(1)}, u32[]{:S(2)}, u32[]{:S(2)}) collective-permute-start(bf16[512,256]{1,0:T(8,128)(2,1)S(1)} %collective-permute-done.26.refs_4_), channel_id=1, source_target_pairs={{8,0},{16,8},{24,16},{28,24},{20,28},{12,20},{4,12},{0,4},{9,1},{1... | collective-permute-start | bytes 786440 | tf_op jit(solution)/shard_map/ppermute | solution.py:388
  90.0 14.3 %collective-permute-start.34 = (bf16[512,256]{1,0:T(8,128)(2,1)S(1)}, bf16[512,256]{1,0:T(8,128)(2,1)S(1)}, u32[]{:S(2)}, u32[]{:S(2)}) collective-permute-start(bf16[512,256]{1,0:T(8,128)(2,1)S(1)} %collective-permute-done.28.refs_6_), channel_id=1, source_target_pairs={{8,0},{16,8},{24,16},{28,24},{20,28},{12,20},{4,12},{0,4},{9,1},{1... | collective-permute-start | bytes 786440 | tf_op jit(solution)/shard_map/ppermute | solution.py:395
  94.0 11.5 %collective-permute-start.30 = (bf16[128,1792]{1,0:T(8,128)(2,1)S(1)}, bf16[128,1792]{1,0:T(8,128)(2,1)S(1)}, u32[]{:S(2)}, u32[]{:S(2)}) collective-permute-start(bf16[128,1792]{1,0:T(8,128)(2,1)S(1)} %slice.34), channel_id=1, source_target_pairs={{0,2},{1,3},{2,0},{3,1},{4,6},{5,7},{6,4},{7,5},{8,10},{9,11},{10,... | collective-permute-start | bytes 1376264 | tf_op jit(solution)/shard_map/ppermute | solution.py:383
  (22 other events, 272.4 us)

commit v4 on v3

--- a/solution.py
+++ b/solution.py
@@ -14,6 +14,7 @@
 BF16 = jnp.bfloat16
 VMEM = pl.BlockSpec(memory_space=pltpu.VMEM)
 SMEM = pl.BlockSpec(memory_space=pltpu.SMEM)
+WINDOW = 4
 PARAMS = pltpu.CompilerParams(vmem_limit_bytes=16 * 2**20)
 
 
@@ -333,7 +334,7 @@
     )(tokens, *flat)
 
 
-def head_kernel(distances, sums_ref, came_ref, means_ref, act_ref, bias_ref, out_ref, pooled):
+def head_kernel(distances, slots, sums_ref, came_ref, means_ref, act_ref, bias_ref, out_ref, pooled):
     windows, width = pooled.shape
     columns = means_ref.shape[2]
     first = means_ref.shape[1] - width // columns
@@ -347,14 +348,14 @@
     values = normalize(pooled[...]).astype(BF16)
     logits = jnp.dot(values, act_ref[...], preferred_element_type=F32) + bias_ref[...]
     me = lax.axis_index("fsdp")
-    for i in range(windows):
-        out_ref[pl.ds(me ^ i, 1), 0, 0, :] = logits[i : i + 1]
-
-
-def head_call(distances, sums, came, means, act, bias):
+    for i, slot in enumerate(slots):
+        out_ref[pl.ds(me ^ slot, 1), 0, 0, :] = logits[i : i + 1]
+
+
+def head_call(distances, slots, sums, came, means, act, bias):
     width, columns = act.shape
     return pl.pallas_call(
-        functools.partial(head_kernel, distances),
+        functools.partial(head_kernel, distances, slots),
         out_shape=jax.ShapeDtypeStruct((means.shape[0], 1, 1, columns), F32),
         in_specs=[VMEM] * 5,
         out_specs=VMEM,
@@ -382,32 +383,29 @@
     def over_seq(value, bit):
         return lax.ppermute(value, "seq", [(i, i ^ bit) for i in range(seq)])
 
-    def ring_step(held):
-        blocks, up, down = held
-        up = lax.ppermute(up, "fsdp", forward)
-        down = lax.ppermute(down, "fsdp", backward)
-        return blocks + [up, down], up, down
-
-    def ring_last(held, upwards):
-        blocks, up, down = held
-        if upwards:
-            return blocks + [lax.ppermute(up, "fsdp", forward)]
-        return blocks + [lax.ppermute(down, "fsdp", backward)]
-
-    def gate(held, *done):
-        blocks, up, down = held
-        return blocks, after(up, *done), after(down, *done)
-
     def per_device(tokens, frame_valid, w_qkv, w_out, w_act, class_table, cam_bias):
         frame_rows, width = tokens.shape[3], tokens.shape[4]
         own_tokens = tokens.reshape(frame_rows, width)
         by_tensor = jnp.transpose(w_qkv, (1, 0, 2))
-        steps = fsdp // 2
-        rings = [ring_step(([part], part, part)) for part in by_tensor]
-
-        normed, token_mean = norm_call(
-            distances, own_tokens, w_qkv.shape[2]
-        )
+        sent = []
+        chains = {"q": by_tensor[0], "k": by_tensor[1], "v": by_tensor[2], "o": w_out}
+        edge = {name: [start, start] for name, start in chains.items()}
+        came = {name: [start] for name, start in chains.items()}
+
+        def move(name, way):
+            value = edge[name][way]
+            if len(sent) >= WINDOW:
+                value = after(value, sent[-WINDOW])
+            value = lax.ppermute(value, "fsdp", backward if way else forward)
+            edge[name][way] = value
+            came[name].append(value)
+            sent.append(value)
+
+        def both(name):
+            move(name, 0)
+            move(name, 1)
+
+        normed, token_mean = norm_call(distances, own_tokens, w_qkv.shape[2])
         own = normed[None]
         frame_slots = [0]
         for bit in wide_bits:
@@ -415,57 +413,70 @@
             frame_slots = frame_slots + [o ^ bit for o in frame_slots]
         frame_slots = frame_slots + [o ^ 1 for o in frame_slots]
 
+        steps = fsdp // 2
         soon = 2 if steps > 2 else 1
-        for _ in range(1, soon):
-            rings = [ring_step(held) for held in rings]
-        rows = (own, over_seq(after(own, rings[0][1], rings[0][2]), 1))
+        for _ in range(soon):
+            for name in "qkv":
+                both(name)
         count = 2 * soon + 1
-        part = early_call(rows, [held[0][i] for i in range(count) for held in rings], len(rings))
-        start = after(w_out, rings[2][1], rings[2][2])
-        out = ([start], start, start)
-        for i in range(soon, steps - 1):
-            rings = [ring_step(held) for held in rings]
-            out = ring_step(out)
-        out = gate(out, *rings[2][1:])
-        qkv = [ring_last(held, upwards) for held, upwards in zip(rings, (True, False, True))]
-        while len(out[0]) < 2 * steps - 1:
-            out = ring_step(out)
-        blocks = [[block] for block in ring_last(out, False)]
+        rows = (own, over_seq(own, 1))
+        part = early_call(rows, [came[name][i] for i in range(count) for name in "qkv"], 3)
+        for _ in range(soon, steps - 1):
+            for name in "qkv":
+                both(name)
+        both("o")
+        move("q", 0)
+        move("k", 1)
+        move("v", 0)
+        for _ in range(1, steps - 1):
+            both("o")
+        move("o", 1)
+
+        qkv, blocks = [came[name] for name in "qkv"], [[block] for block in came["o"]]
 
         q, k = late_call(rows, part, [qkv[0][count:], qkv[1][count:]])
         mixed, means = attend_call(
             frame_slots, frame_valid.reshape(seq), token_mean, rows, part, q, k, qkv[2][count:]
         )
 
-        cut = len(blocks) - 1
-        send, keep = out_call(mixed, blocks[:cut])
-        came = over_seq(send, 1)
-        bits = [1 << i for i in range((fsdp - 1).bit_length())]
-        for bit in bits:
-            means = after(means, came) if bit == bits[-1] else means
-            means = jnp.concatenate([means, over_fsdp(means, bit)], axis=0)
-
         def reduce_once(keep, arrived, to):
             total = keep + arrived.astype(F32)
-            count = total.shape[0] // 2
-            return total[:count], total[count:].astype(to)
-
-        def reduce_all(send, keep, to, arrived=None):
-            arrived = over_seq(send, 1) if arrived is None else arrived
+            half = total.shape[0] // 2
+            return total[:half], total[half:].astype(to)
+
+        def reduce_all(send, keep, to, *done):
+            crossed = arrived = over_seq(send, 1)
             for bit in wide_bits[::-1]:
                 keep, leave = reduce_once(keep, arrived, to)
-                arrived = over_seq(leave, bit)
-            return keep, arrived
-
-        early = reduce_all(send, keep, BF16, came)
-        pool_keep, pool_came = reduce_all(*pool_call(after(means, early[1]), blocks, seq), F32)
-        sums = [early, reduce_all(*out_call(after(mixed, means), blocks[cut:]), BF16)]
+                arrived = over_seq(after(leave, *done) if done else leave, bit)
+            return keep, arrived, crossed
+
+        windows = [0]
+        bits = [1 << i for i in range((fsdp - 1).bit_length())][::-1]
+        seen = []
+
+        def gather(means, bit, *done):
+            seen.append(over_fsdp(after(means, *done) if done else means, bit))
+            windows.extend([window ^ bit for window in windows])
+            return jnp.concatenate([means, seen[-1]], axis=0)
+
+        means = gather(means, bits[0])
+        cut = min(5, len(blocks) - 1)
+        near, last = [block for (block,) in blocks[cut:-1]], blocks[-1][0]
+        *early, crossed = reduce_all(*out_call(after(mixed, seen[0]), blocks[:cut]), BF16)
+        waits = {2: (early[1],)}
+        for i, bit in enumerate(bits[1:], 1):
+            means = gather(means, bit, *waits.get(i, ()))
+
+        pool_keep, pool_came, _ = reduce_all(*pool_call(after(means, early[1]), blocks, seq), F32)
+        later = reduce_all(*out_call(after(mixed, means), blocks[cut:]), BF16)
+        sums = [early, later[:2]]
         hidden = finish_call(distances, own_tokens, sums)
 
         camera_ids = jnp.arange(cam_bias.shape[0], dtype=jnp.int32)
         onehot = (class_table[:, None] == camera_ids[None, :]).astype(F32)
         bias = jnp.dot(onehot, cam_bias, precision=lax.Precision.HIGHEST)[None]
-        logits = head_call(distances, pool_keep, pool_came, means, w_act, bias)
+        logits = head_call(distances, windows, pool_keep, pool_came, means, w_act, bias)
         return hidden.reshape(tokens.shape), logits
 
     return per_device

time: 114 us -> 112 us (0.982)
  waiting for transfers between devices: 56.9 us -> 48.3 us
  starting transfers between devices: 40.7 us -> 48.3 us
    ppermute x28, waiting for transfers between devices: 44.5 us -> 37 us  [move(): value = lax.ppermute(value, 'fsdp', backward if way else forward)]
    ppermute x28, starting transfers between devices: 29.5 us -> 36.9 us  [move(): value = lax.ppermute(value, 'fsdp', backward if way else forward)]
    ppermute x3, waiting for transfers between devices: 8.55 us -> 5.83 us  [over_fsdp(): return lax.ppermute(value, 'fsdp', [(i, i ^ bit) for i in range(fsdp)])]
    ppermute x8, waiting for transfers between devices: 3.81 us -> 5.48 us  [over_seq(): return lax.ppermute(value, 'seq', [(i, i ^ bit) for i in range(seq)])]
    squeeze x0 -> x1, local copies, waits for them, and re-layouts: none -> 1.22 us  [per_device(): by_tensor[2]]
    another operation x1 -> x0, local copies, waits for them, and re-layouts: 1.2 us -> none  [per_device(): rings = [ring_step(([part], part, part)) for part in by_tensor]]
    ppermute x8, starting transfers between devices: 5.3 us -> 6.5 us  [over_seq(): return lax.ppermute(value, 'seq', [(i, i ^ bit) for i in range(seq)])]
  transfers between devices with their start and end apart: 39 -> 39, of which waited for: 20 -> 28; matrix products, arithmetic and copies ran while one was open for 2% -> 1% of each run, Pallas kernels for 8% -> 9%
where the time goes in v4:
time: 112 us
  starting transfers between devices  48.3 us (43%)
  waiting for transfers between devices  48.3 us (43%)
  Pallas kernels  11.9 us (11%)
  local copies, waits for them, and re-layouts  1.42 us (1%)
    ppermute x28, waiting for transfers between devices, move(): value = lax.ppermute(value, 'fsdp', backward if way else forward)  37 us
    ppermute x28, starting transfers between devices, move(): value = lax.ppermute(value, 'fsdp', backward if way else forward)  36.9 us
    ppermute x8, starting transfers between devices, over_seq(): return lax.ppermute(value, 'seq', [(i, i ^ bit) for i in range(seq)])  6.5 us
    ppermute x3, waiting for transfers between devices, over_fsdp(): return lax.ppermute(value, 'fsdp', [(i, i ^ bit) for i in range(fsdp)])  5.83 us
    ppermute x8, waiting for transfers between devices, over_seq(): return lax.ppermute(value, 'seq', [(i, i ^ bit) for i in range(seq)])  5.48 us
    ppermute x3, starting transfers between devices, over_fsdp(): return lax.ppermute(value, 'fsdp', [(i, i ^ bit) for i in range(fsdp)])  4.82 us
    pallas_call x1, Pallas kernels, early_call(): pl.pallas_call(functools.partial(early_kernel, tensors), out_shape=jax.Sh...  3.15 us
    pallas_call x1, Pallas kernels, attend_call(): pl.pallas_call(functools.partial(attend_kernel, first, slots), out_shape=...  2.5 us
  transfers between devices with their start and end apart: 39, of which 28 were waited for; matrix products, arithmetic and copies ran while one was open for 1% of the time, Pallas kernels for 9%

profile of v4, /device:TPU:0, one launch (start us, length us, event | category | flops | bytes accessed | tf_op | source)
XLA Modules:
  0.0 111.5 jit_solution(12261333264788739339)
XLA Ops:
  1.9 3.1 %collective-permute-start.2 = (bf16[256,512]{1,0:T(8,128)(2,1)S(1)}, bf16[256,512]{1,0:T(8,128)(2,1)S(1)}, u32[]{:S(2)}, u32[]{:S(2)}) collective-permute-start(bf16[256,512]{1,0:T(8,128)(2,1)S(1)} %get-tuple-element.84.refs_0_), channel_id=1, source_target_pairs={{0,8},{8,16},{16,24},{24,28},{28,20},{20,12},{12,4},{4,0},{1,9},{9... | collective-permute-start | bytes 786440 | tf_op jit(solution)/shard_map/ppermute | solution.py:399
  9.4 2.6 %collective-permute-done.2.refs_3_ = bf16[256,512]{1,0:T(8,128)(2,1)S(1)} collective-permute-done((bf16[256,512]{1,0:T(8,128)(2,1)S(1)}, bf16[256,512]{1,0:T(8,128)(2,1)S(1)}, u32[]{:S(2)}, u32[]{:S(2)}) %collective-permute-start.2) | collective-permute-done | bytes 262176 | tf_op jit(solution)/shard_map/ppermute | solution.py:399
  12.0 2.1 %collective-permute-start.4 = (bf16[256,512]{1,0:T(8,128)(2,1)S(1)}, bf16[256,512]{1,0:T(8,128)(2,1)S(1)}, u32[]{:S(2)}, u32[]{:S(2)}) collective-permute-start(bf16[256,512]{1,0:T(8,128)(2,1)S(1)} %get-tuple-element.45.refs_2_), channel_id=1, source_target_pairs={{0,8},{8,16},{16,24},{24,28},{28,20},{20,12},{12,4},{4,0},{1,9},{9... | collective-permute-start | bytes 786440 | tf_op jit(solution)/shard_map/ppermute | solution.py:399
  17.6 2.1 %collective-permute-start.8 = (bf16[256,512]{1,0:T(8,128)(2,1)S(1)}, bf16[256,512]{1,0:T(8,128)(2,1)S(1)}, u32[]{:S(2)}, u32[]{:S(2)}) collective-permute-start(bf16[256,512]{1,0:T(8,128)(2,1)S(1)} %collective-permute-done.2.refs_3_), channel_id=1, source_target_pairs={{0,8},{8,16},{16,24},{24,28},{28,20},{20,12},{12,4},{4,0},{1,9},{9... | collective-permute-start | bytes 786440 | tf_op jit(solution)/shard_map/ppermute | solution.py:399
  19.8 2.1 %collective-permute-done.6.refs_7_ = bf16[256,512]{1,0:T(8,128)(2,1)S(1)} collective-permute-done((bf16[256,512]{1,0:T(8,128)(2,1)S(1)}, bf16[256,512]{1,0:T(8,128)(2,1)S(1)}, u32[]{:S(2)}, u32[]{:S(2)}) %collective-permute-start.6) | collective-permute-done | bytes 262176 | tf_op jit(solution)/shard_map/ppermute | solution.py:399
  23.3 2.1 %collective-permute-start.9 = (bf16[256,512]{1,0:T(8,128)(2,1)S(1)}, bf16[256,512]{1,0:T(8,128)(2,1)S(1)}, u32[]{:S(2)}, u32[]{:S(2)}) collective-permute-start(bf16[256,512]{1,0:T(8,128)(2,1)S(1)} %collective-permute-done.3.refs_4_), channel_id=1, source_target_pairs={{0,8},{8,16},{16,24},{24,28},{28,20},{20,12},{12,4},{4,0},{1,9},{9... | collective-permute-start | bytes 786440 | tf_op jit(solution)/shard_map/ppermute | solution.py:399
  28.9 2.1 %collective-permute-start.10 = (bf16[256,512]{1,0:T(8,128)(2,1)S(1)}, bf16[256,512]{1,0:T(8,128)(2,1)S(1)}, u32[]{:S(2)}, u32[]{:S(2)}) collective-permute-start(bf16[256,512]{1,0:T(8,128)(2,1)S(1)} %collective-permute-done.4.refs_5_), channel_id=1, source_target_pairs={{0,8},{8,16},{16,24},{24,28},{28,20},{20,12},{12,4},{4,0},{1,9},{9... | collective-permute-start | bytes 786440 | tf_op jit(solution)/shard_map/ppermute | solution.py:399
  31.0 2.1 %collective-permute-done.11.refs_12_ = bf16[256,512]{1,0:T(8,128)(2,1)S(1)} collective-permute-done((bf16[256,512]{1,0:T(8,128)(2,1)S(1)}, bf16[256,512]{1,0:T(8,128)(2,1)S(1)}, u32[]{:S(2)}, u32[]{:S(2)}) %collective-permute-start.11) | collective-permute-done | bytes 262176 | tf_op jit(solution)/shard_map/ppermute | solution.py:399
  34.5 2.1 %collective-permute-start.14 = (bf16[256,512]{1,0:T(8,128)(2,1)S(1)}, bf16[256,512]{1,0:T(8,128)(2,1)S(1)}, u32[]{:S(2)}, u32[]{:S(2)}) collective-permute-start(bf16[256,512]{1,0:T(8,128)(2,1)S(1)} %collective-permute-done.8.refs_9_), channel_id=1, source_target_pairs={{0,8},{8,16},{16,24},{24,28},{28,20},{20,12},{12,4},{4,0},{1,9},{9... | collective-permute-start | bytes 786440 | tf_op jit(solution)/shard_map/ppermute | solution.py:399
  36.6 2.1 %collective-permute-done.12.refs_13_ = bf16[256,512]{1,0:T(8,128)(2,1)S(1)} collective-permute-done((bf16[256,512]{1,0:T(8,128)(2,1)S(1)}, bf16[256,512]{1,0:T(8,128)(2,1)S(1)}, u32[]{:S(2)}, u32[]{:S(2)}) %collective-permute-start.12) | collective-permute-done | bytes 262176 | tf_op jit(solution)/shard_map/ppermute | solution.py:399
  40.1 2.1 %collective-permute-start.18 = (bf16[256,512]{1,0:T(8,128)(2,1)S(1)}, bf16[256,512]{1,0:T(8,128)(2,1)S(1)}, u32[]{:S(2)}, u32[]{:S(2)}) collective-permute-start(bf16[256,512]{1,0:T(8,128)(2,1)S(1)} %collective-permute-done.9.refs_10_), channel_id=1, source_target_pairs={{0,8},{8,16},{16,24},{24,28},{28,20},{20,12},{12,4},{4,0},{1,9},{9... | collective-permute-start | bytes 786440 | tf_op jit(solution)/shard_map/ppermute | solution.py:399
  45.7 2.1 %collective-permute-start.16 = (bf16[256,512]{1,0:T(8,128)(2,1)S(1)}, bf16[256,512]{1,0:T(8,128)(2,1)S(1)}, u32[]{:S(2)}, u32[]{:S(2)}) collective-permute-start(bf16[256,512]{1,0:T(8,128)(2,1)S(1)} %collective-permute-done.10.refs_11_), channel_id=1, source_target_pairs={{0,8},{8,16},{16,24},{24,28},{28,20},{20,12},{12,4},{4,0},{1,9},{9... | collective-permute-start | bytes 786440 | tf_op jit(solution)/shard_map/ppermute | solution.py:399
  47.9 2.1 %collective-permute-done.15.refs_1_ = bf16[256,512]{1,0:T(8,128)(2,1)S(1)} collective-permute-done((bf16[256,512]{1,0:T(8,128)(2,1)S(1)}, bf16[256,512]{1,0:T(8,128)(2,1)S(1)}, u32[]{:S(2)}, u32[]{:S(2)}) %collective-permute-start.15) | collective-permute-done | bytes 262176 | tf_op jit(solution)/shard_map/ppermute | solution.py:399
  51.4 2.1 %collective-permute-start.22 = (bf16[512,256]{1,0:T(8,128)(2,1)S(1)}, bf16[512,256]{1,0:T(8,128)(2,1)S(1)}, u32[]{:S(2)}, u32[]{:S(2)}) collective-permute-start(bf16[512,256]{1,0:T(8,128)(2,1)S(1)} %copy-done.3), channel_id=1, source_target_pairs={{0,8},{8,16},{16,24},{24,28},{28,20},{20,12},{12,4},{4,0},{1,9},{9... | collective-permute-start | bytes 786440 | tf_op jit(solution)/shard_map/ppermute | solution.py:399
  57.0 2.1 %collective-permute-start.17 = (bf16[256,512]{1,0:T(8,128)(2,1)S(1)}, bf16[256,512]{1,0:T(8,128)(2,1)S(1)}, u32[]{:S(2)}, u32[]{:S(2)}) collective-permute-start(bf16[256,512]{1,0:T(8,128)(2,1)S(1)} %collective-permute-done.14.refs_0_), channel_id=1, source_target_pairs={{0,8},{8,16},{16,24},{24,28},{28,20},{20,12},{12,4},{4,0},{1,9},{9... | collective-permute-start | bytes 786440 | tf_op jit(solution)/shard_map/ppermute | solution.py:399
  62.6 2.1 %collective-permute-start.23 = (bf16[256,512]{1,0:T(8,128)(2,1)S(1)}, bf16[256,512]{1,0:T(8,128)(2,1)S(1)}, u32[]{:S(2)}, u32[]{:S(2)}) collective-permute-start(bf16[256,512]{1,0:T(8,128)(2,1)S(1)} %collective-permute-done.16.refs_0_), channel_id=1, source_target_pairs={{0,8},{8,16},{16,24},{24,28},{28,20},{20,12},{12,4},{4,0},{1,9},{9... | collective-permute-start | bytes 786440 | tf_op jit(solution)/shard_map/ppermute | solution.py:399
  64.7 2.1 %collective-permute-done.25.refs_2_ = bf16[512,256]{1,0:T(8,128)(2,1)S(1)} collective-permute-done((bf16[512,256]{1,0:T(8,128)(2,1)S(1)}, bf16[512,256]{1,0:T(8,128)(2,1)S(1)}, u32[]{:S(2)}, u32[]{:S(2)}) %collective-permute-start.25) | collective-permute-done | bytes 262176 | tf_op jit(solution)/shard_map/ppermute | solution.py:399
  70.3 3.1 %early.1.part_ref = f32[3,512,512]{2,1,0:T(8,128)S(1)} custom-call(bf16[2,128,2048]{2,1,0:T(8,128)(2,1)S(1)} %pad_maximum_fusion.own_ref, bf16[2,128,2048]{2,1,0:T(8,128)(2,1)S(1)} %collective-permute-done.1.core_ref, bf16[256,512]{1,0:T(8,128)(2,1)S(1)} %get-tuple-element.84.refs_0_, bf16[256,512]{1,0:T(8,128)(2,1)S(1)} %get-tuple-element.83.refs_1_, ...), custom_call_target="tpu_custom_call" | custom-call | flops 2013265920 | bytes 3932160 | tf_op jit(solution)/shard_map/early/pallas_call | solution.py:135
  74.9 2.5 %attend.1 = (bf16[512,512]{1,0:T(8,128)(2,1)S(1)}, f32[1,8,512]{2,1,0:T(8,128)S(1)}) custom-call(s32[4]{0:T(128)S(1)} %bitcast.19, f32[4,512]{1,0:T(4,128)S(1)} %get-tuple-element.42.mean_ref, bf16[2,128,2048]{2,1,0:T(8,128)(2,1)S(1)} %pad_maximum_fusion.own_ref, bf16[2,128,2048]{2,1,0:T(8,128)(2,1)S(1)} %collective-permute-done.1.core_ref, ...), custom_call_target="tpu_custom_call" | custom-call | flops 1610612736 | bytes 2097152 | tf_op jit(solution)/shard_map/attend/pallas_call | solution.py:211
  77.4 2.2 %collective-permute-start.24 = (f32[1,8,512]{2,1,0:T(8,128)S(1)}, f32[1,8,512]{2,1,0:T(8,128)S(1)}, u32[]{:S(2)}, u32[]{:S(2)}) collective-permute-start(f32[1,8,512]{2,1,0:T(8,128)S(1)} %get-tuple-element.65), channel_id=1, source_target_pairs={{0,16},{4,20},{8,24},{12,28},{16,0},{20,4},{24,8},{28,12},{1,17},{... | collective-permute-start | bytes 49160 | tf_op jit(solution)/shard_map/ppermute | solution.py:381
  79.5 2.5 %collective-permute-done.24 = f32[1,8,512]{2,1,0:T(8,128)S(1)} collective-permute-done((f32[1,8,512]{2,1,0:T(8,128)S(1)}, f32[1,8,512]{2,1,0:T(8,128)S(1)}, u32[]{:S(2)}, u32[]{:S(2)}) %collective-permute-start.24) | collective-permute-done | bytes 16416 | tf_op jit(solution)/shard_map/ppermute | solution.py:381
  87.9 5.0 %collective-permute-done.33.refs_1_.refs_6_ = bf16[512,256]{1,0:T(8,128)(2,1)S(1)} collective-permute-done((bf16[512,256]{1,0:T(8,128)(2,1)S(1)}, bf16[512,256]{1,0:T(8,128)(2,1)S(1)}, u32[]{:S(2)}, u32[]{:S(2)}) %collective-permute-start.33) | collective-permute-done | bytes 262176 | tf_op jit(solution)/shard_map/ppermute | solution.py:399
  96.7 3.3 %collective-permute-done.31 = f32[4,8,512]{2,1,0:T(8,128)S(1)} collective-permute-done((f32[4,8,512]{2,1,0:T(8,128)S(1)}, f32[4,8,512]{2,1,0:T(8,128)S(1)}, u32[]{:S(2)}, u32[]{:S(2)}) %collective-permute-start.31) | collective-permute-done | bytes 65568 | tf_op jit(solution)/shard_map/ppermute | solution.py:381
  108.0 2.5 %collective-permute-done.36.refs_3_ = bf16[128,768]{1,0:T(8,128)(2,1)S(1)} collective-permute-done((bf16[128,768]{1,0:T(8,128)(2,1)S(1)}, bf16[128,768]{1,0:T(8,128)(2,1)S(1)}, u32[]{:S(2)}, u32[]{:S(2)}) %collective-permute-start.36) | collective-permute-done | bytes 196640 | tf_op jit(solution)/shard_map/ppermute | solution.py:384
  (92 shorter events, 52.4 us)
Async XLA Ops:
  5.4 20.0 %collective-permute-start = (bf16[1,128,2048]{2,1,0:T(8,128)(2,1)S(1)}, bf16[1,128,2048]{2,1,0:T(8,128)(2,1)S(1)}, u32[]{:S(2)}, u32[]{:S(2)}) collective-permute-start(bf16[1,128,2048]{2,1,0:T(8,128)(2,1)S(1)} %bitcast.17), channel_id=1, source_target_pairs={{0,2},{1,3},{2,0},{3,1},{4,6},{5,7},{6,4},{7,5},{8,10},{9,11},{10,... | collective-permute-start | bytes 1572872 | tf_op jit(solution)/shard_map/ppermute | solution.py:384
  9.0 12.8 %collective-permute-start.6 = (bf16[256,512]{1,0:T(8,128)(2,1)S(1)}, bf16[256,512]{1,0:T(8,128)(2,1)S(1)}, u32[]{:S(2)}, u32[]{:S(2)}) collective-permute-start(bf16[256,512]{1,0:T(8,128)(2,1)S(1)} %get-tuple-element.83.refs_1_), channel_id=1, source_target_pairs={{8,0},{16,8},{24,16},{28,24},{20,28},{12,20},{4,12},{0,4},{9,1},{1... | collective-permute-start | bytes 786440 | tf_op jit(solution)/shard_map/ppermute | solution.py:399
  12.0 11.2 %collective-permute-start.4 = (bf16[256,512]{1,0:T(8,128)(2,1)S(1)}, bf16[256,512]{1,0:T(8,128)(2,1)S(1)}, u32[]{:S(2)}, u32[]{:S(2)}) collective-permute-start(bf16[256,512]{1,0:T(8,128)(2,1)S(1)} %get-tuple-element.45.refs_2_), channel_id=1, source_target_pairs={{0,8},{8,16},{16,24},{24,28},{28,20},{20,12},{12,4},{4,0},{1,9},{9... | collective-permute-start | bytes 786440 | tf_op jit(solution)/shard_map/ppermute | solution.py:399
  16.2 11.2 %collective-permute-start.7 = (bf16[256,512]{1,0:T(8,128)(2,1)S(1)}, bf16[256,512]{1,0:T(8,128)(2,1)S(1)}, u32[]{:S(2)}, u32[]{:S(2)}) collective-permute-start(bf16[256,512]{1,0:T(8,128)(2,1)S(1)} %get-tuple-element.45.refs_2_), channel_id=1, source_target_pairs={{8,0},{16,8},{24,16},{28,24},{20,28},{12,20},{4,12},{0,4},{9,1},{1... | collective-permute-start | bytes 786440 | tf_op jit(solution)/shard_map/ppermute | solution.py:399
  17.6 11.2 %collective-permute-start.8 = (bf16[256,512]{1,0:T(8,128)(2,1)S(1)}, bf16[256,512]{1,0:T(8,128)(2,1)S(1)}, u32[]{:S(2)}, u32[]{:S(2)}) collective-permute-start(bf16[256,512]{1,0:T(8,128)(2,1)S(1)} %collective-permute-done.2.refs_3_), channel_id=1, source_target_pairs={{0,8},{8,16},{16,24},{24,28},{28,20},{20,12},{12,4},{4,0},{1,9},{9... | collective-permute-start | bytes 786440 | tf_op jit(solution)/shard_map/ppermute | solution.py:399
  21.8 11.2 %collective-permute-start.11 = (bf16[256,512]{1,0:T(8,128)(2,1)S(1)}, bf16[256,512]{1,0:T(8,128)(2,1)S(1)}, u32[]{:S(2)}, u32[]{:S(2)}) collective-permute-start(bf16[256,512]{1,0:T(8,128)(2,1)S(1)} %collective-permute-done.5.refs_6_), channel_id=1, source_target_pairs={{8,0},{16,8},{24,16},{28,24},{20,28},{12,20},{4,12},{0,4},{9,1},{1... | collective-permute-start | bytes 786440 | tf_op jit(solution)/shard_map/ppermute | solution.py:399
  23.3 11.2 %collective-permute-start.9 = (bf16[256,512]{1,0:T(8,128)(2,1)S(1)}, bf16[256,512]{1,0:T(8,128)(2,1)S(1)}, u32[]{:S(2)}, u32[]{:S(2)}) collective-permute-start(bf16[256,512]{1,0:T(8,128)(2,1)S(1)} %collective-permute-done.3.refs_4_), channel_id=1, source_target_pairs={{0,8},{8,16},{16,24},{24,28},{28,20},{20,12},{12,4},{4,0},{1,9},{9... | collective-permute-start | bytes 786440 | tf_op jit(solution)/shard_map/ppermute | solution.py:399
  25.5 44.8 %collective-permute-start.1 = (bf16[2,128,2048]{2,1,0:T(8,128)(2,1)S(1)}, bf16[2,128,2048]{2,1,0:T(8,128)(2,1)S(1)}, u32[]{:S(2)}, u32[]{:S(2)}) collective-permute-start(bf16[2,128,2048]{2,1,0:T(8,128)(2,1)S(1)} %pad_maximum_fusion.own_ref), channel_id=1, source_target_pairs={{0,1},{1,0},{2,3},{3,2},{4,5},{5,4},{6,7},{7,6},{8,9},{9,8},{10,11... | collective-permute-start | bytes 3145736 | tf_op jit(solution)/shard_map/ppermute | solution.py:384
  27.4 11.2 %collective-permute-start.12 = (bf16[256,512]{1,0:T(8,128)(2,1)S(1)}, bf16[256,512]{1,0:T(8,128)(2,1)S(1)}, u32[]{:S(2)}, u32[]{:S(2)}) collective-permute-start(bf16[256,512]{1,0:T(8,128)(2,1)S(1)} %collective-permute-done.6.refs_7_), channel_id=1, source_target_pairs={{8,0},{16,8},{24,16},{28,24},{20,28},{12,20},{4,12},{0,4},{9,1},{1... | collective-permute-start | bytes 786440 | tf_op jit(solution)/shard_map/ppermute | solution.py:399
  28.9 11.2 %collective-permute-start.10 = (bf16[256,512]{1,0:T(8,128)(2,1)S(1)}, bf16[256,512]{1,0:T(8,128)(2,1)S(1)}, u32[]{:S(2)}, u32[]{:S(2)}) collective-permute-start(bf16[256,512]{1,0:T(8,128)(2,1)S(1)} %collective-permute-done.4.refs_5_), channel_id=1, source_target_pairs={{0,8},{8,16},{16,24},{24,28},{28,20},{20,12},{12,4},{4,0},{1,9},{9... | collective-permute-start | bytes 786440 | tf_op jit(solution)/shard_map/ppermute | solution.py:399
  33.0 11.2 %collective-permute-start.13 = (bf16[256,512]{1,0:T(8,128)(2,1)S(1)}, bf16[256,512]{1,0:T(8,128)(2,1)S(1)}, u32[]{:S(2)}, u32[]{:S(2)}) collective-permute-start(bf16[256,512]{1,0:T(8,128)(2,1)S(1)} %collective-permute-done.7.refs_8_), channel_id=1, source_target_pairs={{8,0},{16,8},{24,16},{28,24},{20,28},{12,20},{4,12},{0,4},{9,1},{1... | collective-permute-start | bytes 786440 | tf_op jit(solution)/shard_map/ppermute | solution.py:399
  34.5 11.2 %collective-permute-start.14 = (bf16[256,512]{1,0:T(8,128)(2,1)S(1)}, bf16[256,512]{1,0:T(8,128)(2,1)S(1)}, u32[]{:S(2)}, u32[]{:S(2)}) collective-permute-start(bf16[256,512]{1,0:T(8,128)(2,1)S(1)} %collective-permute-done.8.refs_9_), channel_id=1, source_target_pairs={{0,8},{8,16},{16,24},{24,28},{28,20},{20,12},{12,4},{4,0},{1,9},{9... | collective-permute-start | bytes 786440 | tf_op jit(solution)/shard_map/ppermute | solution.py:399
  38.7 11.2 %collective-permute-start.15 = (bf16[256,512]{1,0:T(8,128)(2,1)S(1)}, bf16[256,512]{1,0:T(8,128)(2,1)S(1)}, u32[]{:S(2)}, u32[]{:S(2)}) collective-permute-start(bf16[256,512]{1,0:T(8,128)(2,1)S(1)} %collective-permute-done.11.refs_12_), channel_id=1, source_target_pairs={{8,0},{16,8},{24,16},{28,24},{20,28},{12,20},{4,12},{0,4},{9,1},{1... | collective-permute-start | bytes 786440 | tf_op jit(solution)/shard_map/ppermute | solution.py:399
  40.1 11.2 %collective-permute-start.18 = (bf16[256,512]{1,0:T(8,128)(2,1)S(1)}, bf16[256,512]{1,0:T(8,128)(2,1)S(1)}, u32[]{:S(2)}, u32[]{:S(2)}) collective-permute-start(bf16[256,512]{1,0:T(8,128)(2,1)S(1)} %collective-permute-done.9.refs_10_), channel_id=1, source_target_pairs={{0,8},{8,16},{16,24},{24,28},{28,20},{20,12},{12,4},{4,0},{1,9},{9... | collective-permute-start | bytes 786440 | tf_op jit(solution)/shard_map/ppermute | solution.py:399
  44.3 11.2 %collective-permute-start.19 = (bf16[256,512]{1,0:T(8,128)(2,1)S(1)}, bf16[256,512]{1,0:T(8,128)(2,1)S(1)}, u32[]{:S(2)}, u32[]{:S(2)}) collective-permute-start(bf16[256,512]{1,0:T(8,128)(2,1)S(1)} %collective-permute-done.12.refs_13_), channel_id=1, source_target_pairs={{8,0},{16,8},{24,16},{28,24},{20,28},{12,20},{4,12},{0,4},{9,1},{1... | collective-permute-start | bytes 786440 | tf_op jit(solution)/shard_map/ppermute | solution.py:399
  45.7 11.2 %collective-permute-start.16 = (bf16[256,512]{1,0:T(8,128)(2,1)S(1)}, bf16[256,512]{1,0:T(8,128)(2,1)S(1)}, u32[]{:S(2)}, u32[]{:S(2)}) collective-permute-start(bf16[256,512]{1,0:T(8,128)(2,1)S(1)} %collective-permute-done.10.refs_11_), channel_id=1, source_target_pairs={{0,8},{8,16},{16,24},{24,28},{28,20},{20,12},{12,4},{4,0},{1,9},{9... | collective-permute-start | bytes 786440 | tf_op jit(solution)/shard_map/ppermute | solution.py:399
  49.9 11.2 %collective-permute-start.20 = (bf16[256,512]{1,0:T(8,128)(2,1)S(1)}, bf16[256,512]{1,0:T(8,128)(2,1)S(1)}, u32[]{:S(2)}, u32[]{:S(2)}) collective-permute-start(bf16[256,512]{1,0:T(8,128)(2,1)S(1)} %collective-permute-done.13.refs_14_), channel_id=1, source_target_pairs={{8,0},{16,8},{24,16},{28,24},{20,28},{12,20},{4,12},{0,4},{9,1},{1... | collective-permute-start | bytes 786440 | tf_op jit(solution)/shard_map/ppermute | solution.py:399
  55.5 11.2 %collective-permute-start.25 = (bf16[512,256]{1,0:T(8,128)(2,1)S(1)}, bf16[512,256]{1,0:T(8,128)(2,1)S(1)}, u32[]{:S(2)}, u32[]{:S(2)}) collective-permute-start(bf16[512,256]{1,0:T(8,128)(2,1)S(1)} %copy-done.3), channel_id=1, source_target_pairs={{8,0},{16,8},{24,16},{28,24},{20,28},{12,20},{4,12},{0,4},{9,1},{1... | collective-permute-start | bytes 786440 | tf_op jit(solution)/shard_map/ppermute | solution.py:399
  57.0 11.4 %collective-permute-start.17 = (bf16[256,512]{1,0:T(8,128)(2,1)S(1)}, bf16[256,512]{1,0:T(8,128)(2,1)S(1)}, u32[]{:S(2)}, u32[]{:S(2)}) collective-permute-start(bf16[256,512]{1,0:T(8,128)(2,1)S(1)} %collective-permute-done.14.refs_0_), channel_id=1, source_target_pairs={{0,8},{8,16},{16,24},{24,28},{28,20},{20,12},{12,4},{4,0},{1,9},{9... | collective-permute-start | bytes 786440 | tf_op jit(solution)/shard_map/ppermute | solution.py:399
  61.1 12.3 %collective-permute-start.21 = (bf16[256,512]{1,0:T(8,128)(2,1)S(1)}, bf16[256,512]{1,0:T(8,128)(2,1)S(1)}, u32[]{:S(2)}, u32[]{:S(2)}) collective-permute-start(bf16[256,512]{1,0:T(8,128)(2,1)S(1)} %collective-permute-done.19.refs_4_), channel_id=1, source_target_pairs={{8,0},{16,8},{24,16},{28,24},{20,28},{12,20},{4,12},{0,4},{9,1},{1... | collective-permute-start | bytes 786440 | tf_op jit(solution)/shard_map/ppermute | solution.py:399
  62.6 12.3 %collective-permute-start.23 = (bf16[256,512]{1,0:T(8,128)(2,1)S(1)}, bf16[256,512]{1,0:T(8,128)(2,1)S(1)}, u32[]{:S(2)}, u32[]{:S(2)}) collective-permute-start(bf16[256,512]{1,0:T(8,128)(2,1)S(1)} %collective-permute-done.16.refs_0_), channel_id=1, source_target_pairs={{0,8},{8,16},{16,24},{24,28},{28,20},{20,12},{12,4},{4,0},{1,9},{9... | collective-permute-start | bytes 786440 | tf_op jit(solution)/shard_map/ppermute | solution.py:399
  66.8 15.3 %collective-permute-start.26 = (bf16[512,256]{1,0:T(8,128)(2,1)S(1)}, bf16[512,256]{1,0:T(8,128)(2,1)S(1)}, u32[]{:S(2)}, u32[]{:S(2)}) collective-permute-start(bf16[512,256]{1,0:T(8,128)(2,1)S(1)} %collective-permute-done.22.refs_1_), channel_id=1, source_target_pairs={{0,8},{8,16},{16,24},{24,28},{28,20},{20,12},{12,4},{4,0},{1,9},{9... | collective-permute-start | bytes 786440 | tf_op jit(solution)/shard_map/ppermute | solution.py:399
  68.3 13.7 %collective-permute-start.27 = (bf16[512,256]{1,0:T(8,128)(2,1)S(1)}, bf16[512,256]{1,0:T(8,128)(2,1)S(1)}, u32[]{:S(2)}, u32[]{:S(2)}) collective-permute-start(bf16[512,256]{1,0:T(8,128)(2,1)S(1)} %collective-permute-done.25.refs_2_), channel_id=1, source_target_pairs={{8,0},{16,8},{24,16},{28,24},{20,28},{12,20},{4,12},{0,4},{9,1},{1... | collective-permute-start | bytes 786440 | tf_op jit(solution)/shard_map/ppermute | solution.py:399
  83.0 16.9 %collective-permute-start.32 = (bf16[512,256]{1,0:T(8,128)(2,1)S(1)}, bf16[512,256]{1,0:T(8,128)(2,1)S(1)}, u32[]{:S(2)}, u32[]{:S(2)}) collective-permute-start(bf16[512,256]{1,0:T(8,128)(2,1)S(1)} %collective-permute-done.26.refs_3_), channel_id=1, source_target_pairs={{0,8},{8,16},{16,24},{24,28},{28,20},{20,12},{12,4},{4,0},{1,9},{9... | collective-permute-start | bytes 786440 | tf_op jit(solution)/shard_map/ppermute | solution.py:399
  (21 other events, 265.0 us)

commit v5 on v4

--- a/solution.py
+++ b/solution.py
@@ -429,7 +429,9 @@
         move("k", 1)
         move("v", 0)
         for _ in range(1, steps - 1):
-            both("o")
+            move("o", 1)
+            move("o", 0)
+            came["o"][-2:] = came["o"][:-3:-1]
         move("o", 1)
 
         qkv, blocks = [came[name] for name in "qkv"], [[block] for block in came["o"]]
@@ -463,8 +465,8 @@
         means = gather(means, bits[0])
         cut = min(5, len(blocks) - 1)
         near, last = [block for (block,) in blocks[cut:-1]], blocks[-1][0]
-        *early, crossed = reduce_all(*out_call(after(mixed, seen[0]), blocks[:cut]), BF16)
-        waits = {2: (early[1],)}
+        *early, crossed = reduce_all(*out_call(mixed, blocks[:cut]), BF16)
+        waits = {1: (crossed,), 2: (early[1], *near)}
         for i, bit in enumerate(bits[1:], 1):
             means = gather(means, bit, *waits.get(i, ()))
 

time: 112 us -> 110 us (0.982)
  waiting for transfers between devices: 48.3 us -> 46.3 us
    ppermute x3, waiting for transfers between devices: 5.83 us -> 3.37 us  [over_fsdp(): return lax.ppermute(value, 'fsdp', [(i, i ^ bit) for i in range(fsdp)])]
    ppermute x3, starting transfers between devices: 4.82 us -> 5.97 us  [over_fsdp(): return lax.ppermute(value, 'fsdp', [(i, i ^ bit) for i in range(fsdp)])]
where the time goes in v5:
time: 110 us
  starting transfers between devices  49 us (45%)
  waiting for transfers between devices  46.3 us (42%)
  Pallas kernels  11.9 us (11%)
  local copies, waits for them, and re-layouts  1.42 us (1%)
    ppermute x28, waiting for transfers between devices, move(): value = lax.ppermute(value, 'fsdp', backward if way else forward)  37.5 us
    ppermute x28, starting transfers between devices, move(): value = lax.ppermute(value, 'fsdp', backward if way else forward)  36.5 us
    ppermute x8, starting transfers between devices, over_seq(): return lax.ppermute(value, 'seq', [(i, i ^ bit) for i in range(seq)])  6.5 us
    ppermute x3, starting transfers between devices, over_fsdp(): return lax.ppermute(value, 'fsdp', [(i, i ^ bit) for i in range(fsdp)])  5.97 us
    ppermute x8, waiting for transfers between devices, over_seq(): return lax.ppermute(value, 'seq', [(i, i ^ bit) for i in range(seq)])  5.46 us
    ppermute x3, waiting for transfers between devices, over_fsdp(): return lax.ppermute(value, 'fsdp', [(i, i ^ bit) for i in range(fsdp)])  3.37 us
    pallas_call x1, Pallas kernels, early_call(): pl.pallas_call(functools.partial(early_kernel, tensors), out_shape=jax.Sh...  3.15 us
    pallas_call x1, Pallas kernels, attend_call(): pl.pallas_call(functools.partial(attend_kernel, first, slots), out_shape=...  2.5 us
  transfers between devices with their start and end apart: 39, of which 28 were waited for; matrix products, arithmetic and copies ran while one was open for 1% of the time, Pallas kernels for 9%

profile of v5, /device:TPU:0, one launch (start us, length us, event | category | flops | bytes accessed | tf_op | source)
XLA Modules:
  0.0 110.3 jit_solution(5779046434977089173)
XLA Ops:
  1.9 3.1 %collective-permute-start.2 = (bf16[256,512]{1,0:T(8,128)(2,1)S(1)}, bf16[256,512]{1,0:T(8,128)(2,1)S(1)}, u32[]{:S(2)}, u32[]{:S(2)}) collective-permute-start(bf16[256,512]{1,0:T(8,128)(2,1)S(1)} %get-tuple-element.84.refs_0_), channel_id=1, source_target_pairs={{0,8},{8,16},{16,24},{24,28},{28,20},{20,12},{12,4},{4,0},{1,9},{9... | collective-permute-start | bytes 786440 | tf_op jit(solution)/shard_map/ppermute | solution.py:399
  9.4 2.6 %collective-permute-done.2.refs_3_ = bf16[256,512]{1,0:T(8,128)(2,1)S(1)} collective-permute-done((bf16[256,512]{1,0:T(8,128)(2,1)S(1)}, bf16[256,512]{1,0:T(8,128)(2,1)S(1)}, u32[]{:S(2)}, u32[]{:S(2)}) %collective-permute-start.2) | collective-permute-done | bytes 262176 | tf_op jit(solution)/shard_map/ppermute | solution.py:399
  12.0 2.1 %collective-permute-start.4 = (bf16[256,512]{1,0:T(8,128)(2,1)S(1)}, bf16[256,512]{1,0:T(8,128)(2,1)S(1)}, u32[]{:S(2)}, u32[]{:S(2)}) collective-permute-start(bf16[256,512]{1,0:T(8,128)(2,1)S(1)} %get-tuple-element.45.refs_2_), channel_id=1, source_target_pairs={{0,8},{8,16},{16,24},{24,28},{28,20},{20,12},{12,4},{4,0},{1,9},{9... | collective-permute-start | bytes 786440 | tf_op jit(solution)/shard_map/ppermute | solution.py:399
  17.6 2.1 %collective-permute-start.8 = (bf16[256,512]{1,0:T(8,128)(2,1)S(1)}, bf16[256,512]{1,0:T(8,128)(2,1)S(1)}, u32[]{:S(2)}, u32[]{:S(2)}) collective-permute-start(bf16[256,512]{1,0:T(8,128)(2,1)S(1)} %collective-permute-done.2.refs_3_), channel_id=1, source_target_pairs={{0,8},{8,16},{16,24},{24,28},{28,20},{20,12},{12,4},{4,0},{1,9},{9... | collective-permute-start | bytes 786440 | tf_op jit(solution)/shard_map/ppermute | solution.py:399
  19.8 2.1 %collective-permute-done.6.refs_7_ = bf16[256,512]{1,0:T(8,128)(2,1)S(1)} collective-permute-done((bf16[256,512]{1,0:T(8,128)(2,1)S(1)}, bf16[256,512]{1,0:T(8,128)(2,1)S(1)}, u32[]{:S(2)}, u32[]{:S(2)}) %collective-permute-start.6) | collective-permute-done | bytes 262176 | tf_op jit(solution)/shard_map/ppermute | solution.py:399
  23.3 2.1 %collective-permute-start.9 = (bf16[256,512]{1,0:T(8,128)(2,1)S(1)}, bf16[256,512]{1,0:T(8,128)(2,1)S(1)}, u32[]{:S(2)}, u32[]{:S(2)}) collective-permute-start(bf16[256,512]{1,0:T(8,128)(2,1)S(1)} %collective-permute-done.3.refs_4_), channel_id=1, source_target_pairs={{0,8},{8,16},{16,24},{24,28},{28,20},{20,12},{12,4},{4,0},{1,9},{9... | collective-permute-start | bytes 786440 | tf_op jit(solution)/shard_map/ppermute | solution.py:399
  28.9 2.1 %collective-permute-start.10 = (bf16[256,512]{1,0:T(8,128)(2,1)S(1)}, bf16[256,512]{1,0:T(8,128)(2,1)S(1)}, u32[]{:S(2)}, u32[]{:S(2)}) collective-permute-start(bf16[256,512]{1,0:T(8,128)(2,1)S(1)} %collective-permute-done.4.refs_5_), channel_id=1, source_target_pairs={{0,8},{8,16},{16,24},{24,28},{28,20},{20,12},{12,4},{4,0},{1,9},{9... | collective-permute-start | bytes 786440 | tf_op jit(solution)/shard_map/ppermute | solution.py:399
  31.0 2.1 %collective-permute-done.11.refs_12_ = bf16[256,512]{1,0:T(8,128)(2,1)S(1)} collective-permute-done((bf16[256,512]{1,0:T(8,128)(2,1)S(1)}, bf16[256,512]{1,0:T(8,128)(2,1)S(1)}, u32[]{:S(2)}, u32[]{:S(2)}) %collective-permute-start.11) | collective-permute-done | bytes 262176 | tf_op jit(solution)/shard_map/ppermute | solution.py:399
  34.5 2.1 %collective-permute-start.14 = (bf16[256,512]{1,0:T(8,128)(2,1)S(1)}, bf16[256,512]{1,0:T(8,128)(2,1)S(1)}, u32[]{:S(2)}, u32[]{:S(2)}) collective-permute-start(bf16[256,512]{1,0:T(8,128)(2,1)S(1)} %collective-permute-done.8.refs_9_), channel_id=1, source_target_pairs={{0,8},{8,16},{16,24},{24,28},{28,20},{20,12},{12,4},{4,0},{1,9},{9... | collective-permute-start | bytes 786440 | tf_op jit(solution)/shard_map/ppermute | solution.py:399
  36.6 2.1 %collective-permute-done.12.refs_13_ = bf16[256,512]{1,0:T(8,128)(2,1)S(1)} collective-permute-done((bf16[256,512]{1,0:T(8,128)(2,1)S(1)}, bf16[256,512]{1,0:T(8,128)(2,1)S(1)}, u32[]{:S(2)}, u32[]{:S(2)}) %collective-permute-start.12) | collective-permute-done | bytes 262176 | tf_op jit(solution)/shard_map/ppermute | solution.py:399
  40.1 2.1 %collective-permute-start.18 = (bf16[256,512]{1,0:T(8,128)(2,1)S(1)}, bf16[256,512]{1,0:T(8,128)(2,1)S(1)}, u32[]{:S(2)}, u32[]{:S(2)}) collective-permute-start(bf16[256,512]{1,0:T(8,128)(2,1)S(1)} %collective-permute-done.9.refs_10_), channel_id=1, source_target_pairs={{0,8},{8,16},{16,24},{24,28},{28,20},{20,12},{12,4},{4,0},{1,9},{9... | collective-permute-start | bytes 786440 | tf_op jit(solution)/shard_map/ppermute | solution.py:399
  45.7 2.1 %collective-permute-start.16 = (bf16[256,512]{1,0:T(8,128)(2,1)S(1)}, bf16[256,512]{1,0:T(8,128)(2,1)S(1)}, u32[]{:S(2)}, u32[]{:S(2)}) collective-permute-start(bf16[256,512]{1,0:T(8,128)(2,1)S(1)} %collective-permute-done.10.refs_11_), channel_id=1, source_target_pairs={{0,8},{8,16},{16,24},{24,28},{28,20},{20,12},{12,4},{4,0},{1,9},{9... | collective-permute-start | bytes 786440 | tf_op jit(solution)/shard_map/ppermute | solution.py:399
  47.9 2.1 %collective-permute-done.15.refs_1_ = bf16[256,512]{1,0:T(8,128)(2,1)S(1)} collective-permute-done((bf16[256,512]{1,0:T(8,128)(2,1)S(1)}, bf16[256,512]{1,0:T(8,128)(2,1)S(1)}, u32[]{:S(2)}, u32[]{:S(2)}) %collective-permute-start.15) | collective-permute-done | bytes 262176 | tf_op jit(solution)/shard_map/ppermute | solution.py:399
  51.4 2.1 %collective-permute-start.22 = (bf16[512,256]{1,0:T(8,128)(2,1)S(1)}, bf16[512,256]{1,0:T(8,128)(2,1)S(1)}, u32[]{:S(2)}, u32[]{:S(2)}) collective-permute-start(bf16[512,256]{1,0:T(8,128)(2,1)S(1)} %copy-done.3), channel_id=1, source_target_pairs={{0,8},{8,16},{16,24},{24,28},{28,20},{20,12},{12,4},{4,0},{1,9},{9... | collective-permute-start | bytes 786440 | tf_op jit(solution)/shard_map/ppermute | solution.py:399
  57.0 2.1 %collective-permute-start.17 = (bf16[256,512]{1,0:T(8,128)(2,1)S(1)}, bf16[256,512]{1,0:T(8,128)(2,1)S(1)}, u32[]{:S(2)}, u32[]{:S(2)}) collective-permute-start(bf16[256,512]{1,0:T(8,128)(2,1)S(1)} %collective-permute-done.14.refs_0_), channel_id=1, source_target_pairs={{0,8},{8,16},{16,24},{24,28},{28,20},{20,12},{12,4},{4,0},{1,9},{9... | collective-permute-start | bytes 786440 | tf_op jit(solution)/shard_map/ppermute | solution.py:399
  62.6 2.1 %collective-permute-start.23 = (bf16[256,512]{1,0:T(8,128)(2,1)S(1)}, bf16[256,512]{1,0:T(8,128)(2,1)S(1)}, u32[]{:S(2)}, u32[]{:S(2)}) collective-permute-start(bf16[256,512]{1,0:T(8,128)(2,1)S(1)} %collective-permute-done.16.refs_0_), channel_id=1, source_target_pairs={{0,8},{8,16},{16,24},{24,28},{28,20},{20,12},{12,4},{4,0},{1,9},{9... | collective-permute-start | bytes 786440 | tf_op jit(solution)/shard_map/ppermute | solution.py:399
  64.7 2.1 %collective-permute-done.24.refs_2_ = bf16[512,256]{1,0:T(8,128)(2,1)S(1)} collective-permute-done((bf16[512,256]{1,0:T(8,128)(2,1)S(1)}, bf16[512,256]{1,0:T(8,128)(2,1)S(1)}, u32[]{:S(2)}, u32[]{:S(2)}) %collective-permute-start.24) | collective-permute-done | bytes 262176 | tf_op jit(solution)/shard_map/ppermute | solution.py:399
  68.2 2.1 %collective-permute-start.25 = (bf16[512,256]{1,0:T(8,128)(2,1)S(1)}, bf16[512,256]{1,0:T(8,128)(2,1)S(1)}, u32[]{:S(2)}, u32[]{:S(2)}) collective-permute-start(bf16[512,256]{1,0:T(8,128)(2,1)S(1)} %collective-permute-done.22.refs_1_), channel_id=1, source_target_pairs={{0,8},{8,16},{16,24},{24,28},{28,20},{20,12},{12,4},{4,0},{1,9},{9... | collective-permute-start | bytes 786440 | tf_op jit(solution)/shard_map/ppermute | solution.py:399
  70.3 3.2 %early.1.part_ref = f32[3,512,512]{2,1,0:T(8,128)S(1)} custom-call(bf16[2,128,2048]{2,1,0:T(8,128)(2,1)S(1)} %pad_maximum_fusion.own_ref, bf16[2,128,2048]{2,1,0:T(8,128)(2,1)S(1)} %collective-permute-done.1.core_ref, bf16[256,512]{1,0:T(8,128)(2,1)S(1)} %get-tuple-element.84.refs_0_, bf16[256,512]{1,0:T(8,128)(2,1)S(1)} %get-tuple-element.83.refs_1_, ...), custom_call_target="tpu_custom_call" | custom-call | flops 2013265920 | bytes 3932160 | tf_op jit(solution)/shard_map/early/pallas_call | solution.py:135
  74.9 2.5 %attend.1 = (bf16[512,512]{1,0:T(8,128)(2,1)S(1)}, f32[1,8,512]{2,1,0:T(8,128)S(1)}) custom-call(s32[4]{0:T(128)S(1)} %bitcast.19, f32[4,512]{1,0:T(4,128)S(1)} %get-tuple-element.42.mean_ref, bf16[2,128,2048]{2,1,0:T(8,128)(2,1)S(1)} %pad_maximum_fusion.own_ref, bf16[2,128,2048]{2,1,0:T(8,128)(2,1)S(1)} %collective-permute-done.1.core_ref, ...), custom_call_target="tpu_custom_call" | custom-call | flops 1610612736 | bytes 2097152 | tf_op jit(solution)/shard_map/attend/pallas_call | solution.py:211
  79.5 2.9 %collective-permute-start.29 = (f32[1,8,512]{2,1,0:T(8,128)S(1)}, f32[1,8,512]{2,1,0:T(8,128)S(1)}, u32[]{:S(2)}, u32[]{:S(2)}) collective-permute-start(f32[1,8,512]{2,1,0:T(8,128)S(1)} %get-tuple-element.70), channel_id=1, source_target_pairs={{0,16},{4,20},{8,24},{12,28},{16,0},{20,4},{24,8},{28,12},{1,17},{... | collective-permute-start | bytes 49160 | tf_op jit(solution)/shard_map/ppermute | solution.py:381
  87.8 3.4 %collective-permute-done.32.refs_1_.refs_6_ = bf16[512,256]{1,0:T(8,128)(2,1)S(1)} collective-permute-done((bf16[512,256]{1,0:T(8,128)(2,1)S(1)}, bf16[512,256]{1,0:T(8,128)(2,1)S(1)}, u32[]{:S(2)}, u32[]{:S(2)}) %collective-permute-start.32) | collective-permute-done | bytes 262176 | tf_op jit(solution)/shard_map/ppermute | solution.py:399
  95.4 3.4 %collective-permute-done.33 = f32[4,8,512]{2,1,0:T(8,128)S(1)} collective-permute-done((f32[4,8,512]{2,1,0:T(8,128)S(1)}, f32[4,8,512]{2,1,0:T(8,128)S(1)}, u32[]{:S(2)}, u32[]{:S(2)}) %collective-permute-start.33) | collective-permute-done | bytes 65568 | tf_op jit(solution)/shard_map/ppermute | solution.py:381
  106.7 2.5 %collective-permute-done.36.refs_3_ = bf16[128,768]{1,0:T(8,128)(2,1)S(1)} collective-permute-done((bf16[128,768]{1,0:T(8,128)(2,1)S(1)}, bf16[128,768]{1,0:T(8,128)(2,1)S(1)}, u32[]{:S(2)}, u32[]{:S(2)}) %collective-permute-start.36) | collective-permute-done | bytes 196640 | tf_op jit(solution)/shard_map/ppermute | solution.py:384
  (92 shorter events, 52.4 us)
Async XLA Ops:
  5.4 20.0 %collective-permute-start = (bf16[1,128,2048]{2,1,0:T(8,128)(2,1)S(1)}, bf16[1,128,2048]{2,1,0:T(8,128)(2,1)S(1)}, u32[]{:S(2)}, u32[]{:S(2)}) collective-permute-start(bf16[1,128,2048]{2,1,0:T(8,128)(2,1)S(1)} %bitcast.17), channel_id=1, source_target_pairs={{0,2},{1,3},{2,0},{3,1},{4,6},{5,7},{6,4},{7,5},{8,10},{9,11},{10,... | collective-permute-start | bytes 1572872 | tf_op jit(solution)/shard_map/ppermute | solution.py:384
  9.0 12.8 %collective-permute-start.6 = (bf16[256,512]{1,0:T(8,128)(2,1)S(1)}, bf16[256,512]{1,0:T(8,128)(2,1)S(1)}, u32[]{:S(2)}, u32[]{:S(2)}) collective-permute-start(bf16[256,512]{1,0:T(8,128)(2,1)S(1)} %get-tuple-element.83.refs_1_), channel_id=1, source_target_pairs={{8,0},{16,8},{24,16},{28,24},{20,28},{12,20},{4,12},{0,4},{9,1},{1... | collective-permute-start | bytes 786440 | tf_op jit(solution)/shard_map/ppermute | solution.py:399
  12.0 11.2 %collective-permute-start.4 = (bf16[256,512]{1,0:T(8,128)(2,1)S(1)}, bf16[256,512]{1,0:T(8,128)(2,1)S(1)}, u32[]{:S(2)}, u32[]{:S(2)}) collective-permute-start(bf16[256,512]{1,0:T(8,128)(2,1)S(1)} %get-tuple-element.45.refs_2_), channel_id=1, source_target_pairs={{0,8},{8,16},{16,24},{24,28},{28,20},{20,12},{12,4},{4,0},{1,9},{9... | collective-permute-start | bytes 786440 | tf_op jit(solution)/shard_map/ppermute | solution.py:399
  16.2 11.2 %collective-permute-start.7 = (bf16[256,512]{1,0:T(8,128)(2,1)S(1)}, bf16[256,512]{1,0:T(8,128)(2,1)S(1)}, u32[]{:S(2)}, u32[]{:S(2)}) collective-permute-start(bf16[256,512]{1,0:T(8,128)(2,1)S(1)} %get-tuple-element.45.refs_2_), channel_id=1, source_target_pairs={{8,0},{16,8},{24,16},{28,24},{20,28},{12,20},{4,12},{0,4},{9,1},{1... | collective-permute-start | bytes 786440 | tf_op jit(solution)/shard_map/ppermute | solution.py:399
  17.6 11.2 %collective-permute-start.8 = (bf16[256,512]{1,0:T(8,128)(2,1)S(1)}, bf16[256,512]{1,0:T(8,128)(2,1)S(1)}, u32[]{:S(2)}, u32[]{:S(2)}) collective-permute-start(bf16[256,512]{1,0:T(8,128)(2,1)S(1)} %collective-permute-done.2.refs_3_), channel_id=1, source_target_pairs={{0,8},{8,16},{16,24},{24,28},{28,20},{20,12},{12,4},{4,0},{1,9},{9... | collective-permute-start | bytes 786440 | tf_op jit(solution)/shard_map/ppermute | solution.py:399
  21.8 11.2 %collective-permute-start.11 = (bf16[256,512]{1,0:T(8,128)(2,1)S(1)}, bf16[256,512]{1,0:T(8,128)(2,1)S(1)}, u32[]{:S(2)}, u32[]{:S(2)}) collective-permute-start(bf16[256,512]{1,0:T(8,128)(2,1)S(1)} %collective-permute-done.5.refs_6_), channel_id=1, source_target_pairs={{8,0},{16,8},{24,16},{28,24},{20,28},{12,20},{4,12},{0,4},{9,1},{1... | collective-permute-start | bytes 786440 | tf_op jit(solution)/shard_map/ppermute | solution.py:399
  23.3 11.2 %collective-permute-start.9 = (bf16[256,512]{1,0:T(8,128)(2,1)S(1)}, bf16[256,512]{1,0:T(8,128)(2,1)S(1)}, u32[]{:S(2)}, u32[]{:S(2)}) collective-permute-start(bf16[256,512]{1,0:T(8,128)(2,1)S(1)} %collective-permute-done.3.refs_4_), channel_id=1, source_target_pairs={{0,8},{8,16},{16,24},{24,28},{28,20},{20,12},{12,4},{4,0},{1,9},{9... | collective-permute-start | bytes 786440 | tf_op jit(solution)/shard_map/ppermute | solution.py:399
  25.5 44.8 %collective-permute-start.1 = (bf16[2,128,2048]{2,1,0:T(8,128)(2,1)S(1)}, bf16[2,128,2048]{2,1,0:T(8,128)(2,1)S(1)}, u32[]{:S(2)}, u32[]{:S(2)}) collective-permute-start(bf16[2,128,2048]{2,1,0:T(8,128)(2,1)S(1)} %pad_maximum_fusion.own_ref), channel_id=1, source_target_pairs={{0,1},{1,0},{2,3},{3,2},{4,5},{5,4},{6,7},{7,6},{8,9},{9,8},{10,11... | collective-permute-start | bytes 3145736 | tf_op jit(solution)/shard_map/ppermute | solution.py:384
  27.4 11.2 %collective-permute-start.12 = (bf16[256,512]{1,0:T(8,128)(2,1)S(1)}, bf16[256,512]{1,0:T(8,128)(2,1)S(1)}, u32[]{:S(2)}, u32[]{:S(2)}) collective-permute-start(bf16[256,512]{1,0:T(8,128)(2,1)S(1)} %collective-permute-done.6.refs_7_), channel_id=1, source_target_pairs={{8,0},{16,8},{24,16},{28,24},{20,28},{12,20},{4,12},{0,4},{9,1},{1... | collective-permute-start | bytes 786440 | tf_op jit(solution)/shard_map/ppermute | solution.py:399
  28.9 11.2 %collective-permute-start.10 = (bf16[256,512]{1,0:T(8,128)(2,1)S(1)}, bf16[256,512]{1,0:T(8,128)(2,1)S(1)}, u32[]{:S(2)}, u32[]{:S(2)}) collective-permute-start(bf16[256,512]{1,0:T(8,128)(2,1)S(1)} %collective-permute-done.4.refs_5_), channel_id=1, source_target_pairs={{0,8},{8,16},{16,24},{24,28},{28,20},{20,12},{12,4},{4,0},{1,9},{9... | collective-permute-start | bytes 786440 | tf_op jit(solution)/shard_map/ppermute | solution.py:399
  33.0 11.2 %collective-permute-start.13 = (bf16[256,512]{1,0:T(8,128)(2,1)S(1)}, bf16[256,512]{1,0:T(8,128)(2,1)S(1)}, u32[]{:S(2)}, u32[]{:S(2)}) collective-permute-start(bf16[256,512]{1,0:T(8,128)(2,1)S(1)} %collective-permute-done.7.refs_8_), channel_id=1, source_target_pairs={{8,0},{16,8},{24,16},{28,24},{20,28},{12,20},{4,12},{0,4},{9,1},{1... | collective-permute-start | bytes 786440 | tf_op jit(solution)/shard_map/ppermute | solution.py:399
  34.5 11.2 %collective-permute-start.14 = (bf16[256,512]{1,0:T(8,128)(2,1)S(1)}, bf16[256,512]{1,0:T(8,128)(2,1)S(1)}, u32[]{:S(2)}, u32[]{:S(2)}) collective-permute-start(bf16[256,512]{1,0:T(8,128)(2,1)S(1)} %collective-permute-done.8.refs_9_), channel_id=1, source_target_pairs={{0,8},{8,16},{16,24},{24,28},{28,20},{20,12},{12,4},{4,0},{1,9},{9... | collective-permute-start | bytes 786440 | tf_op jit(solution)/shard_map/ppermute | solution.py:399
  38.7 11.2 %collective-permute-start.15 = (bf16[256,512]{1,0:T(8,128)(2,1)S(1)}, bf16[256,512]{1,0:T(8,128)(2,1)S(1)}, u32[]{:S(2)}, u32[]{:S(2)}) collective-permute-start(bf16[256,512]{1,0:T(8,128)(2,1)S(1)} %collective-permute-done.11.refs_12_), channel_id=1, source_target_pairs={{8,0},{16,8},{24,16},{28,24},{20,28},{12,20},{4,12},{0,4},{9,1},{1... | collective-permute-start | bytes 786440 | tf_op jit(solution)/shard_map/ppermute | solution.py:399
  40.1 11.2 %collective-permute-start.18 = (bf16[256,512]{1,0:T(8,128)(2,1)S(1)}, bf16[256,512]{1,0:T(8,128)(2,1)S(1)}, u32[]{:S(2)}, u32[]{:S(2)}) collective-permute-start(bf16[256,512]{1,0:T(8,128)(2,1)S(1)} %collective-permute-done.9.refs_10_), channel_id=1, source_target_pairs={{0,8},{8,16},{16,24},{24,28},{28,20},{20,12},{12,4},{4,0},{1,9},{9... | collective-permute-start | bytes 786440 | tf_op jit(solution)/shard_map/ppermute | solution.py:399
  44.3 11.2 %collective-permute-start.19 = (bf16[256,512]{1,0:T(8,128)(2,1)S(1)}, bf16[256,512]{1,0:T(8,128)(2,1)S(1)}, u32[]{:S(2)}, u32[]{:S(2)}) collective-permute-start(bf16[256,512]{1,0:T(8,128)(2,1)S(1)} %collective-permute-done.12.refs_13_), channel_id=1, source_target_pairs={{8,0},{16,8},{24,16},{28,24},{20,28},{12,20},{4,12},{0,4},{9,1},{1... | collective-permute-start | bytes 786440 | tf_op jit(solution)/shard_map/ppermute | solution.py:399
  45.7 11.2 %collective-permute-start.16 = (bf16[256,512]{1,0:T(8,128)(2,1)S(1)}, bf16[256,512]{1,0:T(8,128)(2,1)S(1)}, u32[]{:S(2)}, u32[]{:S(2)}) collective-permute-start(bf16[256,512]{1,0:T(8,128)(2,1)S(1)} %collective-permute-done.10.refs_11_), channel_id=1, source_target_pairs={{0,8},{8,16},{16,24},{24,28},{28,20},{20,12},{12,4},{4,0},{1,9},{9... | collective-permute-start | bytes 786440 | tf_op jit(solution)/shard_map/ppermute | solution.py:399
  49.9 11.2 %collective-permute-start.20 = (bf16[256,512]{1,0:T(8,128)(2,1)S(1)}, bf16[256,512]{1,0:T(8,128)(2,1)S(1)}, u32[]{:S(2)}, u32[]{:S(2)}) collective-permute-start(bf16[256,512]{1,0:T(8,128)(2,1)S(1)} %collective-permute-done.13.refs_14_), channel_id=1, source_target_pairs={{8,0},{16,8},{24,16},{28,24},{20,28},{12,20},{4,12},{0,4},{9,1},{1... | collective-permute-start | bytes 786440 | tf_op jit(solution)/shard_map/ppermute | solution.py:399
  51.4 11.2 %collective-permute-start.22 = (bf16[512,256]{1,0:T(8,128)(2,1)S(1)}, bf16[512,256]{1,0:T(8,128)(2,1)S(1)}, u32[]{:S(2)}, u32[]{:S(2)}) collective-permute-start(bf16[512,256]{1,0:T(8,128)(2,1)S(1)} %copy-done.3), channel_id=1, source_target_pairs={{0,8},{8,16},{16,24},{24,28},{28,20},{20,12},{12,4},{4,0},{1,9},{9... | collective-permute-start | bytes 786440 | tf_op jit(solution)/shard_map/ppermute | solution.py:399
  55.5 11.2 %collective-permute-start.24 = (bf16[512,256]{1,0:T(8,128)(2,1)S(1)}, bf16[512,256]{1,0:T(8,128)(2,1)S(1)}, u32[]{:S(2)}, u32[]{:S(2)}) collective-permute-start(bf16[512,256]{1,0:T(8,128)(2,1)S(1)} %copy-done.3), channel_id=1, source_target_pairs={{8,0},{16,8},{24,16},{28,24},{20,28},{12,20},{4,12},{0,4},{9,1},{1... | collective-permute-start | bytes 786440 | tf_op jit(solution)/shard_map/ppermute | solution.py:399
  57.0 11.2 %collective-permute-start.17 = (bf16[256,512]{1,0:T(8,128)(2,1)S(1)}, bf16[256,512]{1,0:T(8,128)(2,1)S(1)}, u32[]{:S(2)}, u32[]{:S(2)}) collective-permute-start(bf16[256,512]{1,0:T(8,128)(2,1)S(1)} %collective-permute-done.14.refs_0_), channel_id=1, source_target_pairs={{0,8},{8,16},{16,24},{24,28},{28,20},{20,12},{12,4},{4,0},{1,9},{9... | collective-permute-start | bytes 786440 | tf_op jit(solution)/shard_map/ppermute | solution.py:399
  61.1 12.4 %collective-permute-start.21 = (bf16[256,512]{1,0:T(8,128)(2,1)S(1)}, bf16[256,512]{1,0:T(8,128)(2,1)S(1)}, u32[]{:S(2)}, u32[]{:S(2)}) collective-permute-start(bf16[256,512]{1,0:T(8,128)(2,1)S(1)} %collective-permute-done.19.refs_4_), channel_id=1, source_target_pairs={{8,0},{16,8},{24,16},{28,24},{20,28},{12,20},{4,12},{0,4},{9,1},{1... | collective-permute-start | bytes 786440 | tf_op jit(solution)/shard_map/ppermute | solution.py:399
  62.6 12.3 %collective-permute-start.23 = (bf16[256,512]{1,0:T(8,128)(2,1)S(1)}, bf16[256,512]{1,0:T(8,128)(2,1)S(1)}, u32[]{:S(2)}, u32[]{:S(2)}) collective-permute-start(bf16[256,512]{1,0:T(8,128)(2,1)S(1)} %collective-permute-done.16.refs_0_), channel_id=1, source_target_pairs={{0,8},{8,16},{16,24},{24,28},{28,20},{20,12},{12,4},{4,0},{1,9},{9... | collective-permute-start | bytes 786440 | tf_op jit(solution)/shard_map/ppermute | solution.py:399
  66.8 10.7 %collective-permute-start.26 = (bf16[512,256]{1,0:T(8,128)(2,1)S(1)}, bf16[512,256]{1,0:T(8,128)(2,1)S(1)}, u32[]{:S(2)}, u32[]{:S(2)}) collective-permute-start(bf16[512,256]{1,0:T(8,128)(2,1)S(1)} %collective-permute-done.24.refs_2_), channel_id=1, source_target_pairs={{8,0},{16,8},{24,16},{28,24},{20,28},{12,20},{4,12},{0,4},{9,1},{1... | collective-permute-start | bytes 786440 | tf_op jit(solution)/shard_map/ppermute | solution.py:399
  68.2 10.4 %collective-permute-start.25 = (bf16[512,256]{1,0:T(8,128)(2,1)S(1)}, bf16[512,256]{1,0:T(8,128)(2,1)S(1)}, u32[]{:S(2)}, u32[]{:S(2)}) collective-permute-start(bf16[512,256]{1,0:T(8,128)(2,1)S(1)} %collective-permute-done.22.refs_1_), channel_id=1, source_target_pairs={{0,8},{8,16},{16,24},{24,28},{28,20},{20,12},{12,4},{4,0},{1,9},{9... | collective-permute-start | bytes 786440 | tf_op jit(solution)/shard_map/ppermute | solution.py:399
  (21 other events, 265.1 us)

commit v6 on v5

--- a/solution.py
+++ b/solution.py
@@ -388,7 +388,9 @@
         own_tokens = tokens.reshape(frame_rows, width)
         by_tensor = jnp.transpose(w_qkv, (1, 0, 2))
         sent = []
-        chains = {"q": by_tensor[0], "k": by_tensor[1], "v": by_tensor[2], "o": w_out}
+        first = by_tensor[0]
+        others = after(by_tensor, first)
+        chains = {"q": first, "k": others[1], "v": others[2], "o": w_out}
         edge = {name: [start, start] for name, start in chains.items()}
         came = {name: [start] for name, start in chains.items()}
 
@@ -432,7 +434,6 @@
             move("o", 1)
             move("o", 0)
             came["o"][-2:] = came["o"][:-3:-1]
-        move("o", 1)
 
         qkv, blocks = [came[name] for name in "qkv"], [[block] for block in came["o"]]
 
@@ -462,11 +463,14 @@
             windows.extend([window ^ bit for window in windows])
             return jnp.concatenate([means, seen[-1]], axis=0)
 
+        cut = min(5, len(blocks) - 1)
+        near = [block for (block,) in blocks[cut:]]
+        *early, crossed = reduce_all(*out_call(mixed, blocks[:cut]), BF16)
         means = gather(means, bits[0])
-        cut = min(5, len(blocks) - 1)
-        near, last = [block for (block,) in blocks[cut:-1]], blocks[-1][0]
-        *early, crossed = reduce_all(*out_call(mixed, blocks[:cut]), BF16)
-        waits = {1: (crossed,), 2: (early[1], *near)}
+        edge["o"][1] = after(edge["o"][1], crossed)
+        move("o", 1)
+        blocks.append([came["o"][-1]])
+        waits = {1: (crossed,), 2: (early[1],)}
         for i, bit in enumerate(bits[1:], 1):
             means = gather(means, bit, *waits.get(i, ()))
 

time: 110 us -> 110 us (level)
  starting transfers between devices: 49 us -> 43.2 us
  waiting for transfers between devices: 46.3 us -> 50.1 us
  local copies, waits for them, and re-layouts: 1.42 us -> 3.28 us
    ppermute x28, starting transfers between devices: 36.5 us -> 31.7 us  [move(): value = lax.ppermute(value, 'fsdp', backward if way else forward)]
    ppermute x28, waiting for transfers between devices: 37.5 us -> 41.3 us  [move(): value = lax.ppermute(value, 'fsdp', backward if way else forward)]
  transfers between devices with their start and end apart: 39 -> 39, of which waited for: 28 -> 27; matrix products, arithmetic and copies ran while one was open for 1% -> 2% of each run, Pallas kernels for 9% -> 9%
where the time goes in v6:
time: 110 us
  waiting for transfers between devices  50.1 us (46%)
  starting transfers between devices  43.2 us (39%)
  Pallas kernels  11.9 us (11%)
  local copies, waits for them, and re-layouts  3.28 us (3%)
    ppermute x28, waiting for transfers between devices, move(): value = lax.ppermute(value, 'fsdp', backward if way else forward)  41.3 us
    ppermute x28, starting transfers between devices, move(): value = lax.ppermute(value, 'fsdp', backward if way else forward)  31.7 us
    ppermute x8, starting transfers between devices, over_seq(): return lax.ppermute(value, 'seq', [(i, i ^ bit) for i in range(seq)])  6.5 us
    ppermute x8, waiting for transfers between devices, over_seq(): return lax.ppermute(value, 'seq', [(i, i ^ bit) for i in range(seq)])  5.24 us
    ppermute x3, starting transfers between devices, over_fsdp(): return lax.ppermute(value, 'fsdp', [(i, i ^ bit) for i in range(fsdp)])  4.96 us
    ppermute x3, waiting for transfers between devices, over_fsdp(): return lax.ppermute(value, 'fsdp', [(i, i ^ bit) for i in range(fsdp)])  3.54 us
    pallas_call x1, Pallas kernels, early_call(): pl.pallas_call(functools.partial(early_kernel, tensors), out_shape=jax.Sh...  3.15 us
    pallas_call x1, Pallas kernels, attend_call(): pl.pallas_call(functools.partial(attend_kernel, first, slots), out_shape=...  2.5 us
  transfers between devices with their start and end apart: 39, of which 27 were waited for; matrix products, arithmetic and copies ran while one was open for 2% of the time, Pallas kernels for 9%

profile of v6, /device:TPU:0, one launch (start us, length us, event | category | flops | bytes accessed | tf_op | source)
XLA Modules:
  0.0 110.0 jit_solution(4619750924969967092)
XLA Ops:
  1.6 3.1 %collective-permute-start.2 = (bf16[256,512]{1,0:T(8,128)(2,1)S(1)}, bf16[256,512]{1,0:T(8,128)(2,1)S(1)}, u32[]{:S(2)}, u32[]{:S(2)}) collective-permute-start(bf16[256,512]{1,0:T(8,128)(2,1)S(1)} %slice_bitcast_fusion.refs_0_), channel_id=1, source_target_pairs={{0,8},{8,16},{16,24},{24,28},{28,20},{20,12},{12,4},{4,0},{1,9},{9... | collective-permute-start | bytes 786440 | tf_op jit(solution)/shard_map/ppermute | solution.py:401
  9.3 1.6 %collective-permute-start.3 = (bf16[256,512]{1,0:T(8,128)(2,1)S(1)}, bf16[256,512]{1,0:T(8,128)(2,1)S(1)}, u32[]{:S(2)}, u32[]{:S(2)}) collective-permute-start(bf16[256,512]{1,0:T(8,128)(2,1)S(1)} %get-tuple-element.87.refs_1_), channel_id=1, source_target_pairs={{0,8},{8,16},{16,24},{24,28},{28,20},{20,12},{12,4},{4,0},{1,9},{9... | collective-permute-start | bytes 786440 | tf_op jit(solution)/shard_map/ppermute | solution.py:401
  11.3 1.6 %collective-permute-start.4 = (bf16[256,512]{1,0:T(8,128)(2,1)S(1)}, bf16[256,512]{1,0:T(8,128)(2,1)S(1)}, u32[]{:S(2)}, u32[]{:S(2)}) collective-permute-start(bf16[256,512]{1,0:T(8,128)(2,1)S(1)} %get-tuple-element.48.refs_2_), channel_id=1, source_target_pairs={{0,8},{8,16},{16,24},{24,28},{28,20},{20,12},{12,4},{4,0},{1,9},{9... | collective-permute-start | bytes 786440 | tf_op jit(solution)/shard_map/ppermute | solution.py:401
  12.9 4.0 %collective-permute-done.5.refs_6_ = bf16[256,512]{1,0:T(8,128)(2,1)S(1)} collective-permute-done((bf16[256,512]{1,0:T(8,128)(2,1)S(1)}, bf16[256,512]{1,0:T(8,128)(2,1)S(1)}, u32[]{:S(2)}, u32[]{:S(2)}) %collective-permute-start.5) | collective-permute-done | bytes 262176 | tf_op jit(solution)/shard_map/ppermute | solution.py:401
  18.6 1.6 %collective-permute-start.8 = (bf16[256,512]{1,0:T(8,128)(2,1)S(1)}, bf16[256,512]{1,0:T(8,128)(2,1)S(1)}, u32[]{:S(2)}, u32[]{:S(2)}) collective-permute-start(bf16[256,512]{1,0:T(8,128)(2,1)S(1)} %collective-permute-done.2.refs_3_), channel_id=1, source_target_pairs={{0,8},{8,16},{16,24},{24,28},{28,20},{20,12},{12,4},{4,0},{1,9},{9... | collective-permute-start | bytes 786440 | tf_op jit(solution)/shard_map/ppermute | solution.py:401
  20.1 2.5 %collective-permute-done.6.refs_7_ = bf16[256,512]{1,0:T(8,128)(2,1)S(1)} collective-permute-done((bf16[256,512]{1,0:T(8,128)(2,1)S(1)}, bf16[256,512]{1,0:T(8,128)(2,1)S(1)}, u32[]{:S(2)}, u32[]{:S(2)}) %collective-permute-start.6) | collective-permute-done | bytes 262176 | tf_op jit(solution)/shard_map/ppermute | solution.py:401
  24.2 1.6 %collective-permute-start.9 = (bf16[256,512]{1,0:T(8,128)(2,1)S(1)}, bf16[256,512]{1,0:T(8,128)(2,1)S(1)}, u32[]{:S(2)}, u32[]{:S(2)}) collective-permute-start(bf16[256,512]{1,0:T(8,128)(2,1)S(1)} %collective-permute-done.3.refs_4_), channel_id=1, source_target_pairs={{0,8},{8,16},{16,24},{24,28},{28,20},{20,12},{12,4},{4,0},{1,9},{9... | collective-permute-start | bytes 786440 | tf_op jit(solution)/shard_map/ppermute | solution.py:401
  25.9 2.3 %collective-permute-done.7.refs_8_ = bf16[256,512]{1,0:T(8,128)(2,1)S(1)} collective-permute-done((bf16[256,512]{1,0:T(8,128)(2,1)S(1)}, bf16[256,512]{1,0:T(8,128)(2,1)S(1)}, u32[]{:S(2)}, u32[]{:S(2)}) %collective-permute-start.7) | collective-permute-done | bytes 262176 | tf_op jit(solution)/shard_map/ppermute | solution.py:401
  31.4 2.5 %collective-permute-done.11.refs_12_ = bf16[256,512]{1,0:T(8,128)(2,1)S(1)} collective-permute-done((bf16[256,512]{1,0:T(8,128)(2,1)S(1)}, bf16[256,512]{1,0:T(8,128)(2,1)S(1)}, u32[]{:S(2)}, u32[]{:S(2)}) %collective-permute-start.11) | collective-permute-done | bytes 262176 | tf_op jit(solution)/shard_map/ppermute | solution.py:401
  35.4 1.6 %collective-permute-start.14 = (bf16[256,512]{1,0:T(8,128)(2,1)S(1)}, bf16[256,512]{1,0:T(8,128)(2,1)S(1)}, u32[]{:S(2)}, u32[]{:S(2)}) collective-permute-start(bf16[256,512]{1,0:T(8,128)(2,1)S(1)} %collective-permute-done.8.refs_9_), channel_id=1, source_target_pairs={{0,8},{8,16},{16,24},{24,28},{28,20},{20,12},{12,4},{4,0},{1,9},{9... | collective-permute-start | bytes 786440 | tf_op jit(solution)/shard_map/ppermute | solution.py:401
  37.0 2.5 %collective-permute-done.12.refs_13_ = bf16[256,512]{1,0:T(8,128)(2,1)S(1)} collective-permute-done((bf16[256,512]{1,0:T(8,128)(2,1)S(1)}, bf16[256,512]{1,0:T(8,128)(2,1)S(1)}, u32[]{:S(2)}, u32[]{:S(2)}) %collective-permute-start.12) | collective-permute-done | bytes 262176 | tf_op jit(solution)/shard_map/ppermute | solution.py:401
  41.0 1.6 %collective-permute-start.18 = (bf16[256,512]{1,0:T(8,128)(2,1)S(1)}, bf16[256,512]{1,0:T(8,128)(2,1)S(1)}, u32[]{:S(2)}, u32[]{:S(2)}) collective-permute-start(bf16[256,512]{1,0:T(8,128)(2,1)S(1)} %collective-permute-done.9.refs_10_), channel_id=1, source_target_pairs={{0,8},{8,16},{16,24},{24,28},{28,20},{20,12},{12,4},{4,0},{1,9},{9... | collective-permute-start | bytes 786440 | tf_op jit(solution)/shard_map/ppermute | solution.py:401
  42.6 2.5 %collective-permute-done.13.refs_14_ = bf16[256,512]{1,0:T(8,128)(2,1)S(1)} collective-permute-done((bf16[256,512]{1,0:T(8,128)(2,1)S(1)}, bf16[256,512]{1,0:T(8,128)(2,1)S(1)}, u32[]{:S(2)}, u32[]{:S(2)}) %collective-permute-start.13) | collective-permute-done | bytes 262176 | tf_op jit(solution)/shard_map/ppermute | solution.py:401
  48.2 2.5 %collective-permute-done.15.refs_1_ = bf16[256,512]{1,0:T(8,128)(2,1)S(1)} collective-permute-done((bf16[256,512]{1,0:T(8,128)(2,1)S(1)}, bf16[256,512]{1,0:T(8,128)(2,1)S(1)}, u32[]{:S(2)}, u32[]{:S(2)}) %collective-permute-start.15) | collective-permute-done | bytes 262176 | tf_op jit(solution)/shard_map/ppermute | solution.py:401
  52.3 1.6 %collective-permute-start.22 = (bf16[512,256]{1,0:T(8,128)(2,1)S(1)}, bf16[512,256]{1,0:T(8,128)(2,1)S(1)}, u32[]{:S(2)}, u32[]{:S(2)}) collective-permute-start(bf16[512,256]{1,0:T(8,128)(2,1)S(1)} %copy-done.4), channel_id=1, source_target_pairs={{0,8},{8,16},{16,24},{24,28},{28,20},{20,12},{12,4},{4,0},{1,9},{9... | collective-permute-start | bytes 786440 | tf_op jit(solution)/shard_map/ppermute | solution.py:401
  53.8 2.5 %collective-permute-done.19.refs_4_ = bf16[256,512]{1,0:T(8,128)(2,1)S(1)} collective-permute-done((bf16[256,512]{1,0:T(8,128)(2,1)S(1)}, bf16[256,512]{1,0:T(8,128)(2,1)S(1)}, u32[]{:S(2)}, u32[]{:S(2)}) %collective-permute-start.19) | collective-permute-done | bytes 262176 | tf_op jit(solution)/shard_map/ppermute | solution.py:401
  59.5 2.5 %collective-permute-done.20.refs_1_ = bf16[256,512]{1,0:T(8,128)(2,1)S(1)} collective-permute-done((bf16[256,512]{1,0:T(8,128)(2,1)S(1)}, bf16[256,512]{1,0:T(8,128)(2,1)S(1)}, u32[]{:S(2)}, u32[]{:S(2)}) %collective-permute-start.20) | collective-permute-done | bytes 262176 | tf_op jit(solution)/shard_map/ppermute | solution.py:401
  65.1 2.5 %collective-permute-done.24.refs_2_ = bf16[512,256]{1,0:T(8,128)(2,1)S(1)} collective-permute-done((bf16[512,256]{1,0:T(8,128)(2,1)S(1)}, bf16[512,256]{1,0:T(8,128)(2,1)S(1)}, u32[]{:S(2)}, u32[]{:S(2)}) %collective-permute-start.24) | collective-permute-done | bytes 262176 | tf_op jit(solution)/shard_map/ppermute | solution.py:401
  70.7 3.1 %early.1.part_ref = f32[3,512,512]{2,1,0:T(8,128)S(1)} custom-call(bf16[2,128,2048]{2,1,0:T(8,128)(2,1)S(1)} %pad_maximum_fusion.own_ref, bf16[2,128,2048]{2,1,0:T(8,128)(2,1)S(1)} %collective-permute-done.1.core_ref, bf16[256,512]{1,0:T(8,128)(2,1)S(1)} %slice_bitcast_fusion.refs_0_, bf16[256,512]{1,0:T(8,128)(2,1)S(1)} %get-tuple-element.87.refs_1_, ...), custom_call_target="tpu_custom_call" | custom-call | flops 2013265920 | bytes 3932160 | tf_op jit(solution)/shard_map/early/pallas_call | solution.py:135
  75.3 2.5 %attend.1 = (bf16[512,512]{1,0:T(8,128)(2,1)S(1)}, f32[1,8,512]{2,1,0:T(8,128)S(1)}) custom-call(s32[4]{0:T(128)S(1)} %bitcast.19, f32[4,512]{1,0:T(4,128)S(1)} %get-tuple-element.44.mean_ref, bf16[2,128,2048]{2,1,0:T(8,128)(2,1)S(1)} %pad_maximum_fusion.own_ref, bf16[2,128,2048]{2,1,0:T(8,128)(2,1)S(1)} %collective-permute-done.1.core_ref, ...), custom_call_target="tpu_custom_call" | custom-call | flops 1610612736 | bytes 2097152 | tf_op jit(solution)/shard_map/attend/pallas_call | solution.py:211
  79.3 2.9 %collective-permute-start.29 = (f32[1,8,512]{2,1,0:T(8,128)S(1)}, f32[1,8,512]{2,1,0:T(8,128)S(1)}, u32[]{:S(2)}, u32[]{:S(2)}) collective-permute-start(f32[1,8,512]{2,1,0:T(8,128)S(1)} %get-tuple-element.73), channel_id=1, source_target_pairs={{0,16},{4,20},{8,24},{12,28},{16,0},{20,4},{24,8},{28,12},{1,17},{... | collective-permute-start | bytes 49160 | tf_op jit(solution)/shard_map/ppermute | solution.py:381
  87.4 3.5 %collective-permute-done.33.refs_1_.refs_6_ = bf16[512,256]{1,0:T(8,128)(2,1)S(1)} collective-permute-done((bf16[512,256]{1,0:T(8,128)(2,1)S(1)}, bf16[512,256]{1,0:T(8,128)(2,1)S(1)}, u32[]{:S(2)}, u32[]{:S(2)}) %collective-permute-start.33) | collective-permute-done | bytes 262176 | tf_op jit(solution)/shard_map/ppermute | solution.py:401
  95.0 3.5 %collective-permute-done.31 = f32[4,8,512]{2,1,0:T(8,128)S(1)} collective-permute-done((f32[4,8,512]{2,1,0:T(8,128)S(1)}, f32[4,8,512]{2,1,0:T(8,128)S(1)}, u32[]{:S(2)}, u32[]{:S(2)}) %collective-permute-start.31) | collective-permute-done | bytes 65568 | tf_op jit(solution)/shard_map/ppermute | solution.py:381
  106.5 2.5 %collective-permute-done.36.refs_3_ = bf16[128,768]{1,0:T(8,128)(2,1)S(1)} collective-permute-done((bf16[128,768]{1,0:T(8,128)(2,1)S(1)}, bf16[128,768]{1,0:T(8,128)(2,1)S(1)}, u32[]{:S(2)}, u32[]{:S(2)}) %collective-permute-start.36) | collective-permute-done | bytes 196640 | tf_op jit(solution)/shard_map/ppermute | solution.py:384
  (95 shorter events, 50.9 us)
Async XLA Ops:
  6.2 19.6 %collective-permute-start = (bf16[1,128,2048]{2,1,0:T(8,128)(2,1)S(1)}, bf16[1,128,2048]{2,1,0:T(8,128)(2,1)S(1)}, u32[]{:S(2)}, u32[]{:S(2)}) collective-permute-start(bf16[1,128,2048]{2,1,0:T(8,128)(2,1)S(1)} %bitcast.17), channel_id=1, source_target_pairs={{0,2},{1,3},{2,0},{3,1},{4,6},{5,7},{6,4},{7,5},{8,10},{9,11},{10,... | collective-permute-start | bytes 1572872 | tf_op jit(solution)/shard_map/ppermute | solution.py:384
  10.9 11.7 %collective-permute-start.6 = (bf16[256,512]{1,0:T(8,128)(2,1)S(1)}, bf16[256,512]{1,0:T(8,128)(2,1)S(1)}, u32[]{:S(2)}, u32[]{:S(2)}) collective-permute-start(bf16[256,512]{1,0:T(8,128)(2,1)S(1)} %get-tuple-element.87.refs_1_), channel_id=1, source_target_pairs={{8,0},{16,8},{24,16},{28,24},{20,28},{12,20},{4,12},{0,4},{9,1},{1... | collective-permute-start | bytes 786440 | tf_op jit(solution)/shard_map/ppermute | solution.py:401
  11.3 12.8 %collective-permute-start.4 = (bf16[256,512]{1,0:T(8,128)(2,1)S(1)}, bf16[256,512]{1,0:T(8,128)(2,1)S(1)}, u32[]{:S(2)}, u32[]{:S(2)}) collective-permute-start(bf16[256,512]{1,0:T(8,128)(2,1)S(1)} %get-tuple-element.48.refs_2_), channel_id=1, source_target_pairs={{0,8},{8,16},{16,24},{24,28},{28,20},{20,12},{12,4},{4,0},{1,9},{9... | collective-permute-start | bytes 786440 | tf_op jit(solution)/shard_map/ppermute | solution.py:401
  17.0 11.2 %collective-permute-start.7 = (bf16[256,512]{1,0:T(8,128)(2,1)S(1)}, bf16[256,512]{1,0:T(8,128)(2,1)S(1)}, u32[]{:S(2)}, u32[]{:S(2)}) collective-permute-start(bf16[256,512]{1,0:T(8,128)(2,1)S(1)} %get-tuple-element.48.refs_2_), channel_id=1, source_target_pairs={{8,0},{16,8},{24,16},{28,24},{20,28},{12,20},{4,12},{0,4},{9,1},{1... | collective-permute-start | bytes 786440 | tf_op jit(solution)/shard_map/ppermute | solution.py:401
  18.6 11.2 %collective-permute-start.8 = (bf16[256,512]{1,0:T(8,128)(2,1)S(1)}, bf16[256,512]{1,0:T(8,128)(2,1)S(1)}, u32[]{:S(2)}, u32[]{:S(2)}) collective-permute-start(bf16[256,512]{1,0:T(8,128)(2,1)S(1)} %collective-permute-done.2.refs_3_), channel_id=1, source_target_pairs={{0,8},{8,16},{16,24},{24,28},{28,20},{20,12},{12,4},{4,0},{1,9},{9... | collective-permute-start | bytes 786440 | tf_op jit(solution)/shard_map/ppermute | solution.py:401
  22.6 11.2 %collective-permute-start.11 = (bf16[256,512]{1,0:T(8,128)(2,1)S(1)}, bf16[256,512]{1,0:T(8,128)(2,1)S(1)}, u32[]{:S(2)}, u32[]{:S(2)}) collective-permute-start(bf16[256,512]{1,0:T(8,128)(2,1)S(1)} %collective-permute-done.5.refs_6_), channel_id=1, source_target_pairs={{8,0},{16,8},{24,16},{28,24},{20,28},{12,20},{4,12},{0,4},{9,1},{1... | collective-permute-start | bytes 786440 | tf_op jit(solution)/shard_map/ppermute | solution.py:401
  24.2 11.2 %collective-permute-start.9 = (bf16[256,512]{1,0:T(8,128)(2,1)S(1)}, bf16[256,512]{1,0:T(8,128)(2,1)S(1)}, u32[]{:S(2)}, u32[]{:S(2)}) collective-permute-start(bf16[256,512]{1,0:T(8,128)(2,1)S(1)} %collective-permute-done.3.refs_4_), channel_id=1, source_target_pairs={{0,8},{8,16},{16,24},{24,28},{28,20},{20,12},{12,4},{4,0},{1,9},{9... | collective-permute-start | bytes 786440 | tf_op jit(solution)/shard_map/ppermute | solution.py:401
  25.9 44.8 %collective-permute-start.1 = (bf16[2,128,2048]{2,1,0:T(8,128)(2,1)S(1)}, bf16[2,128,2048]{2,1,0:T(8,128)(2,1)S(1)}, u32[]{:S(2)}, u32[]{:S(2)}) collective-permute-start(bf16[2,128,2048]{2,1,0:T(8,128)(2,1)S(1)} %pad_maximum_fusion.own_ref), channel_id=1, source_target_pairs={{0,1},{1,0},{2,3},{3,2},{4,5},{5,4},{6,7},{7,6},{8,9},{9,8},{10,11... | collective-permute-start | bytes 3145736 | tf_op jit(solution)/shard_map/ppermute | solution.py:384
  28.2 11.2 %collective-permute-start.12 = (bf16[256,512]{1,0:T(8,128)(2,1)S(1)}, bf16[256,512]{1,0:T(8,128)(2,1)S(1)}, u32[]{:S(2)}, u32[]{:S(2)}) collective-permute-start(bf16[256,512]{1,0:T(8,128)(2,1)S(1)} %collective-permute-done.6.refs_7_), channel_id=1, source_target_pairs={{8,0},{16,8},{24,16},{28,24},{20,28},{12,20},{4,12},{0,4},{9,1},{1... | collective-permute-start | bytes 786440 | tf_op jit(solution)/shard_map/ppermute | solution.py:401
  29.8 11.2 %collective-permute-start.10 = (bf16[256,512]{1,0:T(8,128)(2,1)S(1)}, bf16[256,512]{1,0:T(8,128)(2,1)S(1)}, u32[]{:S(2)}, u32[]{:S(2)}) collective-permute-start(bf16[256,512]{1,0:T(8,128)(2,1)S(1)} %collective-permute-done.4.refs_5_), channel_id=1, source_target_pairs={{0,8},{8,16},{16,24},{24,28},{28,20},{20,12},{12,4},{4,0},{1,9},{9... | collective-permute-start | bytes 786440 | tf_op jit(solution)/shard_map/ppermute | solution.py:401
  33.8 11.2 %collective-permute-start.13 = (bf16[256,512]{1,0:T(8,128)(2,1)S(1)}, bf16[256,512]{1,0:T(8,128)(2,1)S(1)}, u32[]{:S(2)}, u32[]{:S(2)}) collective-permute-start(bf16[256,512]{1,0:T(8,128)(2,1)S(1)} %collective-permute-done.7.refs_8_), channel_id=1, source_target_pairs={{8,0},{16,8},{24,16},{28,24},{20,28},{12,20},{4,12},{0,4},{9,1},{1... | collective-permute-start | bytes 786440 | tf_op jit(solution)/shard_map/ppermute | solution.py:401
  35.4 11.2 %collective-permute-start.14 = (bf16[256,512]{1,0:T(8,128)(2,1)S(1)}, bf16[256,512]{1,0:T(8,128)(2,1)S(1)}, u32[]{:S(2)}, u32[]{:S(2)}) collective-permute-start(bf16[256,512]{1,0:T(8,128)(2,1)S(1)} %collective-permute-done.8.refs_9_), channel_id=1, source_target_pairs={{0,8},{8,16},{16,24},{24,28},{28,20},{20,12},{12,4},{4,0},{1,9},{9... | collective-permute-start | bytes 786440 | tf_op jit(solution)/shard_map/ppermute | solution.py:401
  39.4 11.2 %collective-permute-start.15 = (bf16[256,512]{1,0:T(8,128)(2,1)S(1)}, bf16[256,512]{1,0:T(8,128)(2,1)S(1)}, u32[]{:S(2)}, u32[]{:S(2)}) collective-permute-start(bf16[256,512]{1,0:T(8,128)(2,1)S(1)} %collective-permute-done.11.refs_12_), channel_id=1, source_target_pairs={{8,0},{16,8},{24,16},{28,24},{20,28},{12,20},{4,12},{0,4},{9,1},{1... | collective-permute-start | bytes 786440 | tf_op jit(solution)/shard_map/ppermute | solution.py:401
  41.0 11.2 %collective-permute-start.18 = (bf16[256,512]{1,0:T(8,128)(2,1)S(1)}, bf16[256,512]{1,0:T(8,128)(2,1)S(1)}, u32[]{:S(2)}, u32[]{:S(2)}) collective-permute-start(bf16[256,512]{1,0:T(8,128)(2,1)S(1)} %collective-permute-done.9.refs_10_), channel_id=1, source_target_pairs={{0,8},{8,16},{16,24},{24,28},{28,20},{20,12},{12,4},{4,0},{1,9},{9... | collective-permute-start | bytes 786440 | tf_op jit(solution)/shard_map/ppermute | solution.py:401
  45.1 11.2 %collective-permute-start.19 = (bf16[256,512]{1,0:T(8,128)(2,1)S(1)}, bf16[256,512]{1,0:T(8,128)(2,1)S(1)}, u32[]{:S(2)}, u32[]{:S(2)}) collective-permute-start(bf16[256,512]{1,0:T(8,128)(2,1)S(1)} %collective-permute-done.12.refs_13_), channel_id=1, source_target_pairs={{8,0},{16,8},{24,16},{28,24},{20,28},{12,20},{4,12},{0,4},{9,1},{1... | collective-permute-start | bytes 786440 | tf_op jit(solution)/shard_map/ppermute | solution.py:401
  46.6 11.2 %collective-permute-start.16 = (bf16[256,512]{1,0:T(8,128)(2,1)S(1)}, bf16[256,512]{1,0:T(8,128)(2,1)S(1)}, u32[]{:S(2)}, u32[]{:S(2)}) collective-permute-start(bf16[256,512]{1,0:T(8,128)(2,1)S(1)} %collective-permute-done.10.refs_11_), channel_id=1, source_target_pairs={{0,8},{8,16},{16,24},{24,28},{28,20},{20,12},{12,4},{4,0},{1,9},{9... | collective-permute-start | bytes 786440 | tf_op jit(solution)/shard_map/ppermute | solution.py:401
  50.7 11.2 %collective-permute-start.20 = (bf16[256,512]{1,0:T(8,128)(2,1)S(1)}, bf16[256,512]{1,0:T(8,128)(2,1)S(1)}, u32[]{:S(2)}, u32[]{:S(2)}) collective-permute-start(bf16[256,512]{1,0:T(8,128)(2,1)S(1)} %collective-permute-done.13.refs_14_), channel_id=1, source_target_pairs={{8,0},{16,8},{24,16},{28,24},{20,28},{12,20},{4,12},{0,4},{9,1},{1... | collective-permute-start | bytes 786440 | tf_op jit(solution)/shard_map/ppermute | solution.py:401
  52.3 11.2 %collective-permute-start.22 = (bf16[512,256]{1,0:T(8,128)(2,1)S(1)}, bf16[512,256]{1,0:T(8,128)(2,1)S(1)}, u32[]{:S(2)}, u32[]{:S(2)}) collective-permute-start(bf16[512,256]{1,0:T(8,128)(2,1)S(1)} %copy-done.4), channel_id=1, source_target_pairs={{0,8},{8,16},{16,24},{24,28},{28,20},{20,12},{12,4},{4,0},{1,9},{9... | collective-permute-start | bytes 786440 | tf_op jit(solution)/shard_map/ppermute | solution.py:401
  56.3 11.2 %collective-permute-start.24 = (bf16[512,256]{1,0:T(8,128)(2,1)S(1)}, bf16[512,256]{1,0:T(8,128)(2,1)S(1)}, u32[]{:S(2)}, u32[]{:S(2)}) collective-permute-start(bf16[512,256]{1,0:T(8,128)(2,1)S(1)} %copy-done.4), channel_id=1, source_target_pairs={{8,0},{16,8},{24,16},{28,24},{20,28},{12,20},{4,12},{0,4},{9,1},{1... | collective-permute-start | bytes 786440 | tf_op jit(solution)/shard_map/ppermute | solution.py:401
  57.9 11.2 %collective-permute-start.17 = (bf16[256,512]{1,0:T(8,128)(2,1)S(1)}, bf16[256,512]{1,0:T(8,128)(2,1)S(1)}, u32[]{:S(2)}, u32[]{:S(2)}) collective-permute-start(bf16[256,512]{1,0:T(8,128)(2,1)S(1)} %collective-permute-done.14.refs_0_), channel_id=1, source_target_pairs={{0,8},{8,16},{16,24},{24,28},{28,20},{20,12},{12,4},{4,0},{1,9},{9... | collective-permute-start | bytes 786440 | tf_op jit(solution)/shard_map/ppermute | solution.py:401
  61.9 11.9 %collective-permute-start.21 = (bf16[256,512]{1,0:T(8,128)(2,1)S(1)}, bf16[256,512]{1,0:T(8,128)(2,1)S(1)}, u32[]{:S(2)}, u32[]{:S(2)}) collective-permute-start(bf16[256,512]{1,0:T(8,128)(2,1)S(1)} %collective-permute-done.19.refs_4_), channel_id=1, source_target_pairs={{8,0},{16,8},{24,16},{28,24},{20,28},{12,20},{4,12},{0,4},{9,1},{1... | collective-permute-start | bytes 786440 | tf_op jit(solution)/shard_map/ppermute | solution.py:401
  63.5 11.8 %collective-permute-start.23 = (bf16[256,512]{1,0:T(8,128)(2,1)S(1)}, bf16[256,512]{1,0:T(8,128)(2,1)S(1)}, u32[]{:S(2)}, u32[]{:S(2)}) collective-permute-start(bf16[256,512]{1,0:T(8,128)(2,1)S(1)} %collective-permute-done.16.refs_0_), channel_id=1, source_target_pairs={{0,8},{8,16},{16,24},{24,28},{28,20},{20,12},{12,4},{4,0},{1,9},{9... | collective-permute-start | bytes 786440 | tf_op jit(solution)/shard_map/ppermute | solution.py:401
  67.5 10.3 %collective-permute-start.26 = (bf16[512,256]{1,0:T(8,128)(2,1)S(1)}, bf16[512,256]{1,0:T(8,128)(2,1)S(1)}, u32[]{:S(2)}, u32[]{:S(2)}) collective-permute-start(bf16[512,256]{1,0:T(8,128)(2,1)S(1)} %collective-permute-done.24.refs_2_), channel_id=1, source_target_pairs={{8,0},{16,8},{24,16},{28,24},{20,28},{12,20},{4,12},{0,4},{9,1},{1... | collective-permute-start | bytes 786440 | tf_op jit(solution)/shard_map/ppermute | solution.py:401
  85.9 12.6 %collective-permute-start.32 = (bf16[512,256]{1,0:T(8,128)(2,1)S(1)}, bf16[512,256]{1,0:T(8,128)(2,1)S(1)}, u32[]{:S(2)}, u32[]{:S(2)}) collective-permute-start(bf16[512,256]{1,0:T(8,128)(2,1)S(1)} %collective-permute-done.25.refs_3_), channel_id=1, source_target_pairs={{0,8},{8,16},{16,24},{24,28},{28,20},{20,12},{12,4},{4,0},{1,9},{9... | collective-permute-start | bytes 786440 | tf_op jit(solution)/shard_map/ppermute | solution.py:401
  (22 other events, 261.8 us)

commit v7 on v6

--- a/solution.py
+++ b/solution.py
@@ -474,8 +474,8 @@
         for i, bit in enumerate(bits[1:], 1):
             means = gather(means, bit, *waits.get(i, ()))
 
-        pool_keep, pool_came, _ = reduce_all(*pool_call(after(means, early[1]), blocks, seq), F32)
         later = reduce_all(*out_call(after(mixed, means), blocks[cut:]), BF16)
+        pool_keep, pool_came, _ = reduce_all(*pool_call(after(means, later[2]), blocks, seq), F32)
         sums = [early, later[:2]]
         hidden = finish_call(distances, own_tokens, sums)
 

time: 110 us -> 112 us (1.018)
  waiting for transfers between devices: 50.1 us -> 52.4 us
    ppermute x8, waiting for transfers between devices: 5.24 us -> 7.62 us  [over_seq(): return lax.ppermute(value, 'seq', [(i, i ^ bit) for i in range(seq)])]
  transfers between devices with their start and end apart: 39 -> 39, of which waited for: 27 -> 26; matrix products, arithmetic and copies ran while one was open for 2% -> 2% of each run, Pallas kernels for 9% -> 8%
where the time goes in v7:
time: 112 us
  waiting for transfers between devices  52.4 us (47%)
  starting transfers between devices  42.8 us (38%)
  Pallas kernels  11.9 us (11%)
  local copies, waits for them, and re-layouts  3.28 us (3%)
    ppermute x28, waiting for transfers between devices, move(): value = lax.ppermute(value, 'fsdp', backward if way else forward)  41.3 us
    ppermute x28, starting transfers between devices, move(): value = lax.ppermute(value, 'fsdp', backward if way else forward)  31.7 us
    ppermute x8, waiting for transfers between devices, over_seq(): return lax.ppermute(value, 'seq', [(i, i ^ bit) for i in range(seq)])  7.62 us
    ppermute x8, starting transfers between devices, over_seq(): return lax.ppermute(value, 'seq', [(i, i ^ bit) for i in range(seq)])  6.14 us
    ppermute x3, starting transfers between devices, over_fsdp(): return lax.ppermute(value, 'fsdp', [(i, i ^ bit) for i in range(fsdp)])  4.96 us
    ppermute x3, waiting for transfers between devices, over_fsdp(): return lax.ppermute(value, 'fsdp', [(i, i ^ bit) for i in range(fsdp)])  3.52 us
    pallas_call x1, Pallas kernels, early_call(): pl.pallas_call(functools.partial(early_kernel, tensors), out_shape=jax.Sh...  3.15 us
    pallas_call x1, Pallas kernels, attend_call(): pl.pallas_call(functools.partial(attend_kernel, first, slots), out_shape=...  2.5 us
  transfers between devices with their start and end apart: 39, of which 26 were waited for; matrix products, arithmetic and copies ran while one was open for 2% of the time, Pallas kernels for 8%

profile of v7, /device:TPU:0, one launch (start us, length us, event | category | flops | bytes accessed | tf_op | source)
XLA Modules:
  0.0 112.0 jit_solution(4211455441789868326)
XLA Ops:
  1.6 3.1 %collective-permute-start.2 = (bf16[256,512]{1,0:T(8,128)(2,1)S(1)}, bf16[256,512]{1,0:T(8,128)(2,1)S(1)}, u32[]{:S(2)}, u32[]{:S(2)}) collective-permute-start(bf16[256,512]{1,0:T(8,128)(2,1)S(1)} %slice_bitcast_fusion.refs_0_), channel_id=1, source_target_pairs={{0,8},{8,16},{16,24},{24,28},{28,20},{20,12},{12,4},{4,0},{1,9},{9... | collective-permute-start | bytes 786440 | tf_op jit(solution)/shard_map/ppermute | solution.py:401
  9.3 1.6 %collective-permute-start.3 = (bf16[256,512]{1,0:T(8,128)(2,1)S(1)}, bf16[256,512]{1,0:T(8,128)(2,1)S(1)}, u32[]{:S(2)}, u32[]{:S(2)}) collective-permute-start(bf16[256,512]{1,0:T(8,128)(2,1)S(1)} %get-tuple-element.87.refs_1_), channel_id=1, source_target_pairs={{0,8},{8,16},{16,24},{24,28},{28,20},{20,12},{12,4},{4,0},{1,9},{9... | collective-permute-start | bytes 786440 | tf_op jit(solution)/shard_map/ppermute | solution.py:401
  11.3 1.6 %collective-permute-start.4 = (bf16[256,512]{1,0:T(8,128)(2,1)S(1)}, bf16[256,512]{1,0:T(8,128)(2,1)S(1)}, u32[]{:S(2)}, u32[]{:S(2)}) collective-permute-start(bf16[256,512]{1,0:T(8,128)(2,1)S(1)} %get-tuple-element.48.refs_2_), channel_id=1, source_target_pairs={{0,8},{8,16},{16,24},{24,28},{28,20},{20,12},{12,4},{4,0},{1,9},{9... | collective-permute-start | bytes 786440 | tf_op jit(solution)/shard_map/ppermute | solution.py:401
  12.9 4.0 %collective-permute-done.5.refs_6_ = bf16[256,512]{1,0:T(8,128)(2,1)S(1)} collective-permute-done((bf16[256,512]{1,0:T(8,128)(2,1)S(1)}, bf16[256,512]{1,0:T(8,128)(2,1)S(1)}, u32[]{:S(2)}, u32[]{:S(2)}) %collective-permute-start.5) | collective-permute-done | bytes 262176 | tf_op jit(solution)/shard_map/ppermute | solution.py:401
  18.6 1.6 %collective-permute-start.8 = (bf16[256,512]{1,0:T(8,128)(2,1)S(1)}, bf16[256,512]{1,0:T(8,128)(2,1)S(1)}, u32[]{:S(2)}, u32[]{:S(2)}) collective-permute-start(bf16[256,512]{1,0:T(8,128)(2,1)S(1)} %collective-permute-done.2.refs_3_), channel_id=1, source_target_pairs={{0,8},{8,16},{16,24},{24,28},{28,20},{20,12},{12,4},{4,0},{1,9},{9... | collective-permute-start | bytes 786440 | tf_op jit(solution)/shard_map/ppermute | solution.py:401
  20.1 2.5 %collective-permute-done.6.refs_7_ = bf16[256,512]{1,0:T(8,128)(2,1)S(1)} collective-permute-done((bf16[256,512]{1,0:T(8,128)(2,1)S(1)}, bf16[256,512]{1,0:T(8,128)(2,1)S(1)}, u32[]{:S(2)}, u32[]{:S(2)}) %collective-permute-start.6) | collective-permute-done | bytes 262176 | tf_op jit(solution)/shard_map/ppermute | solution.py:401
  25.9 2.3 %collective-permute-done.7.refs_8_ = bf16[256,512]{1,0:T(8,128)(2,1)S(1)} collective-permute-done((bf16[256,512]{1,0:T(8,128)(2,1)S(1)}, bf16[256,512]{1,0:T(8,128)(2,1)S(1)}, u32[]{:S(2)}, u32[]{:S(2)}) %collective-permute-start.7) | collective-permute-done | bytes 262176 | tf_op jit(solution)/shard_map/ppermute | solution.py:401
  31.4 2.5 %collective-permute-done.11.refs_12_ = bf16[256,512]{1,0:T(8,128)(2,1)S(1)} collective-permute-done((bf16[256,512]{1,0:T(8,128)(2,1)S(1)}, bf16[256,512]{1,0:T(8,128)(2,1)S(1)}, u32[]{:S(2)}, u32[]{:S(2)}) %collective-permute-start.11) | collective-permute-done | bytes 262176 | tf_op jit(solution)/shard_map/ppermute | solution.py:401
  35.4 1.6 %collective-permute-start.14 = (bf16[256,512]{1,0:T(8,128)(2,1)S(1)}, bf16[256,512]{1,0:T(8,128)(2,1)S(1)}, u32[]{:S(2)}, u32[]{:S(2)}) collective-permute-start(bf16[256,512]{1,0:T(8,128)(2,1)S(1)} %collective-permute-done.8.refs_9_), channel_id=1, source_target_pairs={{0,8},{8,16},{16,24},{24,28},{28,20},{20,12},{12,4},{4,0},{1,9},{9... | collective-permute-start | bytes 786440 | tf_op jit(solution)/shard_map/ppermute | solution.py:401
  37.0 2.5 %collective-permute-done.12.refs_13_ = bf16[256,512]{1,0:T(8,128)(2,1)S(1)} collective-permute-done((bf16[256,512]{1,0:T(8,128)(2,1)S(1)}, bf16[256,512]{1,0:T(8,128)(2,1)S(1)}, u32[]{:S(2)}, u32[]{:S(2)}) %collective-permute-start.12) | collective-permute-done | bytes 262176 | tf_op jit(solution)/shard_map/ppermute | solution.py:401
  42.6 2.5 %collective-permute-done.13.refs_14_ = bf16[256,512]{1,0:T(8,128)(2,1)S(1)} collective-permute-done((bf16[256,512]{1,0:T(8,128)(2,1)S(1)}, bf16[256,512]{1,0:T(8,128)(2,1)S(1)}, u32[]{:S(2)}, u32[]{:S(2)}) %collective-permute-start.13) | collective-permute-done | bytes 262176 | tf_op jit(solution)/shard_map/ppermute | solution.py:401
  48.2 2.5 %collective-permute-done.15.refs_1_ = bf16[256,512]{1,0:T(8,128)(2,1)S(1)} collective-permute-done((bf16[256,512]{1,0:T(8,128)(2,1)S(1)}, bf16[256,512]{1,0:T(8,128)(2,1)S(1)}, u32[]{:S(2)}, u32[]{:S(2)}) %collective-permute-start.15) | collective-permute-done | bytes 262176 | tf_op jit(solution)/shard_map/ppermute | solution.py:401
  52.3 1.6 %collective-permute-start.22 = (bf16[512,256]{1,0:T(8,128)(2,1)S(1)}, bf16[512,256]{1,0:T(8,128)(2,1)S(1)}, u32[]{:S(2)}, u32[]{:S(2)}) collective-permute-start(bf16[512,256]{1,0:T(8,128)(2,1)S(1)} %copy-done.4), channel_id=1, source_target_pairs={{0,8},{8,16},{16,24},{24,28},{28,20},{20,12},{12,4},{4,0},{1,9},{9... | collective-permute-start | bytes 786440 | tf_op jit(solution)/shard_map/ppermute | solution.py:401
  53.8 2.5 %collective-permute-done.19.refs_4_ = bf16[256,512]{1,0:T(8,128)(2,1)S(1)} collective-permute-done((bf16[256,512]{1,0:T(8,128)(2,1)S(1)}, bf16[256,512]{1,0:T(8,128)(2,1)S(1)}, u32[]{:S(2)}, u32[]{:S(2)}) %collective-permute-start.19) | collective-permute-done | bytes 262176 | tf_op jit(solution)/shard_map/ppermute | solution.py:401
  59.5 2.5 %collective-permute-done.20.refs_1_ = bf16[256,512]{1,0:T(8,128)(2,1)S(1)} collective-permute-done((bf16[256,512]{1,0:T(8,128)(2,1)S(1)}, bf16[256,512]{1,0:T(8,128)(2,1)S(1)}, u32[]{:S(2)}, u32[]{:S(2)}) %collective-permute-start.20) | collective-permute-done | bytes 262176 | tf_op jit(solution)/shard_map/ppermute | solution.py:401
  63.5 1.6 %collective-permute-start.23 = (bf16[256,512]{1,0:T(8,128)(2,1)S(1)}, bf16[256,512]{1,0:T(8,128)(2,1)S(1)}, u32[]{:S(2)}, u32[]{:S(2)}) collective-permute-start(bf16[256,512]{1,0:T(8,128)(2,1)S(1)} %collective-permute-done.16.refs_0_), channel_id=1, source_target_pairs={{0,8},{8,16},{16,24},{24,28},{28,20},{20,12},{12,4},{4,0},{1,9},{9... | collective-permute-start | bytes 786440 | tf_op jit(solution)/shard_map/ppermute | solution.py:401
  65.1 2.5 %collective-permute-done.24.refs_2_ = bf16[512,256]{1,0:T(8,128)(2,1)S(1)} collective-permute-done((bf16[512,256]{1,0:T(8,128)(2,1)S(1)}, bf16[512,256]{1,0:T(8,128)(2,1)S(1)}, u32[]{:S(2)}, u32[]{:S(2)}) %collective-permute-start.24) | collective-permute-done | bytes 262176 | tf_op jit(solution)/shard_map/ppermute | solution.py:401
  70.7 3.1 %early.1.part_ref = f32[3,512,512]{2,1,0:T(8,128)S(1)} custom-call(bf16[2,128,2048]{2,1,0:T(8,128)(2,1)S(1)} %pad_maximum_fusion.own_ref, bf16[2,128,2048]{2,1,0:T(8,128)(2,1)S(1)} %collective-permute-done.1.core_ref, bf16[256,512]{1,0:T(8,128)(2,1)S(1)} %slice_bitcast_fusion.refs_0_, bf16[256,512]{1,0:T(8,128)(2,1)S(1)} %get-tuple-element.87.refs_1_, ...), custom_call_target="tpu_custom_call" | custom-call | flops 2013265920 | bytes 3932160 | tf_op jit(solution)/shard_map/early/pallas_call | solution.py:135
  75.3 2.5 %attend.1 = (bf16[512,512]{1,0:T(8,128)(2,1)S(1)}, f32[1,8,512]{2,1,0:T(8,128)S(1)}) custom-call(s32[4]{0:T(128)S(1)} %bitcast.19, f32[4,512]{1,0:T(4,128)S(1)} %get-tuple-element.44.mean_ref, bf16[2,128,2048]{2,1,0:T(8,128)(2,1)S(1)} %pad_maximum_fusion.own_ref, bf16[2,128,2048]{2,1,0:T(8,128)(2,1)S(1)} %collective-permute-done.1.core_ref, ...), custom_call_target="tpu_custom_call" | custom-call | flops 1610612736 | bytes 2097152 | tf_op jit(solution)/shard_map/attend/pallas_call | solution.py:211
  79.3 2.9 %collective-permute-start.29 = (f32[1,8,512]{2,1,0:T(8,128)S(1)}, f32[1,8,512]{2,1,0:T(8,128)S(1)}, u32[]{:S(2)}, u32[]{:S(2)}) collective-permute-start(f32[1,8,512]{2,1,0:T(8,128)S(1)} %get-tuple-element.73), channel_id=1, source_target_pairs={{0,16},{4,20},{8,24},{12,28},{16,0},{20,4},{24,8},{28,12},{1,17},{... | collective-permute-start | bytes 49160 | tf_op jit(solution)/shard_map/ppermute | solution.py:381
  87.5 3.4 %collective-permute-done.33.refs_1_.refs_6_ = bf16[512,256]{1,0:T(8,128)(2,1)S(1)} collective-permute-done((bf16[512,256]{1,0:T(8,128)(2,1)S(1)}, bf16[512,256]{1,0:T(8,128)(2,1)S(1)}, u32[]{:S(2)}, u32[]{:S(2)}) %collective-permute-start.33) | collective-permute-done | bytes 262176 | tf_op jit(solution)/shard_map/ppermute | solution.py:401
  95.0 3.5 %collective-permute-done.31 = f32[4,8,512]{2,1,0:T(8,128)S(1)} collective-permute-done((f32[4,8,512]{2,1,0:T(8,128)S(1)}, f32[4,8,512]{2,1,0:T(8,128)S(1)}, u32[]{:S(2)}, u32[]{:S(2)}) %collective-permute-start.31) | collective-permute-done | bytes 65568 | tf_op jit(solution)/shard_map/ppermute | solution.py:381
  99.2 1.7 %collective-permute-done.35 = bf16[256,768]{1,0:T(8,128)(2,1)S(1)} collective-permute-done((bf16[256,768]{1,0:T(8,128)(2,1)S(1)}, bf16[256,768]{1,0:T(8,128)(2,1)S(1)}, u32[]{:S(2)}, u32[]{:S(2)}) %collective-permute-start.35) | collective-permute-done | bytes 393248 | tf_op jit(solution)/shard_map/ppermute | solution.py:384
  104.9 4.5 %collective-permute-done.36.refs_3_ = bf16[128,768]{1,0:T(8,128)(2,1)S(1)} collective-permute-done((bf16[128,768]{1,0:T(8,128)(2,1)S(1)}, bf16[128,768]{1,0:T(8,128)(2,1)S(1)}, u32[]{:S(2)}, u32[]{:S(2)}) %collective-permute-start.36) | collective-permute-done | bytes 196640 | tf_op jit(solution)/shard_map/ppermute | solution.py:384
  (95 shorter events, 50.8 us)
Async XLA Ops:
  6.2 19.6 %collective-permute-start = (bf16[1,128,2048]{2,1,0:T(8,128)(2,1)S(1)}, bf16[1,128,2048]{2,1,0:T(8,128)(2,1)S(1)}, u32[]{:S(2)}, u32[]{:S(2)}) collective-permute-start(bf16[1,128,2048]{2,1,0:T(8,128)(2,1)S(1)} %bitcast.17), channel_id=1, source_target_pairs={{0,2},{1,3},{2,0},{3,1},{4,6},{5,7},{6,4},{7,5},{8,10},{9,11},{10,... | collective-permute-start | bytes 1572872 | tf_op jit(solution)/shard_map/ppermute | solution.py:384
  10.9 11.7 %collective-permute-start.6 = (bf16[256,512]{1,0:T(8,128)(2,1)S(1)}, bf16[256,512]{1,0:T(8,128)(2,1)S(1)}, u32[]{:S(2)}, u32[]{:S(2)}) collective-permute-start(bf16[256,512]{1,0:T(8,128)(2,1)S(1)} %get-tuple-element.87.refs_1_), channel_id=1, source_target_pairs={{8,0},{16,8},{24,16},{28,24},{20,28},{12,20},{4,12},{0,4},{9,1},{1... | collective-permute-start | bytes 786440 | tf_op jit(solution)/shard_map/ppermute | solution.py:401
  11.3 12.8 %collective-permute-start.4 = (bf16[256,512]{1,0:T(8,128)(2,1)S(1)}, bf16[256,512]{1,0:T(8,128)(2,1)S(1)}, u32[]{:S(2)}, u32[]{:S(2)}) collective-permute-start(bf16[256,512]{1,0:T(8,128)(2,1)S(1)} %get-tuple-element.48.refs_2_), channel_id=1, source_target_pairs={{0,8},{8,16},{16,24},{24,28},{28,20},{20,12},{12,4},{4,0},{1,9},{9... | collective-permute-start | bytes 786440 | tf_op jit(solution)/shard_map/ppermute | solution.py:401
  17.0 11.2 %collective-permute-start.7 = (bf16[256,512]{1,0:T(8,128)(2,1)S(1)}, bf16[256,512]{1,0:T(8,128)(2,1)S(1)}, u32[]{:S(2)}, u32[]{:S(2)}) collective-permute-start(bf16[256,512]{1,0:T(8,128)(2,1)S(1)} %get-tuple-element.48.refs_2_), channel_id=1, source_target_pairs={{8,0},{16,8},{24,16},{28,24},{20,28},{12,20},{4,12},{0,4},{9,1},{1... | collective-permute-start | bytes 786440 | tf_op jit(solution)/shard_map/ppermute | solution.py:401
  18.6 11.2 %collective-permute-start.8 = (bf16[256,512]{1,0:T(8,128)(2,1)S(1)}, bf16[256,512]{1,0:T(8,128)(2,1)S(1)}, u32[]{:S(2)}, u32[]{:S(2)}) collective-permute-start(bf16[256,512]{1,0:T(8,128)(2,1)S(1)} %collective-permute-done.2.refs_3_), channel_id=1, source_target_pairs={{0,8},{8,16},{16,24},{24,28},{28,20},{20,12},{12,4},{4,0},{1,9},{9... | collective-permute-start | bytes 786440 | tf_op jit(solution)/shard_map/ppermute | solution.py:401
  22.6 11.2 %collective-permute-start.11 = (bf16[256,512]{1,0:T(8,128)(2,1)S(1)}, bf16[256,512]{1,0:T(8,128)(2,1)S(1)}, u32[]{:S(2)}, u32[]{:S(2)}) collective-permute-start(bf16[256,512]{1,0:T(8,128)(2,1)S(1)} %collective-permute-done.5.refs_6_), channel_id=1, source_target_pairs={{8,0},{16,8},{24,16},{28,24},{20,28},{12,20},{4,12},{0,4},{9,1},{1... | collective-permute-start | bytes 786440 | tf_op jit(solution)/shard_map/ppermute | solution.py:401
  24.2 11.2 %collective-permute-start.9 = (bf16[256,512]{1,0:T(8,128)(2,1)S(1)}, bf16[256,512]{1,0:T(8,128)(2,1)S(1)}, u32[]{:S(2)}, u32[]{:S(2)}) collective-permute-start(bf16[256,512]{1,0:T(8,128)(2,1)S(1)} %collective-permute-done.3.refs_4_), channel_id=1, source_target_pairs={{0,8},{8,16},{16,24},{24,28},{28,20},{20,12},{12,4},{4,0},{1,9},{9... | collective-permute-start | bytes 786440 | tf_op jit(solution)/shard_map/ppermute | solution.py:401
  25.9 44.8 %collective-permute-start.1 = (bf16[2,128,2048]{2,1,0:T(8,128)(2,1)S(1)}, bf16[2,128,2048]{2,1,0:T(8,128)(2,1)S(1)}, u32[]{:S(2)}, u32[]{:S(2)}) collective-permute-start(bf16[2,128,2048]{2,1,0:T(8,128)(2,1)S(1)} %pad_maximum_fusion.own_ref), channel_id=1, source_target_pairs={{0,1},{1,0},{2,3},{3,2},{4,5},{5,4},{6,7},{7,6},{8,9},{9,8},{10,11... | collective-permute-start | bytes 3145736 | tf_op jit(solution)/shard_map/ppermute | solution.py:384
  28.2 11.2 %collective-permute-start.12 = (bf16[256,512]{1,0:T(8,128)(2,1)S(1)}, bf16[256,512]{1,0:T(8,128)(2,1)S(1)}, u32[]{:S(2)}, u32[]{:S(2)}) collective-permute-start(bf16[256,512]{1,0:T(8,128)(2,1)S(1)} %collective-permute-done.6.refs_7_), channel_id=1, source_target_pairs={{8,0},{16,8},{24,16},{28,24},{20,28},{12,20},{4,12},{0,4},{9,1},{1... | collective-permute-start | bytes 786440 | tf_op jit(solution)/shard_map/ppermute | solution.py:401
  29.8 11.2 %collective-permute-start.10 = (bf16[256,512]{1,0:T(8,128)(2,1)S(1)}, bf16[256,512]{1,0:T(8,128)(2,1)S(1)}, u32[]{:S(2)}, u32[]{:S(2)}) collective-permute-start(bf16[256,512]{1,0:T(8,128)(2,1)S(1)} %collective-permute-done.4.refs_5_), channel_id=1, source_target_pairs={{0,8},{8,16},{16,24},{24,28},{28,20},{20,12},{12,4},{4,0},{1,9},{9... | collective-permute-start | bytes 786440 | tf_op jit(solution)/shard_map/ppermute | solution.py:401
  33.8 11.2 %collective-permute-start.13 = (bf16[256,512]{1,0:T(8,128)(2,1)S(1)}, bf16[256,512]{1,0:T(8,128)(2,1)S(1)}, u32[]{:S(2)}, u32[]{:S(2)}) collective-permute-start(bf16[256,512]{1,0:T(8,128)(2,1)S(1)} %collective-permute-done.7.refs_8_), channel_id=1, source_target_pairs={{8,0},{16,8},{24,16},{28,24},{20,28},{12,20},{4,12},{0,4},{9,1},{1... | collective-permute-start | bytes 786440 | tf_op jit(solution)/shard_map/ppermute | solution.py:401
  35.4 11.2 %collective-permute-start.14 = (bf16[256,512]{1,0:T(8,128)(2,1)S(1)}, bf16[256,512]{1,0:T(8,128)(2,1)S(1)}, u32[]{:S(2)}, u32[]{:S(2)}) collective-permute-start(bf16[256,512]{1,0:T(8,128)(2,1)S(1)} %collective-permute-done.8.refs_9_), channel_id=1, source_target_pairs={{0,8},{8,16},{16,24},{24,28},{28,20},{20,12},{12,4},{4,0},{1,9},{9... | collective-permute-start | bytes 786440 | tf_op jit(solution)/shard_map/ppermute | solution.py:401
  39.4 11.2 %collective-permute-start.15 = (bf16[256,512]{1,0:T(8,128)(2,1)S(1)}, bf16[256,512]{1,0:T(8,128)(2,1)S(1)}, u32[]{:S(2)}, u32[]{:S(2)}) collective-permute-start(bf16[256,512]{1,0:T(8,128)(2,1)S(1)} %collective-permute-done.11.refs_12_), channel_id=1, source_target_pairs={{8,0},{16,8},{24,16},{28,24},{20,28},{12,20},{4,12},{0,4},{9,1},{1... | collective-permute-start | bytes 786440 | tf_op jit(solution)/shard_map/ppermute | solution.py:401
  41.0 11.2 %collective-permute-start.18 = (bf16[256,512]{1,0:T(8,128)(2,1)S(1)}, bf16[256,512]{1,0:T(8,128)(2,1)S(1)}, u32[]{:S(2)}, u32[]{:S(2)}) collective-permute-start(bf16[256,512]{1,0:T(8,128)(2,1)S(1)} %collective-permute-done.9.refs_10_), channel_id=1, source_target_pairs={{0,8},{8,16},{16,24},{24,28},{28,20},{20,12},{12,4},{4,0},{1,9},{9... | collective-permute-start | bytes 786440 | tf_op jit(solution)/shard_map/ppermute | solution.py:401
  45.1 11.2 %collective-permute-start.19 = (bf16[256,512]{1,0:T(8,128)(2,1)S(1)}, bf16[256,512]{1,0:T(8,128)(2,1)S(1)}, u32[]{:S(2)}, u32[]{:S(2)}) collective-permute-start(bf16[256,512]{1,0:T(8,128)(2,1)S(1)} %collective-permute-done.12.refs_13_), channel_id=1, source_target_pairs={{8,0},{16,8},{24,16},{28,24},{20,28},{12,20},{4,12},{0,4},{9,1},{1... | collective-permute-start | bytes 786440 | tf_op jit(solution)/shard_map/ppermute | solution.py:401
  46.6 11.2 %collective-permute-start.16 = (bf16[256,512]{1,0:T(8,128)(2,1)S(1)}, bf16[256,512]{1,0:T(8,128)(2,1)S(1)}, u32[]{:S(2)}, u32[]{:S(2)}) collective-permute-start(bf16[256,512]{1,0:T(8,128)(2,1)S(1)} %collective-permute-done.10.refs_11_), channel_id=1, source_target_pairs={{0,8},{8,16},{16,24},{24,28},{28,20},{20,12},{12,4},{4,0},{1,9},{9... | collective-permute-start | bytes 786440 | tf_op jit(solution)/shard_map/ppermute | solution.py:401
  50.7 11.2 %collective-permute-start.20 = (bf16[256,512]{1,0:T(8,128)(2,1)S(1)}, bf16[256,512]{1,0:T(8,128)(2,1)S(1)}, u32[]{:S(2)}, u32[]{:S(2)}) collective-permute-start(bf16[256,512]{1,0:T(8,128)(2,1)S(1)} %collective-permute-done.13.refs_14_), channel_id=1, source_target_pairs={{8,0},{16,8},{24,16},{28,24},{20,28},{12,20},{4,12},{0,4},{9,1},{1... | collective-permute-start | bytes 786440 | tf_op jit(solution)/shard_map/ppermute | solution.py:401
  52.3 11.2 %collective-permute-start.22 = (bf16[512,256]{1,0:T(8,128)(2,1)S(1)}, bf16[512,256]{1,0:T(8,128)(2,1)S(1)}, u32[]{:S(2)}, u32[]{:S(2)}) collective-permute-start(bf16[512,256]{1,0:T(8,128)(2,1)S(1)} %copy-done.4), channel_id=1, source_target_pairs={{0,8},{8,16},{16,24},{24,28},{28,20},{20,12},{12,4},{4,0},{1,9},{9... | collective-permute-start | bytes 786440 | tf_op jit(solution)/shard_map/ppermute | solution.py:401
  56.3 11.2 %collective-permute-start.24 = (bf16[512,256]{1,0:T(8,128)(2,1)S(1)}, bf16[512,256]{1,0:T(8,128)(2,1)S(1)}, u32[]{:S(2)}, u32[]{:S(2)}) collective-permute-start(bf16[512,256]{1,0:T(8,128)(2,1)S(1)} %copy-done.4), channel_id=1, source_target_pairs={{8,0},{16,8},{24,16},{28,24},{20,28},{12,20},{4,12},{0,4},{9,1},{1... | collective-permute-start | bytes 786440 | tf_op jit(solution)/shard_map/ppermute | solution.py:401
  57.9 11.2 %collective-permute-start.17 = (bf16[256,512]{1,0:T(8,128)(2,1)S(1)}, bf16[256,512]{1,0:T(8,128)(2,1)S(1)}, u32[]{:S(2)}, u32[]{:S(2)}) collective-permute-start(bf16[256,512]{1,0:T(8,128)(2,1)S(1)} %collective-permute-done.14.refs_0_), channel_id=1, source_target_pairs={{0,8},{8,16},{16,24},{24,28},{28,20},{20,12},{12,4},{4,0},{1,9},{9... | collective-permute-start | bytes 786440 | tf_op jit(solution)/shard_map/ppermute | solution.py:401
  61.9 11.9 %collective-permute-start.21 = (bf16[256,512]{1,0:T(8,128)(2,1)S(1)}, bf16[256,512]{1,0:T(8,128)(2,1)S(1)}, u32[]{:S(2)}, u32[]{:S(2)}) collective-permute-start(bf16[256,512]{1,0:T(8,128)(2,1)S(1)} %collective-permute-done.19.refs_4_), channel_id=1, source_target_pairs={{8,0},{16,8},{24,16},{28,24},{20,28},{12,20},{4,12},{0,4},{9,1},{1... | collective-permute-start | bytes 786440 | tf_op jit(solution)/shard_map/ppermute | solution.py:401
  63.5 11.8 %collective-permute-start.23 = (bf16[256,512]{1,0:T(8,128)(2,1)S(1)}, bf16[256,512]{1,0:T(8,128)(2,1)S(1)}, u32[]{:S(2)}, u32[]{:S(2)}) collective-permute-start(bf16[256,512]{1,0:T(8,128)(2,1)S(1)} %collective-permute-done.16.refs_0_), channel_id=1, source_target_pairs={{0,8},{8,16},{16,24},{24,28},{28,20},{20,12},{12,4},{4,0},{1,9},{9... | collective-permute-start | bytes 786440 | tf_op jit(solution)/shard_map/ppermute | solution.py:401
  67.5 10.3 %collective-permute-start.26 = (bf16[512,256]{1,0:T(8,128)(2,1)S(1)}, bf16[512,256]{1,0:T(8,128)(2,1)S(1)}, u32[]{:S(2)}, u32[]{:S(2)}) collective-permute-start(bf16[512,256]{1,0:T(8,128)(2,1)S(1)} %collective-permute-done.24.refs_2_), channel_id=1, source_target_pairs={{8,0},{16,8},{24,16},{28,24},{20,28},{12,20},{4,12},{0,4},{9,1},{1... | collective-permute-start | bytes 786440 | tf_op jit(solution)/shard_map/ppermute | solution.py:401
  85.9 12.6 %collective-permute-start.32 = (bf16[512,256]{1,0:T(8,128)(2,1)S(1)}, bf16[512,256]{1,0:T(8,128)(2,1)S(1)}, u32[]{:S(2)}, u32[]{:S(2)}) collective-permute-start(bf16[512,256]{1,0:T(8,128)(2,1)S(1)} %collective-permute-done.25.refs_3_), channel_id=1, source_target_pairs={{0,8},{8,16},{16,24},{24,28},{28,20},{20,12},{12,4},{4,0},{1,9},{9... | collective-permute-start | bytes 786440 | tf_op jit(solution)/shard_map/ppermute | solution.py:401
  (22 other events, 268.4 us)
